TPU v7x, 32 devices: a whole 2x2x4 slice. The times are simulated.
32 devices in a mesh: group: 4 (over y, x), fsdp: 8 (over z, core).
Axes of the slice: x: 2, y: 2, z: 4, core: 2. Of those that a mesh axis runs over, the one named last changes fastest.
Arguments:
- tokens_in: bfloat16 [32768, 2048], P(('group', 'fsdp')), may hold values from -6 to 6
- out_grad: bfloat16 [32768, 2048], P(('group', 'fsdp')), may hold values from -0.59765625 to 0.59765625
- w_in: bfloat16 [4, 2048, 8192], P('group', None, 'fsdp'), may hold values from -0.125 to 0.125
- w_out: bfloat16 [4, 8192, 2048], P('group', 'fsdp'), may hold values from -0.0625 to 0.0625
- chosen: int32 [32, 4, 16], P(('group', 'fsdp')), may hold values from 0 to 1023, as said below
- counts: int32 [32, 4], P(('group', 'fsdp')), may hold values from 1 to 16, as said below
- gates: float32 [32, 4, 16], P(('group', 'fsdp')), may hold values from 0.05 to 1
Outputs:
- grad_in: bfloat16 [32768, 2048], P(('group', 'fsdp'))
- grad_w_in: float32 [4, 2048, 8192], P('group', None, 'fsdp')
- grad_w_out: float32 [4, 8192, 2048], P('group', 'fsdp')
Inputs may be any that keep to these rules, and one draw needn't show every extreme that they name: `chosen`: the 16 slots of one image and one expert name distinct positions. `counts`: each image fills all 16 slots of at least one expert.
All inputs are finite; a program needn't handle non-finite values.
Results may differ from a plain program's by a relative error of at most 0.0057.
Values may be sent and summed in bfloat16 or wider, within the bound.
No kernel may reach another device: no remote copies, remote signals or barrier semaphores. Data moves between devices by JAX's collectives and lax.ppermute only.
A program may use at most 128 MiB of HBM per device.

v0:
```python
import jax
import jax.numpy as jnp
from jax import lax
from jax.sharding import PartitionSpec as P

gelu_coef = 0.7978845608028654


def gelu_parts(hidden):
    inner_arg = gelu_coef * (hidden + 0.044715 * hidden * hidden * hidden)
    tangent = jnp.tanh(inner_arg)
    activation = 0.5 * hidden * (1.0 + tangent)
    slope = 0.5 * (1.0 + tangent) + 0.5 * hidden * (1.0 - tangent * tangent) * gelu_coef * (
        1.0 + 3.0 * 0.044715 * hidden * hidden
    )
    return (activation, slope)


def shards(tokens_in, out_grad, w_in, w_out, chosen, counts, gates):
    group_count = lax.axis_size("group")
    exp_local = w_in.shape[0]
    slot_count = chosen.shape[2]
    model_width = tokens_in.shape[1]
    slot_rows = chosen[0].reshape(-1)
    slot_iota = lax.broadcasted_iota(jnp.int32, chosen.shape[1:], 1)
    live_gate = jnp.where(slot_iota < counts[0][:, None], gates[0], jnp.float32(0.0))
    block_shape = (group_count, exp_local, slot_count, model_width)
    picked_x = jnp.take(tokens_in, slot_rows, axis=0).reshape(block_shape)
    picked_grad = (
        (live_gate.reshape(-1)[:, None] * jnp.take(out_grad, slot_rows, axis=0).astype(jnp.float32))
        .astype(jnp.bfloat16)
        .reshape(block_shape)
    )
    near_x, near_grad = (
        lax.all_to_all(picked_x, "group", split_axis=0, concat_axis=0, tiled=True),
        lax.all_to_all(picked_grad, "group", split_axis=0, concat_axis=0, tiled=True),
    )
    rows_x, rows_grad = (
        lax.all_gather(near_x, "fsdp", axis=0, tiled=True),
        lax.all_gather(near_grad, "fsdp", axis=0, tiled=True),
    )
    sources = rows_x.shape[0]
    expert_x = rows_x[:, 0].reshape(-1, model_width)
    expert_grad = rows_grad[:, 0].reshape(-1, model_width)
    hidden = jnp.dot(expert_x, w_in[0], preferred_element_type=jnp.float32)
    activation, gelu_slope = gelu_parts(hidden)
    activation = activation.astype(jnp.bfloat16)
    back_hidden = lax.dot_general(
        expert_grad, w_out[0], (((1,), (1,)), ((), ())), preferred_element_type=jnp.float32
    )
    hidden_grad = (back_hidden * gelu_slope).astype(jnp.bfloat16)
    grads_in_w = [
        lax.dot_general(
            expert_x, hidden_grad, (((0,), (0,)), ((), ())), preferred_element_type=jnp.float32
        )
    ]
    grads_out_w = [
        lax.dot_general(
            activation, expert_grad, (((0,), (0,)), ((), ())), preferred_element_type=jnp.float32
        )
    ]
    hidden_grads = [hidden_grad.reshape(sources, slot_count, -1)]
    stacked_grad = jnp.stack(hidden_grads, axis=1)
    term = jnp.einsum("secf,edf->secd", stacked_grad, w_in, preferred_element_type=jnp.float32)
    partial_grad = term.reshape(sources * exp_local * slot_count, model_width)
    shares = lax.psum_scatter(partial_grad, "fsdp", scatter_dimension=0, tiled=True)
    summed = lax.all_to_all(
        shares.reshape(group_count, exp_local, slot_count, model_width),
        "group",
        split_axis=0,
        concat_axis=0,
        tiled=True,
    )
    grad_tokens = (
        jnp.zeros((tokens_in.shape[0], model_width), jnp.float32)
        .at[slot_rows]
        .add(summed.reshape(-1, model_width))
    )
    return (
        grad_tokens.astype(jnp.bfloat16),
        jnp.stack(grads_in_w, axis=0),
        jnp.stack(grads_out_w, axis=0),
    )


def solution(mesh):
    placed = (
        P(("group", "fsdp"), None),
        P(("group", "fsdp"), None),
        P("group", None, "fsdp"),
        P("group", "fsdp", None),
        P(("group", "fsdp"), None, None),
        P(("group", "fsdp"), None),
        P(("group", "fsdp"), None, None),
    )
    return jax.shard_map(
        shards,
        mesh=mesh,
        in_specs=placed,
        out_specs=(P(("group", "fsdp"), None), P("group", None, "fsdp"), P("group", "fsdp", None)),
        check_vma=False,
    )
```

profile of v0, /device:TPU:0, one launch (start us, length us, event | category | flops | bytes accessed | tf_op | source)
XLA Modules:
  0.0 170.6 jit_solution(7998018423158543640)
XLA Ops:
  7.2 0.0 all-gather.5.cloned.1.call-start
  7.2 0.8 reshape_squeeze.12
  8.0 3.7 %gather_fusion.1 = bf16[64,2048]{1,0:T(8,128)(2,1)S(1)} fusion(bf16[1024,2048]{1,0:T(8,128)(2,1)} %param.9, s32[1024]{0:T(1024)S(1)} %pad_clamp_fusion), kind=kCustom, calls=%fused_computation.1.clone | custom fusion | bytes 524544 | tf_op jit(solution)/shard_map/jit(_take)/gather | solution.py:28
  11.7 0.0 copy-start.4
  11.7 0.0 copy-start.1
  11.7 0.1 broadcast_select_fusion
  11.8 10.8 %all_to_all.15 = bf16[4,1,16,2048]{3,2,1,0:T(8,128)(2,1)} all-to-all(bf16[4,1,16,2048]{3,2,1,0:T(8,128)(2,1)S(1)} %bitcast.43), channel_id=1, replica_groups=mesh['group'=4,'fsdp'=8] {'group'}, dimensions={0} | all-to-all | bytes 524288 | tf_op jit(solution)/shard_map/all_to_all | solution.py:35
  22.6 0.0 all-gather.5.cloned.1.call-update
  22.7 0.0 all-gather.3.cloned.1.call-start
  22.7 3.7 %gather_fusion = bf16[64,2048]{1,0:T(8,128)(2,1)S(1)} fusion(bf16[1024,2048]{1,0:T(8,128)(2,1)} %param.10, s32[1024]{0:T(1024)S(1)} %pad_clamp_fusion), kind=kCustom, calls=%fused_computation.clone | custom fusion | bytes 524544 | tf_op jit(solution)/shard_map/jit(_take)/gather | solution.py:30
  26.4 0.0 copy-done.4
  26.4 0.1 iota_compare_fusion
  26.5 0.1 lt.41
  26.6 0.0 copy-done.1
  26.6 0.1 squeeze.9
  26.7 0.2 multiply_convert_fusion.2
  26.9 8.8 %all_to_all.16 = bf16[4,1,16,2048]{3,2,1,0:T(8,128)(2,1)} all-to-all(bf16[4,1,16,2048]{3,2,1,0:T(8,128)(2,1)S(1)} %bitcast.44), channel_id=1, replica_groups=mesh['group'=4,'fsdp'=8] {'group'}, dimensions={0} | all-to-all | bytes 524288 | tf_op jit(solution)/shard_map/all_to_all | solution.py:36
  35.7 0.0 all-gather.3.cloned.1.call-update
  35.7 0.0 reduce-scatter.2.cloned.1.call-start
  35.7 15.9 %all-gather.5.cloned.1.call-done = bf16[32,1,16,2048]{3,2,1,0:T(8,128)(2,1)} async-done(((bf16[4,1,16,2048]{3,2,1,0:T(8,128)(2,1)}), bf16[32,1,16,2048]{3,2,1,0:T(8,128)(2,1)}) %all-gather.5.cloned.1.call-update) | async-done | bytes 2097168 | tf_op jit(solution)/shard_map/all_gather | solution.py:39
  51.6 5.2 %fusion.2 = f32[512,1024]{1,0:T(8,128)S(1)} fusion(bf16[512,2048]{1,0:T(8,128)(2,1)} %bitcast.47, bf16[1,2048,1024]{2,1,0:T(8,128)(2,1)} %param.11), kind=kOutput, calls=%fused_computation.7 | convolution fusion | flops 2147483648 | bytes 8388608 | tf_op jit(solution)/shard_map/dot_general | solution.py:45
  56.8 0.0 copy-start.6
  56.8 25.1 %all-gather.3.cloned.1.call-done = bf16[32,1,16,2048]{3,2,1,0:T(8,128)(2,1)} async-done(((bf16[4,1,16,2048]{3,2,1,0:T(8,128)(2,1)}), bf16[32,1,16,2048]{3,2,1,0:T(8,128)(2,1)}) %all-gather.3.cloned.1.call-update) | async-done | bytes 2097168 | tf_op jit(solution)/shard_map/all_gather | solution.py:40
  81.9 0.0 copy-start.2
  81.9 6.3 %fusion.14 = bf16[512,1024]{1,0:T(8,128)(2,1)S(1)} fusion(f32[512,1024]{1,0:T(8,128)S(1)} %fusion.2, bf16[512,2048]{1,0:T(8,128)(2,1)} %bitcast.49, bf16[1,1024,2048]{2,1,0:T(8,128)(2,1)} %param.12), kind=kOutput, calls=%fused_computation.21 | convolution fusion | flops 2157445120 | bytes 9437184 | tf_op jit(solution)/shard_map/dot_general | solution.py:48
  88.1 0.0 copy-done.6
  88.1 0.0 copy-start.5
  88.2 0.0 copy-done.2
  88.2 4.4 %fusion = f32[32,16,2048]{2,1,0:T(8,128)} fusion(bf16[32,16,1024]{2,1,0:T(8,128)(2,1)S(1)} %bitcast.52, bf16[1,2048,1024]{2,1,0:T(8,128)(2,1)S(1)} %copy-done.2), kind=kOutput, calls=%fused_computation.5 | convolution fusion | flops 2147483648 | bytes 9437184 | tf_op jit(solution)/shard_map/secf,edf->secd/dot_general | solution.py:64
  92.6 0.0 copy-done.5
  92.6 0.0 copy-start
  92.6 0.0 reduce-scatter.2.cloned.1.call-update
  92.6 0.7 copy-done
  93.2 0.1 reshape_squeeze.11
  93.3 0.0 copy-start.3
  93.3 8.3 %convolution_bitcast_fusion = f32[1,1024,2048]{2,1,0:T(8,128)} fusion(bf16[512,2048]{1,0:T(8,128)(2,1)} %bitcast.50, f32[512,1024]{1,0:T(8,128)} %copy-done.6), kind=kOutput, calls=%fused_computation.3 | convolution fusion | flops 2152202240 | bytes 12582912 | tf_op jit(solution)/shard_map/dot_general | solution.py:58
  101.7 40.6 %reduce-scatter.2.cloned.1.call-done = f32[64,2048]{1,0:T(8,128)} async-done(((f32[512,2048]{1,0:T(8,128)}), f32[64,2048]{1,0:T(8,128)}) %reduce-scatter.2.cloned.1.call-update) | async-done | bytes 524304 | tf_op jit(solution)/shard_map/reduce_scatter | solution.py:66
  142.3 3.6 %all-to-all-start.2 = ((f32[4,1,16,2048]{3,2,1,0:T(8,128)}), f32[4,1,16,2048]{3,2,1,0:T(8,128)S(1)}, u32[]{:S(2)}, u32[]{:S(2)}) async-start(f32[4,1,16,2048]{3,2,1,0:T(8,128)} %bitcast.45), calls=%async_computation.3 | async-start | bytes 1048576 | tf_op jit(solution)/shard_map/all_to_all | solution.py:67
  145.9 0.0 copy-done.3
  145.9 7.0 %convolution_bitcast_fusion.1 = f32[1,2048,1024]{2,1,0:T(8,128)} fusion(bf16[512,2048]{1,0:T(8,128)(2,1)S(1)} %bitcast.48, bf16[512,1024]{1,0:T(8,128)(2,1)} %copy-done.5), kind=kOutput, calls=%fused_computation.4 | convolution fusion | flops 2147483648 | bytes 11534336 | tf_op jit(solution)/shard_map/dot_general | solution.py:53
  152.9 0.0 all-to-all-done.2
  152.9 5.1 %scatter_custom_fusion = f32[1024,2048]{1,0:T(8,128)} fusion(s32[64]{0:T(128)S(1)} %fusion.21, f32[64,2048]{1,0:T(8,128)S(1)} %bitcast.46, f32[]{:T(128)} %constant.0.clone.1), kind=kCustom, calls=%fused_computation.11 | custom fusion | flops 131072 | bytes 8388612 | tf_op jit(solution)/shard_map/scatter-add | solution.py:77
  158.0 6.0 %convert_element_type.18 = bf16[1024,2048]{1,0:T(8,128)(2,1)} convert(f32[1024,2048]{1,0:T(8,128)} %scatter_custom_fusion) | non-fusion elementwise | flops 2097152 | bytes 12582912 | tf_op jit(solution)/shard_map/convert_element_type | solution.py:80
  (5 shorter events, 0.0 us)
Async XLA Ops:
  7.2 44.5 %all-gather.5.cloned.1.call-start = ((), (), s32[]{:S(2)}) async-start(), calls=%async_computation.5 | async-start | bytes 2359296 | tf_op jit(solution)/shard_map/all_gather | solution.py:39
  11.7 14.7 %copy-start.4 = (s32[1,4]{1,0:T(1,128)S(1)}, s32[1,4]{1,0:T(1,128)}, u32[]{:S(2)}) copy-start(s32[1,4]{1,0:T(1,128)} %param.14) | copy-start | bytes 52
  11.7 14.9 %copy-start.1 = (f32[1,4,16]{2,1,0:T(4,128)S(1)}, f32[1,4,16]{2,1,0:T(4,128)}, u32[]{:S(2)}) copy-start(f32[1,4,16]{2,1,0:T(4,128)} %param.15) | copy-start | bytes 772
  22.7 59.2 %all-gather.3.cloned.1.call-start = ((), (), s32[]{:S(2)}) async-start(), calls=%async_computation.4 | async-start | bytes 2359296 | tf_op jit(solution)/shard_map/all_gather | solution.py:40
  35.7 106.6 %reduce-scatter.2.cloned.1.call-start = ((), (), s32[]{:S(2)}) async-start(), calls=%async_computation.6 | async-start | bytes 4718592 | tf_op jit(solution)/shard_map/reduce_scatter | solution.py:66
  56.8 31.3 %copy-start.6 = (f32[512,1024]{1,0:T(8,128)}, f32[512,1024]{1,0:T(8,128)S(1)}, u32[]{:S(2)}) copy-start(f32[512,1024]{1,0:T(8,128)S(1)} %fusion.2) | copy-start | bytes 6291460
  81.9 6.3 %copy-start.2 = (bf16[1,2048,1024]{2,1,0:T(8,128)(2,1)S(1)}, bf16[1,2048,1024]{2,1,0:T(8,128)(2,1)}, u32[]{:S(2)}) copy-start(bf16[1,2048,1024]{2,1,0:T(8,128)(2,1)} %param.11) | copy-start | bytes 12582916
  88.1 4.4 %copy-start.5 = (bf16[512,1024]{1,0:T(8,128)(2,1)}, bf16[512,1024]{1,0:T(8,128)(2,1)S(1)}, u32[]{:S(2)}) copy-start(bf16[512,1024]{1,0:T(8,128)(2,1)S(1)} %fusion.14) | copy-start | bytes 3145732
  92.6 0.7 copy-start
  93.3 52.6 %copy-start.3 = (bf16[32,1,16,2048]{3,2,1,0:T(8,128)(2,1)S(1)}, bf16[32,1,16,2048]{3,2,1,0:T(8,128)(2,1)}, u32[]{:S(2)}) copy-start(bf16[32,1,16,2048]{3,2,1,0:T(8,128)(2,1)} %all-gather.5.cloned.1.call-done) | copy-start | bytes 6291460
  142.3 10.7 %all-to-all-start.2 = ((f32[4,1,16,2048]{3,2,1,0:T(8,128)}), f32[4,1,16,2048]{3,2,1,0:T(8,128)S(1)}, u32[]{:S(2)}, u32[]{:S(2)}) async-start(f32[4,1,16,2048]{3,2,1,0:T(8,128)} %bitcast.45), calls=%async_computation.3 | async-start | bytes 1048576 | tf_op jit(solution)/shard_map/all_to_all | solution.py:67
Sparse Core Ops, SparseCore 0:
  22.8 28.8 all-gather.4
  53.2 28.5 all-gather.2
  92.7 49.4 reduce-scatter.1
where the time goes:
time: 171 us
  waiting for transfers between devices  81.6 us (48%)
  matrix products  31.1 us (18%)
  blocking collectives  19.6 us (11%)
  between operations  13.9 us (8%)
  other arithmetic  11.5 us (7%)
  local copies, waits for them, and re-layouts  9.14 us (5%)
  starting transfers between devices  3.77 us (2%)
    reduce_scatter x1, waiting for transfers between devices, shards(): lax.psum_scatter(partial_grad, 'fsdp', scatter_dimension=0, tiled=True)  40.6 us
    all_gather x1, waiting for transfers between devices, shards(): lax.all_gather(near_grad, 'fsdp', axis=0, tiled=True)  25.1 us
    all_gather x1, waiting for transfers between devices, shards(): lax.all_gather(near_x, 'fsdp', axis=0, tiled=True)  15.9 us
    all_to_all x1, blocking collectives, shards(): lax.all_to_all(picked_x, 'group', split_axis=0, concat_axis=0, tiled=True)  10.8 us
    all_to_all x1, blocking collectives, shards(): lax.all_to_all(picked_grad, 'group', split_axis=0, concat_axis=0, tiled=T...  8.8 us
    dot_general x1, matrix products, shards(): lax.dot_general(activation, expert_grad, (((0,), (0,)), ((), ())), prefer...  8.33 us
    dot_general x1, matrix products, shards(): lax.dot_general(expert_x, hidden_grad, (((0,), (0,)), ((), ())), preferre...  7.01 us
    dot_general x1, matrix products, shards(): lax.dot_general(expert_grad, w_out[0], (((1,), (1,)), ((), ())), preferre...  6.25 us
  transfers between devices with their start and end apart: 4, of which 3 were waited for; matrix products, arithmetic and copies ran while one was open for 14% of the time, Pallas kernels for 0%

commit v1 on v0

v1 whole, which is shorter than its diff:
```python
import functools

import jax
import jax.numpy as jnp
from jax import lax
from jax.experimental import pallas as pl
from jax.experimental.pallas import tpu as pltpu
from jax.sharding import PartitionSpec as P

gelu_coef = 0.7978845608028654
both = ("group", "fsdp")


def gelu_parts(hidden):
    inner_arg = gelu_coef * (hidden + 0.044715 * hidden * hidden * hidden)
    tangent = jnp.tanh(inner_arg)
    activation = 0.5 * hidden * (1.0 + tangent)
    slope = 0.5 * (1.0 + tangent) + 0.5 * hidden * (1.0 - tangent * tangent) * gelu_coef * (
        1.0 + 3.0 * 0.044715 * hidden * hidden
    )
    return (activation, slope)


def params(limit=48 * 2**20):
    return pltpu.CompilerParams(vmem_limit_bytes=limit)


def cost(flops, moved, trans=0):
    return pl.CostEstimate(flops=flops, bytes_accessed=moved, transcendentals=trans)


def smem():
    return pl.BlockSpec(memory_space=pltpu.SMEM)


def column_of(values, rows, dtype):
    at = lax.broadcasted_iota(jnp.int32, (8, 128), 0)
    tiles = []
    for base in range(0, rows, 8):
        tile = jnp.full((8, 128), values[base], dtype)
        for r in range(1, 8):
            tile = jnp.where(at == r, values[base + r], tile)
        tiles.append(tile)
    return jnp.concatenate(tiles, axis=0)


def pick_kernel(gated, groups, slots, chosen, counts, gates, tokens, *rest):
    outs, onehot, scale = rest[:groups], rest[groups], rest[groups + 1]
    length, width = tokens.shape
    rows = groups * slots

    @pl.when(pl.program_id(0) == 0)
    def _():
        me = lax.axis_index("group")
        owner = [lax.rem(me + r, groups) for r in range(groups)]
        column = column_of([chosen[0, owner[r // slots], r % slots] for r in range(rows)], rows, jnp.int32)
        place = jnp.concatenate([column] * (length // 128), axis=1)
        onehot[...] = jnp.where(
            place == lax.broadcasted_iota(jnp.int32, (rows, length), 1), 1.0, 0.0
        ).astype(jnp.bfloat16)
        if gated:
            live = []
            for r in range(rows):
                e, c = owner[r // slots], r % slots
                live.append(jnp.where(c < counts[0, e], gates[0, e, c], jnp.float32(0.0)))
            scale[...] = column_of(live, rows, jnp.float32)

    picked = jnp.dot(onehot[...], tokens[...], preferred_element_type=jnp.float32)
    if gated:
        picked = picked * jnp.concatenate([scale[...]] * (width // 128), axis=1)
    picked = picked.astype(jnp.bfloat16)
    for d in range(groups):
        outs[d][...] = picked[d * slots : (d + 1) * slots]


def pick(gated, tokens, chosen, counts, gates, groups):
    slots = chosen.shape[2]
    length, model = tokens.shape
    tile = min(512, model)
    rows = groups * slots
    return pl.pallas_call(
        functools.partial(pick_kernel, gated, groups, slots),
        grid=(model // tile,),
        in_specs=[smem(), smem(), smem(), pl.BlockSpec((length, tile), lambda i: (0, i))],
        out_specs=[pl.BlockSpec((slots, tile), lambda i: (0, i))] * groups,
        out_shape=[jax.ShapeDtypeStruct((slots, model), jnp.bfloat16)] * groups,
        scratch_shapes=[pltpu.VMEM((rows, length), jnp.bfloat16), pltpu.VMEM((rows, 128), jnp.float32)],
        compiler_params=params(),
        cost_estimate=cost(2 * rows * length * model, 2 * length * model),
        name="pick_grad" if gated else "pick_x",
    )(chosen, counts, gates, tokens)


def whole_spec(shape):
    return pl.BlockSpec(shape, lambda i: (0,) * len(shape))


def fwd_kernel(x, xp, w, act, slope, lhs):
    half = x.shape[0]

    @pl.when(pl.program_id(0) == 0)
    def _():
        lhs[:half] = x[...]
        lhs[half:] = xp[...]

    hidden = jnp.dot(lhs[...], w[0], preferred_element_type=jnp.float32)
    activation, gelu_slope = gelu_parts(hidden)
    act[...] = activation.astype(jnp.bfloat16)
    slope[...] = gelu_slope


def fwd(x, xp, w_in):
    half, model = x.shape
    units = w_in.shape[2]
    tile = min(256, units)
    rows = 2 * half
    return pl.pallas_call(
        fwd_kernel,
        grid=(units // tile,),
        in_specs=[
            whole_spec((half, model)),
            whole_spec((half, model)),
            pl.BlockSpec((1, model, tile), lambda i: (0, 0, i)),
        ],
        out_specs=[pl.BlockSpec((rows, tile), lambda i: (0, i))] * 2,
        out_shape=[
            jax.ShapeDtypeStruct((rows, units), jnp.bfloat16),
            jax.ShapeDtypeStruct((rows, units), jnp.float32),
        ],
        scratch_shapes=[pltpu.VMEM((rows, model), jnp.bfloat16)],
        compiler_params=params(),
        cost_estimate=cost(2 * rows * model * units, 2 * model * units, rows * units),
        name="hidden",
    )(x, xp, w_in)


def bwd_kernel(g, gp, w_out, w_in, slope, hgrad, mine, theirs, lhs, total):
    half = g.shape[0]
    step = pl.program_id(0)

    @pl.when(step == 0)
    def _():
        lhs[:half] = g[...]
        lhs[half:] = gp[...]

    back = lax.dot_general(
        lhs[...], w_out[0], (((1,), (1,)), ((), ())), preferred_element_type=jnp.float32
    )
    hg = (back * slope[...]).astype(jnp.bfloat16)
    hgrad[...] = hg
    part = lax.dot_general(hg, w_in[0], (((1,), (1,)), ((), ())), preferred_element_type=jnp.float32)

    @pl.when(step == 0)
    def _():
        total[...] = part

    @pl.when(step > 0)
    def _():
        total[...] += part

    @pl.when(step == pl.num_programs(0) - 1)
    def _():
        mine[...] = total[:half]
        theirs[...] = total[half:].astype(theirs.dtype)


def bwd(g, gp, w_out, w_in, slope):
    half, model = g.shape
    units = w_in.shape[2]
    tile = min(256, units)
    rows = 2 * half
    return pl.pallas_call(
        bwd_kernel,
        grid=(units // tile,),
        in_specs=[
            whole_spec((half, model)),
            whole_spec((half, model)),
            pl.BlockSpec((1, tile, model), lambda i: (0, i, 0)),
            pl.BlockSpec((1, model, tile), lambda i: (0, 0, i)),
            pl.BlockSpec((rows, tile), lambda i: (0, i)),
        ],
        out_specs=[
            pl.BlockSpec((rows, tile), lambda i: (0, i)),
            whole_spec((half, model)),
            whole_spec((half, model)),
        ],
        out_shape=[
            jax.ShapeDtypeStruct((rows, units), jnp.bfloat16),
            jax.ShapeDtypeStruct((half, model), jnp.float32),
            jax.ShapeDtypeStruct((half, model), jnp.bfloat16),
        ],
        scratch_shapes=[pltpu.VMEM((rows, model), jnp.bfloat16), pltpu.VMEM((rows, model), jnp.float32)],
        compiler_params=params(),
        cost_estimate=cost(4 * rows * model * units, 4 * model * units),
        name="hidden_grad",
    )(g, gp, w_out, w_in, slope)


def outer_kernel(n_left, *refs):
    left, right, out = refs[:n_left], refs[n_left:-1], refs[-1]
    a = jnp.concatenate([r[...] for r in left], axis=0)
    b = jnp.concatenate([r[...] for r in right], axis=0)
    out[0] = lax.dot_general(a, b, (((0,), (0,)), ((), ())), preferred_element_type=jnp.float32)


def outer(left, right, tile, name):
    m, n = left[0].shape[1], right[0].shape[1]
    rows = sum(r.shape[0] for r in left)
    tile = min(tile, m)
    return pl.pallas_call(
        functools.partial(outer_kernel, len(left)),
        grid=(m // tile,),
        in_specs=[pl.BlockSpec((r.shape[0], tile), lambda i: (0, i)) for r in left]
        + [whole_spec(r.shape) for r in right],
        out_specs=pl.BlockSpec((1, tile, n), lambda i: (0, i, 0)),
        out_shape=jax.ShapeDtypeStruct((1, m, n), jnp.float32),
        compiler_params=params(),
        cost_estimate=cost(2 * rows * m * n, 4 * m * n),
        name=name,
    )(*left, *right)


def add_kernel(n_in, *refs):
    ins, outs = refs[:n_in], refs[n_in:]
    total = ins[0][...].astype(jnp.float32)
    for r in ins[1:]:
        total = total + r[...].astype(jnp.float32)
    total = total.astype(jnp.bfloat16)
    rows = outs[0].shape[0]
    for i, out in enumerate(outs):
        out[...] = total[i * rows : (i + 1) * rows]


def add_up(ins, pieces):
    rows, model = ins[0].shape
    return pl.pallas_call(
        functools.partial(add_kernel, len(ins)),
        out_shape=[jax.ShapeDtypeStruct((rows // pieces, model), jnp.bfloat16)] * pieces,
        compiler_params=params(),
        cost_estimate=cost(rows * model, 12 * rows * model),
        name="add_up",
    )(*ins)


def place_kernel(groups, slots, chosen, *rest):
    parts, out, onehot = rest[:-2], rest[-2], rest[-1]
    length, width = out.shape
    rows = len(parts) * slots

    @pl.when(pl.program_id(0) == 0)
    def _():
        me = lax.axis_index("group")
        lane = lax.broadcasted_iota(jnp.int32, (8, rows), 1)
        place = jnp.full((8, rows), -1, jnp.int32)
        for d in range(groups):
            owner = lax.rem(me + d, groups)
            for c in range(slots):
                hit = lane == d * slots + c
                for again in range(1, len(parts) // groups):
                    hit = hit | (lane == (again * groups + d) * slots + c)
                place = jnp.where(hit, chosen[0, owner, c], place)
        place = jnp.concatenate([place] * (length // 8), axis=0)
        onehot[...] = jnp.where(
            place == lax.broadcasted_iota(jnp.int32, (length, rows), 0), 1.0, 0.0
        ).astype(jnp.bfloat16)

    values = jnp.concatenate([p[...] for p in parts], axis=0)
    out[...] = jnp.dot(onehot[...], values, preferred_element_type=jnp.float32).astype(jnp.bfloat16)


def place(parts, chosen, length, groups):
    slots = chosen.shape[2]
    model = parts[0].shape[1]
    tile = min(512, model)
    rows = len(parts) * slots
    return pl.pallas_call(
        functools.partial(place_kernel, groups, slots),
        grid=(model // tile,),
        in_specs=[smem()] + [pl.BlockSpec((slots, tile), lambda i: (0, i))] * len(parts),
        out_specs=pl.BlockSpec((length, tile), lambda i: (0, i)),
        out_shape=jax.ShapeDtypeStruct((length, model), jnp.bfloat16),
        scratch_shapes=[pltpu.VMEM((length, rows), jnp.bfloat16)],
        compiler_params=params(),
        cost_estimate=cost(2 * rows * length * model, 2 * length * model),
        name="place",
    )(chosen, *parts)


def shards(tokens_in, out_grad, w_in, w_out, chosen, counts, gates):
    groups = lax.axis_size("group")
    fsdp = lax.axis_size("fsdp")
    ring_len = fsdp // 2

    def send(x, group_step, chip_step):
        pairs = [
            (g * fsdp + f, (g + group_step) % groups * fsdp + (f + 2 * chip_step) % fsdp)
            for g in range(groups)
            for f in range(fsdp)
        ]
        return lax.ppermute(x, both, pairs)

    def ring(x):
        return lax.ppermute(x, "fsdp", [(f, (f + 2) % fsdp) for f in range(fsdp)])

    def pair(x):
        return lax.ppermute(x, "fsdp", [(f, f ^ 1) for f in range(fsdp)])

    def spread(pieces):
        next_pieces = [send(pieces[d], d, 1) for d in range(groups)]
        own_pieces = [pieces[0]] + [send(pieces[d], d, 0) for d in range(1, groups)]
        blocks = [jnp.concatenate(own_pieces, axis=0), jnp.concatenate(next_pieces, axis=0)]
        while len(blocks) < ring_len:
            blocks.append(ring(blocks[-1]))
        return blocks

    picked_x = pick(False, tokens_in, chosen, counts, gates, groups)
    picked_grad = pick(True, out_grad, chosen, counts, gates, groups)
    xs = spread(picked_x)
    gs = spread(picked_grad)
    xps = [pair(x) for x in xs]
    gps = [pair(g) for g in gs]

    acts, hgrads, mines, pair_parts = [], [], [], []
    for k in range(ring_len):
        act, slope = fwd(xs[k], xps[k], w_in)
        hgrad, mine, theirs = bwd(gs[k], gps[k], w_out, w_in, slope)
        acts.append(act)
        hgrads.append(hgrad)
        mines.append(mine)
        pair_parts.append(pair(theirs))

    own = add_up([mines[0], pair_parts[0]], groups)
    running = []
    for k in range(1, ring_len):
        last = k == ring_len - 1
        pieces = add_up([mines[k], pair_parts[k]] + running, groups if last else 1)
        if not last:
            running = [ring(pieces[0])]
    parts = [own[0]] + [send(own[d], -d, 0) for d in range(1, groups)]
    parts += [send(pieces[d], -d, 1) for d in range(groups)]

    grad_w_in = outer([r for k in range(ring_len) for r in (xs[k], xps[k])], hgrads, 512, "grad_w_in")
    grad_w_out = outer(acts, [r for k in range(ring_len) for r in (gs[k], gps[k])], 256, "grad_w_out")
    return place(parts, chosen, tokens_in.shape[0], groups), grad_w_in, grad_w_out


def solution(mesh):
    placed = (
        P(("group", "fsdp"), None),
        P(("group", "fsdp"), None),
        P("group", None, "fsdp"),
        P("group", "fsdp", None),
        P(("group", "fsdp"), None, None),
        P(("group", "fsdp"), None),
        P(("group", "fsdp"), None, None),
    )
    return jax.shard_map(
        shards,
        mesh=mesh,
        in_specs=placed,
        out_specs=(P(("group", "fsdp"), None), P("group", None, "fsdp"), P("group", "fsdp", None)),
        check_vma=False,
    )
```

time: 171 us -> 127 us (0.74)
  Pallas kernels: 0 us -> 58.2 us
  waiting for transfers between devices: 81.6 us -> 28.3 us
  matrix products: 31.1 us -> 0 us
  starting transfers between devices: 3.77 us -> 31.7 us
  blocking collectives: 19.6 us -> 0 us
  between operations: 13.9 us -> 1.04 us
  other arithmetic: 11.5 us -> 0 us
  local copies, waits for them, and re-layouts: 9.14 us -> 6.82 us
    pallas_call x0 -> x17, Pallas kernels: none -> 58.2 us  [the longest x4 30.4 us: bwd(): pl.pallas_call(bwd_kernel, grid=(units // tile,), in_specs=[whole_spec((h...]
    all_gather x2 -> x0, waiting for transfers between devices: 41 us -> none  [the longest x1 25.1 us: shards(): lax.all_gather(near_grad, 'fsdp', axis=0, tiled=True)]
    reduce_scatter x1 -> x0, waiting for transfers between devices: 40.6 us -> none  [shards(): lax.psum_scatter(partial_grad, 'fsdp', scatter_dimension=0, tiled=True)]
    ppermute x0 -> x39, starting transfers between devices: none -> 31.7 us  [the longest x21 28.4 us: send(): return lax.ppermute(x, both, pairs)]
    dot_general x5 -> x0, matrix products: 31.1 us -> none  [the longest x1 8.33 us: shards(): lax.dot_general(activation, expert_grad, (((0,), (0,)), ((), ())), prefer...]
    ppermute x0 -> x39, waiting for transfers between devices: none -> 28.3 us  [the longest x21 17.1 us: send(): return lax.ppermute(x, both, pairs)]
    all_to_all x2 -> x0, blocking collectives: 19.6 us -> none  [the longest x1 10.8 us: shards(): lax.all_to_all(picked_x, 'group', split_axis=0, concat_axis=0, tiled=True)]
    gather x2 -> x0, local copies, waits for them, and re-layouts: 7.43 us -> none  [the longest x1 3.72 us: shards(): jnp.take(out_grad, slot_rows, axis=0).astype(jnp.float32)]
  transfers between devices with their start and end apart: 4 -> 39, of which waited for: 3 -> 9; matrix products, arithmetic and copies ran while one was open for 14% -> 0% of each run, Pallas kernels for 0% -> 41%
where the time goes in v1:
time: 127 us; the launch traced here: 126 us
  Pallas kernels  58.2 us (46%)
  starting transfers between devices  31.7 us (25%)
  waiting for transfers between devices  28.3 us (22%)
  local copies, waits for them, and re-layouts  6.82 us (5%)
    pallas_call x4, Pallas kernels, bwd(): pl.pallas_call(bwd_kernel, grid=(units // tile,), in_specs=[whole_spec((h...  30.4 us
    ppermute x21, starting transfers between devices, send(): return lax.ppermute(x, both, pairs)  28.4 us
    ppermute x21, waiting for transfers between devices, send(): return lax.ppermute(x, both, pairs)  17.1 us
    pallas_call x2, Pallas kernels, outer(): pl.pallas_call(functools.partial(outer_kernel, len(left)), grid=(m // til...  10.1 us
    ppermute x6, waiting for transfers between devices, ring(): return lax.ppermute(x, 'fsdp', [(f, (f + 2) % fsdp) for f in range(fsdp)])  9.42 us
    pallas_call x4, Pallas kernels, fwd(): pl.pallas_call(fwd_kernel, grid=(units // tile,), in_specs=[whole_spec((h...  8.86 us
    unnamed x32, local copies, waits for them, and re-layouts  6.8 us
    pallas_call x2, Pallas kernels, pick(): pl.pallas_call(functools.partial(pick_kernel, gated, groups, slots), grid...  4.62 us
  transfers between devices with their start and end apart: 39, of which 9 were waited for; matrix products, arithmetic and copies ran while one was open for 0% of the time, Pallas kernels for 41%

profile of v1, /device:TPU:0, one launch (start us, length us, event | category | flops | bytes accessed | tf_op | source)
XLA Modules:
  0.0 126.1 jit_solution(4147585285380462136)
XLA Ops:
  0.6 0.0 copy-start
  0.7 2.3 %copy-done.4 = bf16[1024,2048]{1,0:T(8,128)(2,1)S(1)} copy-done((bf16[1024,2048]{1,0:T(8,128)(2,1)S(1)}, bf16[1024,2048]{1,0:T(8,128)(2,1)}, u32[]{:S(2)}) %copy-start.4) | copy-done | bytes 4194328
  3.0 0.9 copy-done.6
  3.8 0.7 copy-done.8
  4.5 0.7 copy-done.9
  5.2 2.3 %pick_x.1 = (bf16[16,2048]{1,0:T(8,128)(2,1)S(1)}, bf16[16,2048]{1,0:T(8,128)(2,1)S(1)}, bf16[16,2048]{1,0:T(8,128)(2,1)S(1)}, bf16[16,2048]{1,0:T(8,128)(2,1)S(1)}) custom-call(s32[1,4,16]{2,1,0:T(4,128)S(1)} %copy-done.6, s32[1,4]{1,0:T(1,128)S(1)} %copy-done.9, f32[1,4,16]{2,1,0:T(4,128)S(1)} %copy-done.8, bf16[1024,2048]{1,0:T(8,128)(2,1)S(1)} %copy-done.4), custom_call_target="tpu_custom_call" | custom-call | flops 268435456 | bytes 4194304 | tf_op jit(solution)/shard_map/pick_x/pallas_call | solution.py:81
  7.4 4.0 %collective-permute-start.20 = (bf16[16,2048]{1,0:T(8,128)(2,1)S(1)}, bf16[16,2048]{1,0:T(8,128)(2,1)S(1)}, u32[]{:S(2)}, u32[]{:S(2)}) collective-permute-start(bf16[16,2048]{1,0:T(8,128)(2,1)S(1)} %get-tuple-element.44), channel_id=1, source_target_pairs={{0,10},{1,11},{2,12},{3,13},{4,14},{5,15},{6,8},{7,9},{8,18},{9,19... | collective-permute-start | bytes 196616 | tf_op jit(solution)/shard_map/ppermute | solution.py:300
  11.5 1.5 %collective-permute-start.4 = (bf16[16,2048]{1,0:T(8,128)(2,1)S(1)}, bf16[16,2048]{1,0:T(8,128)(2,1)S(1)}, u32[]{:S(2)}, u32[]{:S(2)}) collective-permute-start(bf16[16,2048]{1,0:T(8,128)(2,1)S(1)} %get-tuple-element.44), channel_id=1, source_target_pairs={{0,8},{1,9},{2,10},{3,11},{4,12},{5,13},{6,14},{7,15},{8,16},{9,17... | collective-permute-start | bytes 196616 | tf_op jit(solution)/shard_map/ppermute | solution.py:300
  12.9 1.5 %collective-permute-start.21 = (bf16[16,2048]{1,0:T(8,128)(2,1)S(1)}, bf16[16,2048]{1,0:T(8,128)(2,1)S(1)}, u32[]{:S(2)}, u32[]{:S(2)}) collective-permute-start(bf16[16,2048]{1,0:T(8,128)(2,1)S(1)} %get-tuple-element.45), channel_id=1, source_target_pairs={{0,18},{1,19},{2,20},{3,21},{4,22},{5,23},{6,16},{7,17},{8,26},{9,... | collective-permute-start | bytes 196616 | tf_op jit(solution)/shard_map/ppermute | solution.py:300
  14.5 1.5 %collective-permute-start.5 = (bf16[16,2048]{1,0:T(8,128)(2,1)S(1)}, bf16[16,2048]{1,0:T(8,128)(2,1)S(1)}, u32[]{:S(2)}, u32[]{:S(2)}) collective-permute-start(bf16[16,2048]{1,0:T(8,128)(2,1)S(1)} %get-tuple-element.45), channel_id=1, source_target_pairs={{0,16},{1,17},{2,18},{3,19},{4,20},{5,21},{6,22},{7,23},{8,24},{9,... | collective-permute-start | bytes 196616 | tf_op jit(solution)/shard_map/ppermute | solution.py:300
  16.0 1.6 %collective-permute-start.19 = (bf16[16,2048]{1,0:T(8,128)(2,1)S(1)}, bf16[16,2048]{1,0:T(8,128)(2,1)S(1)}, u32[]{:S(2)}, u32[]{:S(2)}) collective-permute-start(bf16[16,2048]{1,0:T(8,128)(2,1)S(1)} %get-tuple-element.43), channel_id=1, source_target_pairs={{0,2},{1,3},{2,4},{3,5},{4,6},{5,7},{6,0},{7,1},{8,10},{9,11},{10,... | collective-permute-start | bytes 196616 | tf_op jit(solution)/shard_map/ppermute | solution.py:300
  17.6 2.2 %copy-done.5 = bf16[1024,2048]{1,0:T(8,128)(2,1)S(1)} copy-done((bf16[1024,2048]{1,0:T(8,128)(2,1)S(1)}, bf16[1024,2048]{1,0:T(8,128)(2,1)}, u32[]{:S(2)}) %copy-start.5) | copy-done | bytes 4194328
  19.8 2.4 %pick_grad.1 = (bf16[16,2048]{1,0:T(8,128)(2,1)S(1)}, bf16[16,2048]{1,0:T(8,128)(2,1)S(1)}, bf16[16,2048]{1,0:T(8,128)(2,1)S(1)}, bf16[16,2048]{1,0:T(8,128)(2,1)S(1)}) custom-call(s32[1,4,16]{2,1,0:T(4,128)S(1)} %copy-done.6, s32[1,4]{1,0:T(1,128)S(1)} %copy-done.9, f32[1,4,16]{2,1,0:T(4,128)S(1)} %copy-done.8, bf16[1024,2048]{1,0:T(8,128)(2,1)S(1)} %copy-done.5), custom_call_target="tpu_custom_call" | custom-call | flops 268435456 | bytes 4194304 | tf_op jit(solution)/shard_map/pick_grad/pallas_call | solution.py:81
  22.1 0.3 collective-permute-start.12
  22.4 5.8 %collective-permute-done.12 = bf16[16,2048]{1,0:T(8,128)(2,1)S(1)} collective-permute-done((bf16[16,2048]{1,0:T(8,128)(2,1)S(1)}, bf16[16,2048]{1,0:T(8,128)(2,1)S(1)}, u32[]{:S(2)}, u32[]{:S(2)}) %collective-permute-start.12) | collective-permute-done | bytes 65568 | tf_op jit(solution)/shard_map/ppermute | solution.py:300
  28.3 1.5 %collective-permute-start.6 = (bf16[16,2048]{1,0:T(8,128)(2,1)S(1)}, bf16[16,2048]{1,0:T(8,128)(2,1)S(1)}, u32[]{:S(2)}, u32[]{:S(2)}) collective-permute-start(bf16[16,2048]{1,0:T(8,128)(2,1)S(1)} %get-tuple-element.46), channel_id=1, source_target_pairs={{0,24},{1,25},{2,26},{3,27},{4,28},{5,29},{6,30},{7,31},{8,0},{9,1... | collective-permute-start | bytes 196616 | tf_op jit(solution)/shard_map/ppermute | solution.py:300
  29.8 1.2 collective-permute-start.13
  30.9 4.3 %collective-permute-done.22 = bf16[16,2048]{1,0:T(8,128)(2,1)S(1)} collective-permute-done((bf16[16,2048]{1,0:T(8,128)(2,1)S(1)}, bf16[16,2048]{1,0:T(8,128)(2,1)S(1)}, u32[]{:S(2)}, u32[]{:S(2)}) %collective-permute-start.22) | collective-permute-done | bytes 65568 | tf_op jit(solution)/shard_map/ppermute | solution.py:300
  35.3 2.5 %collective-permute-start = (bf16[16,2048]{1,0:T(8,128)(2,1)S(1)}, bf16[16,2048]{1,0:T(8,128)(2,1)S(1)}, u32[]{:S(2)}, u32[]{:S(2)}) collective-permute-start(bf16[16,2048]{1,0:T(8,128)(2,1)S(1)} %get-tuple-element.40), channel_id=1, source_target_pairs={{0,8},{1,9},{2,10},{3,11},{4,12},{5,13},{6,14},{7,15},{8,16},{9,17... | collective-permute-start | bytes 196616 | tf_op jit(solution)/shard_map/ppermute | solution.py:300
  37.8 0.1 collective-permute-start.14
  37.9 0.5 collective-permute-start.1
  38.4 1.4 %collective-permute-start.15 = (bf16[16,2048]{1,0:T(8,128)(2,1)S(1)}, bf16[16,2048]{1,0:T(8,128)(2,1)S(1)}, u32[]{:S(2)}, u32[]{:S(2)}) collective-permute-start(bf16[16,2048]{1,0:T(8,128)(2,1)S(1)} %get-tuple-element.42), channel_id=1, source_target_pairs={{0,26},{1,27},{2,28},{3,29},{4,30},{5,31},{6,24},{7,25},{8,2},{9,3... | collective-permute-start | bytes 196616 | tf_op jit(solution)/shard_map/ppermute | solution.py:300
  39.8 0.6 collective-permute-start.2
  40.4 5.0 %collective-permute-done.14 = bf16[16,2048]{1,0:T(8,128)(2,1)S(1)} collective-permute-done((bf16[16,2048]{1,0:T(8,128)(2,1)S(1)}, bf16[16,2048]{1,0:T(8,128)(2,1)S(1)}, u32[]{:S(2)}, u32[]{:S(2)}) %collective-permute-start.14) | collective-permute-done | bytes 65568 | tf_op jit(solution)/shard_map/ppermute | solution.py:300
  45.4 0.7 collective-permute-done.15
  46.1 0.6 collective-permute-start.30
  46.7 0.9 collective-permute-done.31.xp.refs_3_
  47.6 2.2 %hidden.7 = (bf16[128,1024]{1,0:T(8,128)(2,1)S(1)}, f32[128,1024]{1,0:T(8,128)S(1)}) custom-call(bf16[64,2048]{1,0:T(8,128)(2,1)S(1)} %constant_dynamic-update-slice_fusion.12.x.refs_2_, bf16[64,2048]{1,0:T(8,128)(2,1)S(1)} %collective-permute-done.31.xp.refs_3_, bf16[1,2048,1024]{2,1,0:T(8,128)(2,1)S(1)} %copy-done), custom_call_target="tpu_custom_call" | custom-call | flops 536870912 | bytes 4194304 | tf_op jit(solution)/shard_map/hidden/pallas_call | solution.py:117
  49.8 5.1 %collective-permute-done.23.x.refs_4_ = bf16[64,2048]{1,0:T(8,128)(2,1)S(1)} collective-permute-done((bf16[64,2048]{1,0:T(8,128)(2,1)S(1)}, bf16[64,2048]{1,0:T(8,128)(2,1)S(1)}, u32[]{:S(2)}, u32[]{:S(2)}) %collective-permute-start.23) | collective-permute-done | bytes 262176 | tf_op jit(solution)/shard_map/ppermute | solution.py:303
  54.9 0.5 collective-permute-start.28
  55.4 7.6 %hidden_grad.7 = (bf16[128,1024]{1,0:T(8,128)(2,1)S(1)}, f32[64,2048]{1,0:T(8,128)S(1)}, bf16[64,2048]{1,0:T(8,128)(2,1)S(1)}) custom-call(bf16[64,2048]{1,0:T(8,128)(2,1)S(1)} %constant_dynamic-update-slice_fusion.8.g.refs_6_, bf16[64,2048]{1,0:T(8,128)(2,1)S(1)} %collective-permute-done.30.gp.refs_7_, bf16[1,1024,2048]{2,1,0:T(8,128)(2,1)} %w_out.7, ...), custom_call_target="tpu_custom_call" | custom-call | flops 1073741824 | bytes 8388608 | tf_op jit(solution)/shard_map/hidden_grad/pallas_call | solution.py:172
  63.1 0.1 collective-permute-start.32
  63.2 0.1 collective-permute-start.24
  63.3 0.1 collective-permute-start.17
  63.3 0.5 collective-permute-start.27
  63.9 0.8 collective-permute-done.32.refs_1_
  64.7 0.1 collective-permute-start.3
  64.9 2.2 %hidden.6 = (bf16[128,1024]{1,0:T(8,128)(2,1)S(1)}, f32[128,1024]{1,0:T(8,128)S(1)}) custom-call(bf16[64,2048]{1,0:T(8,128)(2,1)S(1)} %collective-permute-done.23.x.refs_4_, bf16[64,2048]{1,0:T(8,128)(2,1)S(1)} %collective-permute-done.28.xp.refs_5_, bf16[1,2048,1024]{2,1,0:T(8,128)(2,1)S(1)} %copy-done.1), custom_call_target="tpu_custom_call" | custom-call | flops 536870912 | bytes 4194304 | tf_op jit(solution)/shard_map/hidden/pallas_call | solution.py:117
  67.1 0.1 collective-permute-start.33
  67.2 0.0 copy-start.2
  67.2 7.6 %hidden_grad.6 = (bf16[128,1024]{1,0:T(8,128)(2,1)S(1)}, f32[64,2048]{1,0:T(8,128)S(1)}, bf16[64,2048]{1,0:T(8,128)(2,1)S(1)}) custom-call(bf16[64,2048]{1,0:T(8,128)(2,1)S(1)} %collective-permute-done.16.g.refs_8_, bf16[64,2048]{1,0:T(8,128)(2,1)S(1)} %collective-permute-done.27.gp.refs_9_, bf16[1,1024,2048]{2,1,0:T(8,128)(2,1)} %w_out.7, ...), custom_call_target="tpu_custom_call" | custom-call | flops 1073741824 | bytes 8388608 | tf_op jit(solution)/shard_map/hidden_grad/pallas_call | solution.py:172
  74.8 0.4 collective-permute-start.29
  75.3 0.1 collective-permute-start.25
  75.4 4.3 %collective-permute-done.17.g.refs_10_ = bf16[64,2048]{1,0:T(8,128)(2,1)S(1)} collective-permute-done((bf16[64,2048]{1,0:T(8,128)(2,1)S(1)}, bf16[64,2048]{1,0:T(8,128)(2,1)S(1)}, u32[]{:S(2)}, u32[]{:S(2)}) %collective-permute-start.17) | collective-permute-done | bytes 262176 | tf_op jit(solution)/shard_map/ppermute | solution.py:303
  79.8 2.2 %hidden.4 = (bf16[128,1024]{1,0:T(8,128)(2,1)S(1)}, f32[128,1024]{1,0:T(8,128)S(1)}) custom-call(bf16[64,2048]{1,0:T(8,128)(2,1)S(1)} %constant_dynamic-update-slice_fusion.4.x.refs_0_, bf16[64,2048]{1,0:T(8,128)(2,1)S(1)} %collective-permute-done.7.xp.refs_1_, bf16[1,2048,1024]{2,1,0:T(8,128)(2,1)S(1)} %copy-done.2), custom_call_target="tpu_custom_call" | custom-call | flops 536870912 | bytes 4194304 | tf_op jit(solution)/shard_map/hidden/pallas_call | solution.py:117
  82.0 7.6 %hidden_grad.4 = (bf16[128,1024]{1,0:T(8,128)(2,1)S(1)}, f32[64,2048]{1,0:T(8,128)S(1)}, bf16[64,2048]{1,0:T(8,128)(2,1)S(1)}) custom-call(bf16[64,2048]{1,0:T(8,128)(2,1)S(1)} %constant_dynamic-update-slice_fusion.g.refs_4_, bf16[64,2048]{1,0:T(8,128)(2,1)S(1)} %collective-permute-done.3.gp.refs_5_, bf16[1,1024,2048]{2,1,0:T(8,128)(2,1)} %w_out.7, ...), custom_call_target="tpu_custom_call" | custom-call | flops 1073741824 | bytes 8388608 | tf_op jit(solution)/shard_map/hidden_grad/pallas_call | solution.py:172
  89.6 0.6 collective-permute-start.8
  90.2 0.1 add_up.6
  90.3 0.1 collective-permute-start.34
  90.4 2.2 %hidden.5 = (bf16[128,1024]{1,0:T(8,128)(2,1)S(1)}, f32[128,1024]{1,0:T(8,128)S(1)}) custom-call(bf16[64,2048]{1,0:T(8,128)(2,1)S(1)} %collective-permute-done.24.x.refs_6_, bf16[64,2048]{1,0:T(8,128)(2,1)S(1)} %collective-permute-done.25.xp.refs_7_, bf16[1,2048,1024]{2,1,0:T(8,128)(2,1)S(1)} %copy-done.3), custom_call_target="tpu_custom_call" | custom-call | flops 536870912 | bytes 4194304 | tf_op jit(solution)/shard_map/hidden/pallas_call | solution.py:117
  92.6 7.5 %hidden_grad.5 = (bf16[128,1024]{1,0:T(8,128)(2,1)S(1)}, f32[64,2048]{1,0:T(8,128)S(1)}, bf16[64,2048]{1,0:T(8,128)(2,1)S(1)}) custom-call(bf16[64,2048]{1,0:T(8,128)(2,1)S(1)} %collective-permute-done.17.g.refs_10_, bf16[64,2048]{1,0:T(8,128)(2,1)S(1)} %collective-permute-done.18.gp.refs_11_, bf16[1,1024,2048]{2,1,0:T(8,128)(2,1)} %w_out.7, ...), custom_call_target="tpu_custom_call" | custom-call | flops 1073741824 | bytes 8388608 | tf_op jit(solution)/shard_map/hidden_grad/pallas_call | solution.py:172
  100.1 0.1 collective-permute-start.26
  100.3 0.1 collective-permute-start.10
  100.4 0.1 collective-permute-start.11
  100.4 2.9 %collective-permute-start.9 = (bf16[16,2048]{1,0:T(8,128)(2,1)S(1)}, bf16[16,2048]{1,0:T(8,128)(2,1)S(1)}, u32[]{:S(2)}, u32[]{:S(2)}) collective-permute-start(bf16[16,2048]{1,0:T(8,128)(2,1)S(1)} %get-tuple-element.51), channel_id=1, source_target_pairs={{0,24},{1,25},{2,26},{3,27},{4,28},{5,29},{6,30},{7,31},{8,0},{9,1... | collective-permute-start | bytes 196616 | tf_op jit(solution)/shard_map/ppermute | solution.py:300
  103.3 5.0 %grad_w_out.1 = f32[1,1024,2048]{2,1,0:T(8,128)} custom-call(bf16[128,1024]{1,0:T(8,128)(2,1)S(1)} %get-tuple-element.71.refs_0_, bf16[128,1024]{1,0:T(8,128)(2,1)S(1)} %get-tuple-element.72.refs_1_, bf16[128,1024]{1,0:T(8,128)(2,1)S(1)} %get-tuple-element.73.refs_2_, bf16[128,1024]{1,0:T(8,128)(2,1)S(1)} %get-tuple-element.74.refs_3_, ...), custom_call_target="tpu_custom_call" | custom-call | flops 2147483648 | bytes 8388608 | tf_op jit(solution)/shard_map/grad_w_out/pallas_call | solution.py:210
  108.4 0.1 add_up.7
  108.5 0.1 collective-permute-start.35
  108.5 0.5 collective-permute-start.36
  109.1 5.2 %collective-permute-start.37 = (bf16[16,2048]{1,0:T(8,128)(2,1)S(1)}, bf16[16,2048]{1,0:T(8,128)(2,1)S(1)}, u32[]{:S(2)}, u32[]{:S(2)}) collective-permute-start(bf16[16,2048]{1,0:T(8,128)(2,1)S(1)} %get-tuple-element.65), channel_id=1, source_target_pairs={{0,18},{1,19},{2,20},{3,21},{4,22},{5,23},{6,16},{7,17},{8,26},{9,... | collective-permute-start | bytes 196616 | tf_op jit(solution)/shard_map/ppermute | solution.py:300
  114.2 1.5 %collective-permute-start.38 = (bf16[16,2048]{1,0:T(8,128)(2,1)S(1)}, bf16[16,2048]{1,0:T(8,128)(2,1)S(1)}, u32[]{:S(2)}, u32[]{:S(2)}) collective-permute-start(bf16[16,2048]{1,0:T(8,128)(2,1)S(1)} %get-tuple-element.66), channel_id=1, source_target_pairs={{0,10},{1,11},{2,12},{3,13},{4,14},{5,15},{6,8},{7,9},{8,18},{9,19... | collective-permute-start | bytes 196616 | tf_op jit(solution)/shard_map/ppermute | solution.py:300
  115.8 5.1 %grad_w_in.1 = f32[1,2048,1024]{2,1,0:T(8,128)} custom-call(bf16[64,2048]{1,0:T(8,128)(2,1)S(1)} %constant_dynamic-update-slice_fusion.4.x.refs_0_, bf16[64,2048]{1,0:T(8,128)(2,1)S(1)} %collective-permute-done.7.xp.refs_1_, bf16[64,2048]{1,0:T(8,128)(2,1)S(1)} %constant_dynamic-update-slice_fusion.12.x.refs_2_, ...), custom_call_target="tpu_custom_call" | custom-call | flops 2147483648 | bytes 8388608 | tf_op jit(solution)/shard_map/grad_w_in/pallas_call | solution.py:210
  120.9 1.2 collective-permute-done.38.rest_7_
  122.1 4.0 %place.1 = bf16[1024,2048]{1,0:T(8,128)(2,1)} custom-call(s32[1,4,16]{2,1,0:T(4,128)S(1)} %copy-done.7, bf16[16,2048]{1,0:T(8,128)(2,1)S(1)} %get-tuple-element.50.rest_0_, bf16[16,2048]{1,0:T(8,128)(2,1)S(1)} %collective-permute-done.9.rest_1_, bf16[16,2048]{1,0:T(8,128)(2,1)S(1)} %collective-permute-done.10.rest_2_, ...), custom_call_target="tpu_custom_call" | custom-call | flops 536870912 | bytes 4194304 | tf_op jit(solution)/shard_map/place/pallas_call | solution.py:276
  (67 shorter events, 0.3 us)
Async XLA Ops:
  0.6 47.0 %copy-start = (bf16[1,2048,1024]{2,1,0:T(8,128)(2,1)S(1)}, bf16[1,2048,1024]{2,1,0:T(8,128)(2,1)}, u32[]{:S(2)}) copy-start(bf16[1,2048,1024]{2,1,0:T(8,128)(2,1)} %w_in.7) | copy-start | bytes 12582916
  0.6 2.3 %copy-start.4 = (bf16[1024,2048]{1,0:T(8,128)(2,1)S(1)}, bf16[1024,2048]{1,0:T(8,128)(2,1)}, u32[]{:S(2)}) copy-start(bf16[1024,2048]{1,0:T(8,128)(2,1)} %tokens.3) | copy-start | bytes 12582916
  3.0 0.9 copy-start.6
  3.8 0.7 copy-start.8
  4.5 0.7 copy-start.9
  7.4 20.8 %collective-permute-start.20 = (bf16[16,2048]{1,0:T(8,128)(2,1)S(1)}, bf16[16,2048]{1,0:T(8,128)(2,1)S(1)}, u32[]{:S(2)}, u32[]{:S(2)}) collective-permute-start(bf16[16,2048]{1,0:T(8,128)(2,1)S(1)} %get-tuple-element.44), channel_id=1, source_target_pairs={{0,10},{1,11},{2,12},{3,13},{4,14},{5,15},{6,8},{7,9},{8,18},{9,19... | collective-permute-start | bytes 196616 | tf_op jit(solution)/shard_map/ppermute | solution.py:300
  11.5 26.3 %collective-permute-start.4 = (bf16[16,2048]{1,0:T(8,128)(2,1)S(1)}, bf16[16,2048]{1,0:T(8,128)(2,1)S(1)}, u32[]{:S(2)}, u32[]{:S(2)}) collective-permute-start(bf16[16,2048]{1,0:T(8,128)(2,1)S(1)} %get-tuple-element.44), channel_id=1, source_target_pairs={{0,8},{1,9},{2,10},{3,11},{4,12},{5,13},{6,14},{7,15},{8,16},{9,17... | collective-permute-start | bytes 196616 | tf_op jit(solution)/shard_map/ppermute | solution.py:300
  12.9 16.8 %collective-permute-start.21 = (bf16[16,2048]{1,0:T(8,128)(2,1)S(1)}, bf16[16,2048]{1,0:T(8,128)(2,1)S(1)}, u32[]{:S(2)}, u32[]{:S(2)}) collective-permute-start(bf16[16,2048]{1,0:T(8,128)(2,1)S(1)} %get-tuple-element.45), channel_id=1, source_target_pairs={{0,18},{1,19},{2,20},{3,21},{4,22},{5,23},{6,16},{7,17},{8,26},{9,... | collective-permute-start | bytes 196616 | tf_op jit(solution)/shard_map/ppermute | solution.py:300
  14.5 23.4 %collective-permute-start.5 = (bf16[16,2048]{1,0:T(8,128)(2,1)S(1)}, bf16[16,2048]{1,0:T(8,128)(2,1)S(1)}, u32[]{:S(2)}, u32[]{:S(2)}) collective-permute-start(bf16[16,2048]{1,0:T(8,128)(2,1)S(1)} %get-tuple-element.45), channel_id=1, source_target_pairs={{0,16},{1,17},{2,18},{3,19},{4,20},{5,21},{6,22},{7,23},{8,24},{9,... | collective-permute-start | bytes 196616 | tf_op jit(solution)/shard_map/ppermute | solution.py:300
  16.0 6.2 %collective-permute-start.19 = (bf16[16,2048]{1,0:T(8,128)(2,1)S(1)}, bf16[16,2048]{1,0:T(8,128)(2,1)S(1)}, u32[]{:S(2)}, u32[]{:S(2)}) collective-permute-start(bf16[16,2048]{1,0:T(8,128)(2,1)S(1)} %get-tuple-element.43), channel_id=1, source_target_pairs={{0,2},{1,3},{2,4},{3,5},{4,6},{5,7},{6,0},{7,1},{8,10},{9,11},{10,... | collective-permute-start | bytes 196616 | tf_op jit(solution)/shard_map/ppermute | solution.py:300
  17.6 2.2 %copy-start.5 = (bf16[1024,2048]{1,0:T(8,128)(2,1)S(1)}, bf16[1024,2048]{1,0:T(8,128)(2,1)}, u32[]{:S(2)}) copy-start(bf16[1024,2048]{1,0:T(8,128)(2,1)} %tokens.2) | copy-start | bytes 12582916
  22.1 6.1 %collective-permute-start.12 = (bf16[16,2048]{1,0:T(8,128)(2,1)S(1)}, bf16[16,2048]{1,0:T(8,128)(2,1)S(1)}, u32[]{:S(2)}, u32[]{:S(2)}) collective-permute-start(bf16[16,2048]{1,0:T(8,128)(2,1)S(1)} %get-tuple-element.39), channel_id=1, source_target_pairs={{0,2},{1,3},{2,4},{3,5},{4,6},{5,7},{6,0},{7,1},{8,10},{9,11},{10,... | collective-permute-start | bytes 196616 | tf_op jit(solution)/shard_map/ppermute | solution.py:300
  28.3 7.0 %collective-permute-start.22 = (bf16[16,2048]{1,0:T(8,128)(2,1)S(1)}, bf16[16,2048]{1,0:T(8,128)(2,1)S(1)}, u32[]{:S(2)}, u32[]{:S(2)}) collective-permute-start(bf16[16,2048]{1,0:T(8,128)(2,1)S(1)} %get-tuple-element.46), channel_id=1, source_target_pairs={{0,26},{1,27},{2,28},{3,29},{4,30},{5,31},{6,24},{7,25},{8,2},{9,3... | collective-permute-start | bytes 196616 | tf_op jit(solution)/shard_map/ppermute | solution.py:300
  28.3 10.1 %collective-permute-start.6 = (bf16[16,2048]{1,0:T(8,128)(2,1)S(1)}, bf16[16,2048]{1,0:T(8,128)(2,1)S(1)}, u32[]{:S(2)}, u32[]{:S(2)}) collective-permute-start(bf16[16,2048]{1,0:T(8,128)(2,1)S(1)} %get-tuple-element.46), channel_id=1, source_target_pairs={{0,24},{1,25},{2,26},{3,27},{4,28},{5,29},{6,30},{7,31},{8,0},{9,1... | collective-permute-start | bytes 196616 | tf_op jit(solution)/shard_map/ppermute | solution.py:300
  29.8 10.0 %collective-permute-start.13 = (bf16[16,2048]{1,0:T(8,128)(2,1)S(1)}, bf16[16,2048]{1,0:T(8,128)(2,1)S(1)}, u32[]{:S(2)}, u32[]{:S(2)}) collective-permute-start(bf16[16,2048]{1,0:T(8,128)(2,1)S(1)} %get-tuple-element.40), channel_id=1, source_target_pairs={{0,10},{1,11},{2,12},{3,13},{4,14},{5,15},{6,8},{7,9},{8,18},{9,19... | collective-permute-start | bytes 196616 | tf_op jit(solution)/shard_map/ppermute | solution.py:300
  35.3 10.8 %collective-permute-start = (bf16[16,2048]{1,0:T(8,128)(2,1)S(1)}, bf16[16,2048]{1,0:T(8,128)(2,1)S(1)}, u32[]{:S(2)}, u32[]{:S(2)}) collective-permute-start(bf16[16,2048]{1,0:T(8,128)(2,1)S(1)} %get-tuple-element.40), channel_id=1, source_target_pairs={{0,8},{1,9},{2,10},{3,11},{4,12},{5,13},{6,14},{7,15},{8,16},{9,17... | collective-permute-start | bytes 196616 | tf_op jit(solution)/shard_map/ppermute | solution.py:300
  37.8 7.6 %collective-permute-start.14 = (bf16[16,2048]{1,0:T(8,128)(2,1)S(1)}, bf16[16,2048]{1,0:T(8,128)(2,1)S(1)}, u32[]{:S(2)}, u32[]{:S(2)}) collective-permute-start(bf16[16,2048]{1,0:T(8,128)(2,1)S(1)} %get-tuple-element.41), channel_id=1, source_target_pairs={{0,18},{1,19},{2,20},{3,21},{4,22},{5,23},{6,16},{7,17},{8,26},{9,... | collective-permute-start | bytes 196616 | tf_op jit(solution)/shard_map/ppermute | solution.py:300
  37.9 25.2 %collective-permute-start.1 = (bf16[16,2048]{1,0:T(8,128)(2,1)S(1)}, bf16[16,2048]{1,0:T(8,128)(2,1)S(1)}, u32[]{:S(2)}, u32[]{:S(2)}) collective-permute-start(bf16[16,2048]{1,0:T(8,128)(2,1)S(1)} %get-tuple-element.41), channel_id=1, source_target_pairs={{0,16},{1,17},{2,18},{3,19},{4,20},{5,21},{6,22},{7,23},{8,24},{9,... | collective-permute-start | bytes 196616 | tf_op jit(solution)/shard_map/ppermute | solution.py:300
  38.4 7.7 %collective-permute-start.15 = (bf16[16,2048]{1,0:T(8,128)(2,1)S(1)}, bf16[16,2048]{1,0:T(8,128)(2,1)S(1)}, u32[]{:S(2)}, u32[]{:S(2)}) collective-permute-start(bf16[16,2048]{1,0:T(8,128)(2,1)S(1)} %get-tuple-element.42), channel_id=1, source_target_pairs={{0,26},{1,27},{2,28},{3,29},{4,30},{5,31},{6,24},{7,25},{8,2},{9,3... | collective-permute-start | bytes 196616 | tf_op jit(solution)/shard_map/ppermute | solution.py:300
  39.8 23.4 %collective-permute-start.2 = (bf16[16,2048]{1,0:T(8,128)(2,1)S(1)}, bf16[16,2048]{1,0:T(8,128)(2,1)S(1)}, u32[]{:S(2)}, u32[]{:S(2)}) collective-permute-start(bf16[16,2048]{1,0:T(8,128)(2,1)S(1)} %get-tuple-element.42), channel_id=1, source_target_pairs={{0,24},{1,25},{2,26},{3,27},{4,28},{5,29},{6,30},{7,31},{8,0},{9,1... | collective-permute-start | bytes 196616 | tf_op jit(solution)/shard_map/ppermute | solution.py:300
  45.4 9.5 %collective-permute-start.23 = (bf16[64,2048]{1,0:T(8,128)(2,1)S(1)}, bf16[64,2048]{1,0:T(8,128)(2,1)S(1)}, u32[]{:S(2)}, u32[]{:S(2)}) collective-permute-start(bf16[64,2048]{1,0:T(8,128)(2,1)S(1)} %constant_dynamic-update-slice_fusion.12.x.refs_2_), channel_id=1, source_target_pairs={{0,2},{1,3},{2,4},{3,5},{4,6},{5,7},{6,0},{7,1},{8,10},{9,11},{10,... | collective-permute-start | bytes 786440 | tf_op jit(solution)/shard_map/ppermute | solution.py:303
  46.1 1.5 %collective-permute-start.31 = (bf16[64,2048]{1,0:T(8,128)(2,1)S(1)}, bf16[64,2048]{1,0:T(8,128)(2,1)S(1)}, u32[]{:S(2)}, u32[]{:S(2)}) collective-permute-start(bf16[64,2048]{1,0:T(8,128)(2,1)S(1)} %constant_dynamic-update-slice_fusion.12.x.refs_2_), channel_id=1, source_target_pairs={{0,1},{1,0},{2,3},{3,2},{4,5},{5,4},{6,7},{7,6},{8,9},{9,8},{10,11... | collective-permute-start | bytes 786440 | tf_op jit(solution)/shard_map/ppermute | solution.py:306
  46.1 8.8 %collective-permute-start.30 = (bf16[64,2048]{1,0:T(8,128)(2,1)S(1)}, bf16[64,2048]{1,0:T(8,128)(2,1)S(1)}, u32[]{:S(2)}, u32[]{:S(2)}) collective-permute-start(bf16[64,2048]{1,0:T(8,128)(2,1)S(1)} %constant_dynamic-update-slice_fusion.8.g.refs_6_), channel_id=1, source_target_pairs={{0,1},{1,0},{2,3},{3,2},{4,5},{5,4},{6,7},{7,6},{8,9},{9,8},{10,11... | collective-permute-start | bytes 786440 | tf_op jit(solution)/shard_map/ppermute | solution.py:306
  47.6 15.6 %collective-permute-start.16 = (bf16[64,2048]{1,0:T(8,128)(2,1)S(1)}, bf16[64,2048]{1,0:T(8,128)(2,1)S(1)}, u32[]{:S(2)}, u32[]{:S(2)}) collective-permute-start(bf16[64,2048]{1,0:T(8,128)(2,1)S(1)} %constant_dynamic-update-slice_fusion.8.g.refs_6_), channel_id=1, source_target_pairs={{0,2},{1,3},{2,4},{3,5},{4,6},{5,7},{6,0},{7,1},{8,10},{9,11},{10,... | collective-permute-start | bytes 786440 | tf_op jit(solution)/shard_map/ppermute | solution.py:303
  54.9 19.9 %collective-permute-start.7 = (bf16[64,2048]{1,0:T(8,128)(2,1)S(1)}, bf16[64,2048]{1,0:T(8,128)(2,1)S(1)}, u32[]{:S(2)}, u32[]{:S(2)}) collective-permute-start(bf16[64,2048]{1,0:T(8,128)(2,1)S(1)} %constant_dynamic-update-slice_fusion.4.x.refs_0_), channel_id=1, source_target_pairs={{0,1},{1,0},{2,3},{3,2},{4,5},{5,4},{6,7},{7,6},{8,9},{9,8},{10,11... | collective-permute-start | bytes 786440 | tf_op jit(solution)/shard_map/ppermute | solution.py:306
  54.9 8.4 %collective-permute-start.28 = (bf16[64,2048]{1,0:T(8,128)(2,1)S(1)}, bf16[64,2048]{1,0:T(8,128)(2,1)S(1)}, u32[]{:S(2)}, u32[]{:S(2)}) collective-permute-start(bf16[64,2048]{1,0:T(8,128)(2,1)S(1)} %collective-permute-done.23.x.refs_4_), channel_id=1, source_target_pairs={{0,1},{1,0},{2,3},{3,2},{4,5},{5,4},{6,7},{7,6},{8,9},{9,8},{10,11... | collective-permute-start | bytes 786440 | tf_op jit(solution)/shard_map/ppermute | solution.py:306
  55.4 9.4 %copy-start.1 = (bf16[1,2048,1024]{2,1,0:T(8,128)(2,1)S(1)}, bf16[1,2048,1024]{2,1,0:T(8,128)(2,1)}, u32[]{:S(2)}) copy-start(bf16[1,2048,1024]{2,1,0:T(8,128)(2,1)} %w_in.7) | copy-start | bytes 12582916
  63.1 1.6 %collective-permute-start.32 = (bf16[64,2048]{1,0:T(8,128)(2,1)S(1)}, bf16[64,2048]{1,0:T(8,128)(2,1)S(1)}, u32[]{:S(2)}, u32[]{:S(2)}) collective-permute-start(bf16[64,2048]{1,0:T(8,128)(2,1)S(1)} %get-tuple-element.62), channel_id=1, source_target_pairs={{0,1},{1,0},{2,3},{3,2},{4,5},{5,4},{6,7},{7,6},{8,9},{9,8},{10,11... | collective-permute-start | bytes 786440 | tf_op jit(solution)/shard_map/ppermute | solution.py:306
  63.2 12.1 %collective-permute-start.24 = (bf16[64,2048]{1,0:T(8,128)(2,1)S(1)}, bf16[64,2048]{1,0:T(8,128)(2,1)S(1)}, u32[]{:S(2)}, u32[]{:S(2)}) collective-permute-start(bf16[64,2048]{1,0:T(8,128)(2,1)S(1)} %collective-permute-done.23.x.refs_4_), channel_id=1, source_target_pairs={{0,2},{1,3},{2,4},{3,5},{4,6},{5,7},{6,0},{7,1},{8,10},{9,11},{10,... | collective-permute-start | bytes 786440 | tf_op jit(solution)/shard_map/ppermute | solution.py:303
  63.3 16.5 %collective-permute-start.17 = (bf16[64,2048]{1,0:T(8,128)(2,1)S(1)}, bf16[64,2048]{1,0:T(8,128)(2,1)S(1)}, u32[]{:S(2)}, u32[]{:S(2)}) collective-permute-start(bf16[64,2048]{1,0:T(8,128)(2,1)S(1)} %collective-permute-done.16.g.refs_8_), channel_id=1, source_target_pairs={{0,2},{1,3},{2,4},{3,5},{4,6},{5,7},{6,0},{7,1},{8,10},{9,11},{10,... | collective-permute-start | bytes 786440 | tf_op jit(solution)/shard_map/ppermute | solution.py:303
  63.3 3.8 %collective-permute-start.27 = (bf16[64,2048]{1,0:T(8,128)(2,1)S(1)}, bf16[64,2048]{1,0:T(8,128)(2,1)S(1)}, u32[]{:S(2)}, u32[]{:S(2)}) collective-permute-start(bf16[64,2048]{1,0:T(8,128)(2,1)S(1)} %collective-permute-done.16.g.refs_8_), channel_id=1, source_target_pairs={{0,1},{1,0},{2,3},{3,2},{4,5},{5,4},{6,7},{7,6},{8,9},{9,8},{10,11... | collective-permute-start | bytes 786440 | tf_op jit(solution)/shard_map/ppermute | solution.py:306
  64.7 17.3 %collective-permute-start.3 = (bf16[64,2048]{1,0:T(8,128)(2,1)S(1)}, bf16[64,2048]{1,0:T(8,128)(2,1)S(1)}, u32[]{:S(2)}, u32[]{:S(2)}) collective-permute-start(bf16[64,2048]{1,0:T(8,128)(2,1)S(1)} %constant_dynamic-update-slice_fusion.g.refs_4_), channel_id=1, source_target_pairs={{0,1},{1,0},{2,3},{3,2},{4,5},{5,4},{6,7},{7,6},{8,9},{9,8},{10,11... | collective-permute-start | bytes 786440 | tf_op jit(solution)/shard_map/ppermute | solution.py:306
  67.1 23.1 %collective-permute-start.33 = (bf16[64,2048]{1,0:T(8,128)(2,1)S(1)}, bf16[64,2048]{1,0:T(8,128)(2,1)S(1)}, u32[]{:S(2)}, u32[]{:S(2)}) collective-permute-start(bf16[64,2048]{1,0:T(8,128)(2,1)S(1)} %add_up.5), channel_id=1, source_target_pairs={{0,2},{1,3},{2,4},{3,5},{4,6},{5,7},{6,0},{7,1},{8,10},{9,11},{10,... | collective-permute-start | bytes 786440 | tf_op jit(solution)/shard_map/ppermute | solution.py:303
  67.2 12.6 %copy-start.2 = (bf16[1,2048,1024]{2,1,0:T(8,128)(2,1)S(1)}, bf16[1,2048,1024]{2,1,0:T(8,128)(2,1)}, u32[]{:S(2)}) copy-start(bf16[1,2048,1024]{2,1,0:T(8,128)(2,1)} %w_in.7) | copy-start | bytes 12582916
  74.8 15.4 %collective-permute-start.29 = (bf16[64,2048]{1,0:T(8,128)(2,1)S(1)}, bf16[64,2048]{1,0:T(8,128)(2,1)S(1)}, u32[]{:S(2)}, u32[]{:S(2)}) collective-permute-start(bf16[64,2048]{1,0:T(8,128)(2,1)S(1)} %get-tuple-element.59), channel_id=1, source_target_pairs={{0,1},{1,0},{2,3},{3,2},{4,5},{5,4},{6,7},{7,6},{8,9},{9,8},{10,11... | collective-permute-start | bytes 786440 | tf_op jit(solution)/shard_map/ppermute | solution.py:306
  75.3 15.1 %collective-permute-start.25 = (bf16[64,2048]{1,0:T(8,128)(2,1)S(1)}, bf16[64,2048]{1,0:T(8,128)(2,1)S(1)}, u32[]{:S(2)}, u32[]{:S(2)}) collective-permute-start(bf16[64,2048]{1,0:T(8,128)(2,1)S(1)} %collective-permute-done.24.x.refs_6_), channel_id=1, source_target_pairs={{0,1},{1,0},{2,3},{3,2},{4,5},{5,4},{6,7},{7,6},{8,9},{9,8},{10,11... | collective-permute-start | bytes 786440 | tf_op jit(solution)/shard_map/ppermute | solution.py:306
  79.7 12.9 %collective-permute-start.18 = (bf16[64,2048]{1,0:T(8,128)(2,1)S(1)}, bf16[64,2048]{1,0:T(8,128)(2,1)S(1)}, u32[]{:S(2)}, u32[]{:S(2)}) collective-permute-start(bf16[64,2048]{1,0:T(8,128)(2,1)S(1)} %collective-permute-done.17.g.refs_10_), channel_id=1, source_target_pairs={{0,1},{1,0},{2,3},{3,2},{4,5},{5,4},{6,7},{7,6},{8,9},{9,8},{10,11... | collective-permute-start | bytes 786440 | tf_op jit(solution)/shard_map/ppermute | solution.py:306
  82.0 8.4 %copy-start.3 = (bf16[1,2048,1024]{2,1,0:T(8,128)(2,1)S(1)}, bf16[1,2048,1024]{2,1,0:T(8,128)(2,1)}, u32[]{:S(2)}) copy-start(bf16[1,2048,1024]{2,1,0:T(8,128)(2,1)} %w_in.7) | copy-start | bytes 12582916
  89.6 10.6 %collective-permute-start.8 = (bf16[64,2048]{1,0:T(8,128)(2,1)S(1)}, bf16[64,2048]{1,0:T(8,128)(2,1)S(1)}, u32[]{:S(2)}, u32[]{:S(2)}) collective-permute-start(bf16[64,2048]{1,0:T(8,128)(2,1)S(1)} %get-tuple-element.49), channel_id=1, source_target_pairs={{0,1},{1,0},{2,3},{3,2},{4,5},{5,4},{6,7},{7,6},{8,9},{9,8},{10,11... | collective-permute-start | bytes 786440 | tf_op jit(solution)/shard_map/ppermute | solution.py:306
  90.3 18.1 %collective-permute-start.34 = (bf16[64,2048]{1,0:T(8,128)(2,1)S(1)}, bf16[64,2048]{1,0:T(8,128)(2,1)S(1)}, u32[]{:S(2)}, u32[]{:S(2)}) collective-permute-start(bf16[64,2048]{1,0:T(8,128)(2,1)S(1)} %add_up.6), channel_id=1, source_target_pairs={{0,2},{1,3},{2,4},{3,5},{4,6},{5,7},{6,0},{7,1},{8,10},{9,11},{10,... | collective-permute-start | bytes 786440 | tf_op jit(solution)/shard_map/ppermute | solution.py:303
  100.1 8.2 %collective-permute-start.26 = (bf16[64,2048]{1,0:T(8,128)(2,1)S(1)}, bf16[64,2048]{1,0:T(8,128)(2,1)S(1)}, u32[]{:S(2)}, u32[]{:S(2)}) collective-permute-start(bf16[64,2048]{1,0:T(8,128)(2,1)S(1)} %get-tuple-element.56), channel_id=1, source_target_pairs={{0,1},{1,0},{2,3},{3,2},{4,5},{5,4},{6,7},{7,6},{8,9},{9,8},{10,11... | collective-permute-start | bytes 786440 | tf_op jit(solution)/shard_map/ppermute | solution.py:306
  100.3 8.8 %collective-permute-start.10 = (bf16[16,2048]{1,0:T(8,128)(2,1)S(1)}, bf16[16,2048]{1,0:T(8,128)(2,1)S(1)}, u32[]{:S(2)}, u32[]{:S(2)}) collective-permute-start(bf16[16,2048]{1,0:T(8,128)(2,1)S(1)} %get-tuple-element.52), channel_id=1, source_target_pairs={{0,16},{1,17},{2,18},{3,19},{4,20},{5,21},{6,22},{7,23},{8,24},{9,... | collective-permute-start | bytes 196616 | tf_op jit(solution)/shard_map/ppermute | solution.py:300
  100.4 13.9 %collective-permute-start.11 = (bf16[16,2048]{1,0:T(8,128)(2,1)S(1)}, bf16[16,2048]{1,0:T(8,128)(2,1)S(1)}, u32[]{:S(2)}, u32[]{:S(2)}) collective-permute-start(bf16[16,2048]{1,0:T(8,128)(2,1)S(1)} %get-tuple-element.53), channel_id=1, source_target_pairs={{0,8},{1,9},{2,10},{3,11},{4,12},{5,13},{6,14},{7,15},{8,16},{9,17... | collective-permute-start | bytes 196616 | tf_op jit(solution)/shard_map/ppermute | solution.py:300
  100.4 20.4 %collective-permute-start.9 = (bf16[16,2048]{1,0:T(8,128)(2,1)S(1)}, bf16[16,2048]{1,0:T(8,128)(2,1)S(1)}, u32[]{:S(2)}, u32[]{:S(2)}) collective-permute-start(bf16[16,2048]{1,0:T(8,128)(2,1)S(1)} %get-tuple-element.51), channel_id=1, source_target_pairs={{0,24},{1,25},{2,26},{3,27},{4,28},{5,29},{6,30},{7,31},{8,0},{9,1... | collective-permute-start | bytes 196616 | tf_op jit(solution)/shard_map/ppermute | solution.py:300
  108.5 12.4 %collective-permute-start.35 = (bf16[16,2048]{1,0:T(8,128)(2,1)S(1)}, bf16[16,2048]{1,0:T(8,128)(2,1)S(1)}, u32[]{:S(2)}, u32[]{:S(2)}) collective-permute-start(bf16[16,2048]{1,0:T(8,128)(2,1)S(1)} %get-tuple-element.63), channel_id=1, source_target_pairs={{0,2},{1,3},{2,4},{3,5},{4,6},{5,7},{6,0},{7,1},{8,10},{9,11},{10,... | collective-permute-start | bytes 196616 | tf_op jit(solution)/shard_map/ppermute | solution.py:300
  108.5 12.3 %collective-permute-start.36 = (bf16[16,2048]{1,0:T(8,128)(2,1)S(1)}, bf16[16,2048]{1,0:T(8,128)(2,1)S(1)}, u32[]{:S(2)}, u32[]{:S(2)}) collective-permute-start(bf16[16,2048]{1,0:T(8,128)(2,1)S(1)} %get-tuple-element.64), channel_id=1, source_target_pairs={{0,26},{1,27},{2,28},{3,29},{4,30},{5,31},{6,24},{7,25},{8,2},{9,3... | collective-permute-start | bytes 196616 | tf_op jit(solution)/shard_map/ppermute | solution.py:300
  109.1 11.8 %collective-permute-start.37 = (bf16[16,2048]{1,0:T(8,128)(2,1)S(1)}, bf16[16,2048]{1,0:T(8,128)(2,1)S(1)}, u32[]{:S(2)}, u32[]{:S(2)}) collective-permute-start(bf16[16,2048]{1,0:T(8,128)(2,1)S(1)} %get-tuple-element.65), channel_id=1, source_target_pairs={{0,18},{1,19},{2,20},{3,21},{4,22},{5,23},{6,16},{7,17},{8,26},{9,... | collective-permute-start | bytes 196616 | tf_op jit(solution)/shard_map/ppermute | solution.py:300
  114.2 7.9 %collective-permute-start.38 = (bf16[16,2048]{1,0:T(8,128)(2,1)S(1)}, bf16[16,2048]{1,0:T(8,128)(2,1)S(1)}, u32[]{:S(2)}, u32[]{:S(2)}) collective-permute-start(bf16[16,2048]{1,0:T(8,128)(2,1)S(1)} %get-tuple-element.66), channel_id=1, source_target_pairs={{0,10},{1,11},{2,12},{3,13},{4,14},{5,15},{6,8},{7,9},{8,18},{9,19... | collective-permute-start | bytes 196616 | tf_op jit(solution)/shard_map/ppermute | solution.py:300
  115.8 6.3 %copy-start.7 = (s32[1,4,16]{2,1,0:T(4,128)S(1)}, s32[1,4,16]{2,1,0:T(4,128)}, u32[]{:S(2)}) copy-start(s32[1,4,16]{2,1,0:T(4,128)} %chosen.5) | copy-start | bytes 772

commit v2 on v1

v2 whole, which is shorter than its diff:
```python
import functools

import jax
import jax.numpy as jnp
from jax import lax
from jax.experimental import pallas as pl
from jax.experimental.pallas import tpu as pltpu
from jax.sharding import PartitionSpec as P

gelu_coef = 0.7978845608028654
both = ("group", "fsdp")


def gelu_parts(hidden):
    inner_arg = gelu_coef * (hidden + 0.044715 * hidden * hidden * hidden)
    tangent = jnp.tanh(inner_arg)
    activation = 0.5 * hidden * (1.0 + tangent)
    slope = 0.5 * (1.0 + tangent) + 0.5 * hidden * (1.0 - tangent * tangent) * gelu_coef * (
        1.0 + 3.0 * 0.044715 * hidden * hidden
    )
    return (activation, slope)


def params(limit=48 * 2**20):
    return pltpu.CompilerParams(vmem_limit_bytes=limit)


def cost(flops, moved, trans=0):
    return pl.CostEstimate(flops=flops, bytes_accessed=moved, transcendentals=trans)


def smem():
    return pl.BlockSpec(memory_space=pltpu.SMEM)


def column_of(values, rows, dtype):
    at = lax.broadcasted_iota(jnp.int32, (8, 128), 0)
    tiles = []
    for base in range(0, rows, 8):
        tile = jnp.full((8, 128), values[base], dtype)
        for r in range(1, 8):
            tile = jnp.where(at == r, values[base + r], tile)
        tiles.append(tile)
    return jnp.concatenate(tiles, axis=0)


def pick_kernel(groups, slots, chosen, counts, gates, tokens, grads, *rest):
    outs, spot, onehot, scale = rest[:groups], rest[groups], rest[groups + 1], rest[groups + 2]
    length, width = tokens.shape
    rows = groups * slots

    @pl.when(pl.program_id(0) == 0)
    def _():
        me = lax.axis_index("group")
        owner = [lax.rem(me + r, groups) for r in range(groups)]
        where = [chosen[0, owner[r // slots], r % slots] for r in range(rows)]
        column = jnp.concatenate([column_of(where, rows, jnp.int32)] * (length // 128), axis=1)
        onehot[...] = jnp.where(
            column == lax.broadcasted_iota(jnp.int32, (rows, length), 1), 1.0, 0.0
        ).astype(jnp.bfloat16)
        live = []
        for r in range(rows):
            e, c = owner[r // slots], r % slots
            live.append(jnp.where(c < counts[0, e], gates[0, e, c], jnp.float32(0.0)))
        scale[...] = column_of(live, rows, jnp.float32)
        lane = lax.rem(lax.broadcasted_iota(jnp.int32, (8, 2 * rows), 1), rows)
        line = jnp.full((8, 2 * rows), -1, jnp.int32)
        for r in range(rows):
            line = jnp.where(lane == r, where[r], line)
        line = jnp.concatenate([line] * (length // 8), axis=0)
        spot[...] = jnp.where(
            line == lax.broadcasted_iota(jnp.int32, (length, 2 * rows), 0), 1.0, 0.0
        ).astype(jnp.bfloat16)

    x = jnp.dot(onehot[...], tokens[...], preferred_element_type=jnp.float32).astype(jnp.bfloat16)
    g = jnp.dot(onehot[...], grads[...], preferred_element_type=jnp.float32)
    g = (g * jnp.concatenate([scale[...]] * (width // 128), axis=1)).astype(jnp.bfloat16)
    for d in range(groups):
        outs[d][:slots] = x[d * slots : (d + 1) * slots]
        outs[d][slots:] = g[d * slots : (d + 1) * slots]


def pick(tokens, grads, chosen, counts, gates, groups):
    slots = chosen.shape[2]
    length, model = tokens.shape
    tile = min(512, model)
    rows = groups * slots
    return pl.pallas_call(
        functools.partial(pick_kernel, groups, slots),
        grid=(model // tile,),
        in_specs=[smem(), smem(), smem()] + [pl.BlockSpec((length, tile), lambda i: (0, i))] * 2,
        out_specs=[pl.BlockSpec((2 * slots, tile), lambda i: (0, i))] * groups
        + [whole_spec((length, 2 * rows))],
        out_shape=[jax.ShapeDtypeStruct((2 * slots, model), jnp.bfloat16)] * groups
        + [jax.ShapeDtypeStruct((length, 2 * rows), jnp.bfloat16)],
        scratch_shapes=[pltpu.VMEM((rows, length), jnp.bfloat16), pltpu.VMEM((rows, 128), jnp.float32)],
        compiler_params=params(60 * 2**20),
        cost_estimate=cost(4 * rows * length * model, 4 * length * model),
        name="pick",
    )(chosen, counts, gates, tokens, grads)


def whole_spec(shape):
    return pl.BlockSpec(shape, lambda i: (0,) * len(shape))


def block_kernel(slots, n_in, *refs):
    ins = refs[:n_in]
    w_in, w_out, x_t, act_t, hgrad, g_all, mine, theirs, x_all, g_t, total = refs[n_in:]
    step = pl.program_id(0)
    half = mine.shape[0]

    @pl.when(step == 0)
    def _():
        at = 0
        for ref in ins:
            for row in range(0, ref.shape[0], 2 * slots):
                x_all[at : at + slots] = ref[row : row + slots]
                g_all[at : at + slots] = ref[row + slots : row + 2 * slots]
                at += slots
        x_t[...] = x_all[...].T
        g_t[...] = g_all[...].T

    hidden = jnp.dot(x_all[...], w_in[0], preferred_element_type=jnp.float32).T
    activation, gelu_slope = gelu_parts(hidden)
    act_t[...] = activation.astype(jnp.bfloat16)
    back = jnp.dot(w_out[0], g_t[...], preferred_element_type=jnp.float32)
    hg_t = (back * gelu_slope).astype(jnp.bfloat16)
    hgrad[...] = hg_t.T
    part = jnp.dot(w_in[0], hg_t, preferred_element_type=jnp.float32)

    @pl.when(step == 0)
    def _():
        total[...] = part

    @pl.when(step > 0)
    def _():
        total[...] += part

    @pl.when(step == pl.num_programs(0) - 1)
    def _():
        slot_grad = total[...].T
        mine[...] = slot_grad[:half]
        theirs[...] = slot_grad[half:].astype(theirs.dtype)


def block(ins, w_in, w_out, slots):
    model = w_in.shape[1]
    units = w_in.shape[2]
    rows = sum(r.shape[0] for r in ins) // 2
    half = rows // 2
    tile = min(256, units)
    bf = functools.partial(jax.ShapeDtypeStruct, dtype=jnp.bfloat16)
    return pl.pallas_call(
        functools.partial(block_kernel, slots, len(ins)),
        grid=(units // tile,),
        in_specs=[whole_spec(r.shape) for r in ins]
        + [
            pl.BlockSpec((1, model, tile), lambda i: (0, 0, i)),
            pl.BlockSpec((1, tile, model), lambda i: (0, i, 0)),
        ],
        out_specs=[
            whole_spec((model, rows)),
            pl.BlockSpec((tile, rows), lambda i: (i, 0)),
            pl.BlockSpec((rows, tile), lambda i: (0, i)),
            whole_spec((rows, model)),
            whole_spec((half, model)),
            whole_spec((half, model)),
        ],
        out_shape=[
            bf((model, rows)),
            bf((units, rows)),
            bf((rows, units)),
            bf((rows, model)),
            jax.ShapeDtypeStruct((half, model), jnp.float32),
            bf((half, model)),
        ],
        scratch_shapes=[
            pltpu.VMEM((rows, model), jnp.bfloat16),
            pltpu.VMEM((model, rows), jnp.bfloat16),
            pltpu.VMEM((model, rows), jnp.float32),
        ],
        compiler_params=params(),
        cost_estimate=cost(6 * rows * model * units, 4 * model * units, rows * units),
        name="block",
    )(*ins, w_in, w_out)


def outer_kernel(n, *refs):
    left, right, out = refs[:n], refs[n:-1], refs[-1]
    a = jnp.concatenate([r[...] for r in left], axis=1)
    b = jnp.concatenate([r[...] for r in right], axis=0)
    out[0] = jnp.dot(a, b, preferred_element_type=jnp.float32)


def outer(left_t, right, tile, name):
    m, n = left_t[0].shape[0], right[0].shape[1]
    rows = sum(r.shape[0] for r in right)
    tile = min(tile, m)
    return pl.pallas_call(
        functools.partial(outer_kernel, len(right)),
        grid=(m // tile,),
        in_specs=[pl.BlockSpec((tile, r.shape[1]), lambda i: (i, 0)) for r in left_t]
        + [whole_spec(r.shape) for r in right],
        out_specs=pl.BlockSpec((1, tile, n), lambda i: (0, i, 0)),
        out_shape=jax.ShapeDtypeStruct((1, m, n), jnp.float32),
        compiler_params=params(),
        cost_estimate=cost(2 * rows * m * n, 4 * m * n),
        name=name,
    )(*left_t, *right)


def add_kernel(plan, n_in, *refs):
    ins, outs = refs[:n_in], refs[n_in:]
    total = ins[0][...].astype(jnp.float32)
    for r in ins[1:]:
        if r.shape == total.shape:
            total = total + r[...].astype(jnp.float32)
    total = total.astype(jnp.bfloat16)
    at = 0
    for out in outs:
        out[...] = total[at : at + out.shape[0]]
        at += out.shape[0]


def add_up(ins, cuts):
    rows, model = ins[0].shape
    return pl.pallas_call(
        functools.partial(add_kernel, None, len(ins)),
        out_shape=[jax.ShapeDtypeStruct((c, model), jnp.bfloat16) for c in cuts],
        compiler_params=params(),
        cost_estimate=cost(rows * model, 12 * rows * model),
        name="add_up",
    )(*ins)


def place_kernel(spot, *rest):
    parts, out = rest[:-1], rest[-1]
    values = jnp.concatenate([p[...] for p in parts], axis=0)
    out[...] = jnp.dot(spot[...], values, preferred_element_type=jnp.float32).astype(jnp.bfloat16)


def place(parts, spot):
    slots, model = parts[0].shape
    length, rows = spot.shape
    tile = min(512, model)
    return pl.pallas_call(
        place_kernel,
        grid=(model // tile,),
        in_specs=[whole_spec(spot.shape)] + [pl.BlockSpec((slots, tile), lambda i: (0, i))] * len(parts),
        out_specs=pl.BlockSpec((length, tile), lambda i: (0, i)),
        out_shape=jax.ShapeDtypeStruct((length, model), jnp.bfloat16),
        compiler_params=params(),
        cost_estimate=cost(2 * rows * length * model, 2 * length * model),
        name="place",
    )(spot, *parts)


def shards(tokens_in, out_grad, w_in, w_out, chosen, counts, gates):
    groups = lax.axis_size("group")
    fsdp = lax.axis_size("fsdp")
    ring_len = fsdp // 2
    slots = chosen.shape[2]
    rows = groups * slots

    def send(x, group_step, chip_step):
        pairs = [
            (g * fsdp + f, (g + group_step) % groups * fsdp + (f + 2 * chip_step) % fsdp)
            for g in range(groups)
            for f in range(fsdp)
        ]
        return lax.ppermute(x, both, pairs)

    def ring(x):
        return lax.ppermute(x, "fsdp", [(f, (f + 2) % fsdp) for f in range(fsdp)])

    def pair(x):
        return lax.ppermute(x, "fsdp", [(f, f ^ 1) for f in range(fsdp)])

    *picked, spot = pick(tokens_in, out_grad, chosen, counts, gates, groups)
    cut = groups // 2
    ahead = [send(picked[d], d, 1) for d in range(groups)]
    near = [picked[0]] + [send(picked[d], d, 0) for d in range(1, groups)]
    chains = [[jnp.concatenate(near, axis=0)]]
    chains.append([jnp.concatenate(ahead[:cut], axis=0), jnp.concatenate(ahead[cut:], axis=0)])
    while len(chains) < ring_len:
        chains.append([ring(x) for x in chains[-1]])
    paired = [[pair(x) for x in chain] for chain in chains]

    results = [block(chains[0] + chains[1] + paired[0] + paired[1], w_in, w_out, slots)]
    for k in range(2, ring_len):
        results.append(block(chains[k] + paired[k], w_in, w_out, slots))
    x_ts, act_ts, hgrads, gs, mines, theirs = zip(*results)

    parts, running = [], []
    for i, (mine, other) in enumerate(zip(mines, theirs)):
        last = i == len(mines) - 1
        cuts = [slots] * groups if i == 0 else []
        cuts = cuts + ([slots] * groups if last else [rows])
        pieces = add_up([mine, pair(other)] + running, cuts)
        if i == 0:
            parts += [pieces[0]] + [send(pieces[d], -d, 0) for d in range(1, groups)]
            pieces = pieces[groups:]
        if not last:
            running = [ring(pieces[0])]
    parts += [send(pieces[d], -d, 1) for d in range(groups)]

    grad_w_in = outer(x_ts, hgrads, 512, "grad_w_in")
    grad_w_out = outer(act_ts, gs, 256, "grad_w_out")
    return place(parts, spot), grad_w_in, grad_w_out


def solution(mesh):
    placed = (
        P(("group", "fsdp"), None),
        P(("group", "fsdp"), None),
        P("group", None, "fsdp"),
        P("group", "fsdp", None),
        P(("group", "fsdp"), None, None),
        P(("group", "fsdp"), None),
        P(("group", "fsdp"), None, None),
    )
    return jax.shard_map(
        shards,
        mesh=mesh,
        in_specs=placed,
        out_specs=(P(("group", "fsdp"), None), P("group", None, "fsdp"), P("group", "fsdp", None)),
        check_vma=False,
    )
```

time: 127 us -> 103 us (0.81)
  Pallas kernels: 58.2 us -> 43.1 us
  local copies, waits for them, and re-layouts: 6.82 us -> 1.02 us
  starting transfers between devices: 31.7 us -> 27.6 us
  waiting for transfers between devices: 28.3 us -> 30.4 us
    pallas_call x17 -> x10, Pallas kernels: 58.2 us -> 43.1 us  [the longest x3 24.2 us: block(): pl.pallas_call(functools.partial(block_kernel, slots, len(ins)), grid=(un...]
    ppermute x6, waiting for transfers between devices: 9.42 us -> 17.4 us  [ring(): return lax.ppermute(x, 'fsdp', [(f, (f + 2) % fsdp) for f in range(fsdp)])]
    ppermute x21 -> x14, starting transfers between devices: 28.4 us -> 22.4 us  [send(): return lax.ppermute(x, both, pairs)]
    unnamed x32 -> x9, local copies, waits for them, and re-layouts: 6.8 us -> 0.99 us
    ppermute x21 -> x14, waiting for transfers between devices: 17.1 us -> 13 us  [send(): return lax.ppermute(x, both, pairs)]
    ppermute x6, starting transfers between devices: 0.24 us -> 3.81 us  [ring(): return lax.ppermute(x, 'fsdp', [(f, (f + 2) % fsdp) for f in range(fsdp)])]
    ppermute x12 -> x10, waiting for transfers between devices: 1.76 us -> 0.03 us  [pair(): return lax.ppermute(x, 'fsdp', [(f, f ^ 1) for f in range(fsdp)])]
    ppermute x12 -> x10, starting transfers between devices: 3.1 us -> 1.46 us  [pair(): return lax.ppermute(x, 'fsdp', [(f, f ^ 1) for f in range(fsdp)])]
  transfers between devices with their start and end apart: 39 -> 30, of which waited for: 9 -> 9; matrix products, arithmetic and copies ran while one was open for 0% -> 1% of each run, Pallas kernels for 41% -> 33%
where the time goes in v2:
time: 103 us
  Pallas kernels  43.1 us (42%)
  waiting for transfers between devices  30.4 us (30%)
  starting transfers between devices  27.6 us (27%)
    pallas_call x3, Pallas kernels, block(): pl.pallas_call(functools.partial(block_kernel, slots, len(ins)), grid=(un...  24.2 us
    ppermute x14, starting transfers between devices, send(): return lax.ppermute(x, both, pairs)  22.4 us
    ppermute x6, waiting for transfers between devices, ring(): return lax.ppermute(x, 'fsdp', [(f, (f + 2) % fsdp) for f in range(fsdp)])  17.4 us
    ppermute x14, waiting for transfers between devices, send(): return lax.ppermute(x, both, pairs)  13 us
    pallas_call x2, Pallas kernels, outer(): pl.pallas_call(functools.partial(outer_kernel, len(right)), grid=(m // ti...  9.56 us
    pallas_call x1, Pallas kernels, pick(): pl.pallas_call(functools.partial(pick_kernel, groups, slots), grid=(model...  5.79 us
    ppermute x6, starting transfers between devices, ring(): return lax.ppermute(x, 'fsdp', [(f, (f + 2) % fsdp) for f in range(fsdp)])  3.81 us
    pallas_call x1, Pallas kernels, place(): pl.pallas_call(place_kernel, grid=(model // tile,), in_specs=[whole_spec(...  3.29 us
  transfers between devices with their start and end apart: 30, of which 9 were waited for; matrix products, arithmetic and copies ran while one was open for 1% of the time, Pallas kernels for 33%

profile of v2, /device:TPU:0, one launch (start us, length us, event | category | flops | bytes accessed | tf_op | source)
XLA Modules:
  0.0 103.0 jit_solution(2974936301094026404)
XLA Ops:
  0.6 5.8 %pick.1 = (bf16[32,2048]{1,0:T(8,128)(2,1)}, bf16[32,2048]{1,0:T(8,128)(2,1)}, bf16[32,2048]{1,0:T(8,128)(2,1)}, bf16[32,2048]{1,0:T(8,128)(2,1)}, bf16[1024,128]{1,0:T(8,128)(2,1)}) custom-call(s32[1,4,16]{2,1,0:T(4,128)} %chosen.1, s32[1,4]{1,0:T(1,128)} %counts.1, f32[1,4,16]{2,1,0:T(4,128)} %gates.1, bf16[1024,2048]{1,0:T(8,128)(2,1)} %tokens.1, ...), custom_call_target="tpu_custom_call" | custom-call | flops 536870912 | bytes 8388608 | tf_op jit(solution)/shard_map/pick/pallas_call | solution.py:88
  6.4 3.0 %collective-permute-start = (bf16[32,2048]{1,0:T(8,128)(2,1)}, bf16[32,2048]{1,0:T(8,128)(2,1)S(1)}, u32[]{:S(2)}, u32[]{:S(2)}) collective-permute-start(bf16[32,2048]{1,0:T(8,128)(2,1)} %get-tuple-element.37), channel_id=1, source_target_pairs={{0,8},{1,9},{2,10},{3,11},{4,12},{5,13},{6,14},{7,15},{8,16},{9,17... | collective-permute-start | bytes 393224 | tf_op jit(solution)/shard_map/ppermute | solution.py:272
  9.4 2.5 %collective-permute-start.4 = (bf16[32,2048]{1,0:T(8,128)(2,1)}, bf16[32,2048]{1,0:T(8,128)(2,1)S(1)}, u32[]{:S(2)}, u32[]{:S(2)}) collective-permute-start(bf16[32,2048]{1,0:T(8,128)(2,1)} %get-tuple-element.37), channel_id=1, source_target_pairs={{0,10},{1,11},{2,12},{3,13},{4,14},{5,15},{6,8},{7,9},{8,18},{9,19... | collective-permute-start | bytes 393224 | tf_op jit(solution)/shard_map/ppermute | solution.py:272
  11.9 0.5 collective-permute-start.1
  12.4 2.5 %collective-permute-start.5 = (bf16[32,2048]{1,0:T(8,128)(2,1)}, bf16[32,2048]{1,0:T(8,128)(2,1)S(1)}, u32[]{:S(2)}, u32[]{:S(2)}) collective-permute-start(bf16[32,2048]{1,0:T(8,128)(2,1)} %get-tuple-element.38), channel_id=1, source_target_pairs={{0,18},{1,19},{2,20},{3,21},{4,22},{5,23},{6,16},{7,17},{8,26},{9,... | collective-permute-start | bytes 393224 | tf_op jit(solution)/shard_map/ppermute | solution.py:272
  14.9 1.6 %collective-permute-start.3 = (bf16[32,2048]{1,0:T(8,128)(2,1)}, bf16[32,2048]{1,0:T(8,128)(2,1)S(1)}, u32[]{:S(2)}, u32[]{:S(2)}) collective-permute-start(bf16[32,2048]{1,0:T(8,128)(2,1)} %get-tuple-element.36), channel_id=1, source_target_pairs={{0,2},{1,3},{2,4},{3,5},{4,6},{5,7},{6,0},{7,1},{8,10},{9,11},{10,... | collective-permute-start | bytes 393224 | tf_op jit(solution)/shard_map/ppermute | solution.py:272
  16.5 0.9 constant_dynamic-update-slice_fusion.3
  17.5 0.0 collective-permute-done
  17.5 1.5 %collective-permute-start.2 = (bf16[32,2048]{1,0:T(8,128)(2,1)}, bf16[32,2048]{1,0:T(8,128)(2,1)S(1)}, u32[]{:S(2)}, u32[]{:S(2)}) collective-permute-start(bf16[32,2048]{1,0:T(8,128)(2,1)} %get-tuple-element.39), channel_id=1, source_target_pairs={{0,24},{1,25},{2,26},{3,27},{4,28},{5,29},{6,30},{7,31},{8,0},{9,1... | collective-permute-start | bytes 393224 | tf_op jit(solution)/shard_map/ppermute | solution.py:272
  19.0 3.5 %collective-permute-done.1 = bf16[32,2048]{1,0:T(8,128)(2,1)S(1)} collective-permute-done((bf16[32,2048]{1,0:T(8,128)(2,1)}, bf16[32,2048]{1,0:T(8,128)(2,1)S(1)}, u32[]{:S(2)}, u32[]{:S(2)}) %collective-permute-start.1) | collective-permute-done | bytes 131104 | tf_op jit(solution)/shard_map/ppermute | solution.py:272
  22.5 0.4 collective-permute-start.6
  22.8 0.0 collective-permute-done.2
  22.9 0.1 collective-permute-start.7
  22.9 0.4 collective-permute-done.3
  23.4 0.0 collective-permute-done.4
  23.4 0.1 collective-permute-start.8
  23.6 0.0 collective-permute-done.5
  23.6 6.8 %collective-permute-done.6 = bf16[32,2048]{1,0:T(8,128)(2,1)S(1)} collective-permute-done((bf16[32,2048]{1,0:T(8,128)(2,1)}, bf16[32,2048]{1,0:T(8,128)(2,1)S(1)}, u32[]{:S(2)}, u32[]{:S(2)}) %collective-permute-start.6) | collective-permute-done | bytes 131104 | tf_op jit(solution)/shard_map/ppermute | solution.py:272
  30.4 0.1 collective-permute-start.9
  30.4 0.5 collective-permute-start.14
  30.9 1.6 %collective-permute-start.16 = (bf16[64,2048]{1,0:T(8,128)(2,1)S(1)}, bf16[64,2048]{1,0:T(8,128)(2,1)S(1)}, u32[]{:S(2)}, u32[]{:S(2)}) collective-permute-start(bf16[64,2048]{1,0:T(8,128)(2,1)S(1)} %constant_dynamic-update-slice_fusion.6.refs_2_), channel_id=1, source_target_pairs={{0,2},{1,3},{2,4},{3,5},{4,6},{5,7},{6,0},{7,1},{8,10},{9,11},{10,... | collective-permute-start | bytes 786440 | tf_op jit(solution)/shard_map/ppermute | solution.py:275
  32.5 0.0 collective-permute-done.8.refs_4_
  32.5 0.0 collective-permute-done.9.refs_5_
  32.5 0.0 collective-permute-done.7.refs_3_
  32.5 9.8 %block.3 = (bf16[2048,256]{1,0:T(8,128)(2,1)S(1)}, bf16[1024,256]{1,0:T(8,128)(2,1)S(1)}, bf16[256,1024]{1,0:T(8,128)(2,1)S(1)}, bf16[256,2048]{1,0:T(8,128)(2,1...) custom-call(bf16[128,2048]{1,0:T(8,128)(2,1)S(1)} %constant_dynamic-update-slice_fusion.refs_0_, ...), custom_call_target="tpu_custom_call" | custom-call | flops 3221225472 | bytes 8388608 | tf_op jit(solution)/shard_map/block/pallas_call | solution.py:154
  42.3 0.0 collective-permute-start.10
  42.3 0.0 collective-permute-done.14.refs_0_
  42.3 1.6 %collective-permute-start.15 = (bf16[64,2048]{1,0:T(8,128)(2,1)S(1)}, bf16[64,2048]{1,0:T(8,128)(2,1)S(1)}, u32[]{:S(2)}, u32[]{:S(2)}) collective-permute-start(bf16[64,2048]{1,0:T(8,128)(2,1)S(1)} %collective-permute-done.14.refs_0_), channel_id=1, source_target_pairs={{0,2},{1,3},{2,4},{3,5},{4,6},{5,7},{6,0},{7,1},{8,10},{9,11},{10,... | collective-permute-start | bytes 786440 | tf_op jit(solution)/shard_map/ppermute | solution.py:275
  43.9 2.7 %collective-permute-done.16.refs_1_ = bf16[64,2048]{1,0:T(8,128)(2,1)S(1)} collective-permute-done((bf16[64,2048]{1,0:T(8,128)(2,1)S(1)}, bf16[64,2048]{1,0:T(8,128)(2,1)S(1)}, u32[]{:S(2)}, u32[]{:S(2)}) %collective-permute-start.16) | collective-permute-done | bytes 262176 | tf_op jit(solution)/shard_map/ppermute | solution.py:275
  46.6 0.5 collective-permute-start.22
  47.1 6.1 %collective-permute-done.15.refs_0_ = bf16[64,2048]{1,0:T(8,128)(2,1)S(1)} collective-permute-done((bf16[64,2048]{1,0:T(8,128)(2,1)S(1)}, bf16[64,2048]{1,0:T(8,128)(2,1)S(1)}, u32[]{:S(2)}, u32[]{:S(2)}) %collective-permute-start.15) | collective-permute-done | bytes 262176 | tf_op jit(solution)/shard_map/ppermute | solution.py:275
  53.2 0.0 collective-permute-start.18
  53.2 5.2 %collective-permute-done.17.refs_1_ = bf16[64,2048]{1,0:T(8,128)(2,1)S(1)} collective-permute-done((bf16[64,2048]{1,0:T(8,128)(2,1)S(1)}, bf16[64,2048]{1,0:T(8,128)(2,1)S(1)}, u32[]{:S(2)}, u32[]{:S(2)}) %collective-permute-start.17) | collective-permute-done | bytes 262176 | tf_op jit(solution)/shard_map/ppermute | solution.py:275
  58.4 0.0 collective-permute-done.21.refs_2_
  58.4 0.0 collective-permute-done.22.refs_3_
  58.4 7.2 %block.5 = (bf16[2048,128]{1,0:T(8,128)(2,1)S(1)}, bf16[1024,128]{1,0:T(8,128)(2,1)S(1)}, bf16[128,1024]{1,0:T(8,128)(2,1)S(1)}, bf16[128,2048]{1,0:T(8,128)(2,1...) custom-call(bf16[64,2048]{1,0:T(8,128)(2,1)S(1)} %collective-permute-done.14.refs_0_, ...), custom_call_target="tpu_custom_call" | custom-call | flops 1610612736 | bytes 8388608 | tf_op jit(solution)/shard_map/block/pallas_call | solution.py:154
  65.7 0.6 collective-permute-start.23
  66.2 0.0 collective-permute-done.10.refs_1_
  66.2 0.1 add_up.3
  66.3 0.1 collective-permute-start.24
  66.4 7.2 %block.4 = (bf16[2048,128]{1,0:T(8,128)(2,1)S(1)}, bf16[1024,128]{1,0:T(8,128)(2,1)S(1)}, bf16[128,1024]{1,0:T(8,128)(2,1)S(1)}, bf16[128,2048]{1,0:T(8,128)(2,1...) custom-call(bf16[64,2048]{1,0:T(8,128)(2,1)S(1)} %collective-permute-done.15.refs_0_, ...), custom_call_target="tpu_custom_call" | custom-call | flops 1610612736 | bytes 8388608 | tf_op jit(solution)/shard_map/block/pallas_call | solution.py:154
  73.7 0.1 collective-permute-start.20
  73.8 0.0 collective-permute-done.23.refs_1_
  73.8 2.6 %collective-permute-done.24.refs_2_ = bf16[64,2048]{1,0:T(8,128)(2,1)S(1)} collective-permute-done((bf16[64,2048]{1,0:T(8,128)(2,1)S(1)}, bf16[64,2048]{1,0:T(8,128)(2,1)S(1)}, u32[]{:S(2)}, u32[]{:S(2)}) %collective-permute-start.24) | collective-permute-done | bytes 262176 | tf_op jit(solution)/shard_map/ppermute | solution.py:275
  76.4 0.1 add_up.4
  76.5 0.1 collective-permute-start.25
  76.6 1.7 %collective-permute-start.11 = (bf16[16,2048]{1,0:T(8,128)(2,1)S(1)}, bf16[16,2048]{1,0:T(8,128)(2,1)S(1)}, u32[]{:S(2)}, u32[]{:S(2)}) collective-permute-start(bf16[16,2048]{1,0:T(8,128)(2,1)S(1)} %get-tuple-element.43), channel_id=1, source_target_pairs={{0,24},{1,25},{2,26},{3,27},{4,28},{5,29},{6,30},{7,31},{8,0},{9,1... | collective-permute-start | bytes 196616 | tf_op jit(solution)/shard_map/ppermute | solution.py:272
  78.2 1.5 %collective-permute-start.12 = (bf16[16,2048]{1,0:T(8,128)(2,1)S(1)}, bf16[16,2048]{1,0:T(8,128)(2,1)S(1)}, u32[]{:S(2)}, u32[]{:S(2)}) collective-permute-start(bf16[16,2048]{1,0:T(8,128)(2,1)S(1)} %get-tuple-element.44), channel_id=1, source_target_pairs={{0,16},{1,17},{2,18},{3,19},{4,20},{5,21},{6,22},{7,23},{8,24},{9,... | collective-permute-start | bytes 196616 | tf_op jit(solution)/shard_map/ppermute | solution.py:272
  79.8 4.8 %grad_w_out.1 = f32[1,1024,2048]{2,1,0:T(8,128)} custom-call(bf16[1024,256]{1,0:T(8,128)(2,1)S(1)} %get-tuple-element.61.refs_0_, bf16[1024,128]{1,0:T(8,128)(2,1)S(1)} %get-tuple-element.62.refs_1_, bf16[1024,128]{1,0:T(8,128)(2,1)S(1)} %get-tuple-element.63.refs_2_, bf16[256,2048]{1,0:T(8,128)(2,1)S(1)} %get-tuple-element.64.refs_3_, ...), custom_call_target="tpu_custom_call" | custom-call | flops 2147483648 | bytes 8388608 | tf_op jit(solution)/shard_map/grad_w_out/pallas_call | solution.py:200
  84.5 0.4 collective-permute-start.13
  84.9 0.0 collective-permute-done.20.refs_1_
  84.9 0.8 collective-permute-done.25.refs_2_
  85.8 0.1 add_up.5
  85.8 0.1 collective-permute-start.26
  85.9 3.3 %collective-permute-start.27 = (bf16[16,2048]{1,0:T(8,128)(2,1)S(1)}, bf16[16,2048]{1,0:T(8,128)(2,1)S(1)}, u32[]{:S(2)}, u32[]{:S(2)}) collective-permute-start(bf16[16,2048]{1,0:T(8,128)(2,1)S(1)} %get-tuple-element.52), channel_id=1, source_target_pairs={{0,26},{1,27},{2,28},{3,29},{4,30},{5,31},{6,24},{7,25},{8,2},{9,3... | collective-permute-start | bytes 196616 | tf_op jit(solution)/shard_map/ppermute | solution.py:272
  89.2 0.0 collective-permute-done.11.rest_1_
  89.2 2.6 %collective-permute-start.28 = (bf16[16,2048]{1,0:T(8,128)(2,1)S(1)}, bf16[16,2048]{1,0:T(8,128)(2,1)S(1)}, u32[]{:S(2)}, u32[]{:S(2)}) collective-permute-start(bf16[16,2048]{1,0:T(8,128)(2,1)S(1)} %get-tuple-element.53), channel_id=1, source_target_pairs={{0,18},{1,19},{2,20},{3,21},{4,22},{5,23},{6,16},{7,17},{8,26},{9,... | collective-permute-start | bytes 196616 | tf_op jit(solution)/shard_map/ppermute | solution.py:272
  91.9 0.8 collective-permute-start.29
  92.7 4.8 %grad_w_in.1 = f32[1,2048,1024]{2,1,0:T(8,128)} custom-call(bf16[2048,256]{1,0:T(8,128)(2,1)S(1)} %get-tuple-element.55.refs_0_, bf16[2048,128]{1,0:T(8,128)(2,1)S(1)} %get-tuple-element.56.refs_1_, bf16[2048,128]{1,0:T(8,128)(2,1)S(1)} %get-tuple-element.57.refs_2_, bf16[256,1024]{1,0:T(8,128)(2,1)S(1)} %get-tuple-element.58.refs_3_, ...), custom_call_target="tpu_custom_call" | custom-call | flops 2147483648 | bytes 8388608 | tf_op jit(solution)/shard_map/grad_w_in/pallas_call | solution.py:200
  97.5 0.0 collective-permute-done.13.rest_3_
  97.5 0.0 collective-permute-done.26.rest_4_
  97.5 0.0 collective-permute-done.27.rest_5_
  97.5 2.2 %collective-permute-done.29.rest_7_ = bf16[16,2048]{1,0:T(8,128)(2,1)S(1)} collective-permute-done((bf16[16,2048]{1,0:T(8,128)(2,1)S(1)}, bf16[16,2048]{1,0:T(8,128)(2,1)S(1)}, u32[]{:S(2)}, u32[]{:S(2)}) %collective-permute-start.29) | collective-permute-done | bytes 65568 | tf_op jit(solution)/shard_map/ppermute | solution.py:272
  99.7 3.3 %place.1 = bf16[1024,2048]{1,0:T(8,128)(2,1)} custom-call(bf16[1024,128]{1,0:T(8,128)(2,1)S(1)} %copy-done.1, bf16[16,2048]{1,0:T(8,128)(2,1)S(1)} %get-tuple-element.42.rest_0_, bf16[16,2048]{1,0:T(8,128)(2,1)S(1)} %collective-permute-done.11.rest_1_, bf16[16,2048]{1,0:T(8,128)(2,1)S(1)} %collective-permute-done.12.rest_2_, ...), custom_call_target="tpu_custom_call" | custom-call | flops 536870912 | bytes 4194304 | tf_op jit(solution)/shard_map/place/pallas_call | solution.py:247
  (18 shorter events, 0.1 us)
Async XLA Ops:
  6.4 11.0 %collective-permute-start = (bf16[32,2048]{1,0:T(8,128)(2,1)}, bf16[32,2048]{1,0:T(8,128)(2,1)S(1)}, u32[]{:S(2)}, u32[]{:S(2)}) collective-permute-start(bf16[32,2048]{1,0:T(8,128)(2,1)} %get-tuple-element.37), channel_id=1, source_target_pairs={{0,8},{1,9},{2,10},{3,11},{4,12},{5,13},{6,14},{7,15},{8,16},{9,17... | collective-permute-start | bytes 393224 | tf_op jit(solution)/shard_map/ppermute | solution.py:272
  9.4 14.0 %collective-permute-start.4 = (bf16[32,2048]{1,0:T(8,128)(2,1)}, bf16[32,2048]{1,0:T(8,128)(2,1)S(1)}, u32[]{:S(2)}, u32[]{:S(2)}) collective-permute-start(bf16[32,2048]{1,0:T(8,128)(2,1)} %get-tuple-element.37), channel_id=1, source_target_pairs={{0,10},{1,11},{2,12},{3,13},{4,14},{5,15},{6,8},{7,9},{8,18},{9,19... | collective-permute-start | bytes 393224 | tf_op jit(solution)/shard_map/ppermute | solution.py:272
  11.9 10.6 %collective-permute-start.1 = (bf16[32,2048]{1,0:T(8,128)(2,1)}, bf16[32,2048]{1,0:T(8,128)(2,1)S(1)}, u32[]{:S(2)}, u32[]{:S(2)}) collective-permute-start(bf16[32,2048]{1,0:T(8,128)(2,1)} %get-tuple-element.38), channel_id=1, source_target_pairs={{0,16},{1,17},{2,18},{3,19},{4,20},{5,21},{6,22},{7,23},{8,24},{9,... | collective-permute-start | bytes 393224 | tf_op jit(solution)/shard_map/ppermute | solution.py:272
  12.4 11.2 %collective-permute-start.5 = (bf16[32,2048]{1,0:T(8,128)(2,1)}, bf16[32,2048]{1,0:T(8,128)(2,1)S(1)}, u32[]{:S(2)}, u32[]{:S(2)}) collective-permute-start(bf16[32,2048]{1,0:T(8,128)(2,1)} %get-tuple-element.38), channel_id=1, source_target_pairs={{0,18},{1,19},{2,20},{3,21},{4,22},{5,23},{6,16},{7,17},{8,26},{9,... | collective-permute-start | bytes 393224 | tf_op jit(solution)/shard_map/ppermute | solution.py:272
  14.9 8.4 %collective-permute-start.3 = (bf16[32,2048]{1,0:T(8,128)(2,1)}, bf16[32,2048]{1,0:T(8,128)(2,1)S(1)}, u32[]{:S(2)}, u32[]{:S(2)}) collective-permute-start(bf16[32,2048]{1,0:T(8,128)(2,1)} %get-tuple-element.36), channel_id=1, source_target_pairs={{0,2},{1,3},{2,4},{3,5},{4,6},{5,7},{6,0},{7,1},{8,10},{9,11},{10,... | collective-permute-start | bytes 393224 | tf_op jit(solution)/shard_map/ppermute | solution.py:272
  17.5 5.4 %collective-permute-start.2 = (bf16[32,2048]{1,0:T(8,128)(2,1)}, bf16[32,2048]{1,0:T(8,128)(2,1)S(1)}, u32[]{:S(2)}, u32[]{:S(2)}) collective-permute-start(bf16[32,2048]{1,0:T(8,128)(2,1)} %get-tuple-element.39), channel_id=1, source_target_pairs={{0,24},{1,25},{2,26},{3,27},{4,28},{5,29},{6,30},{7,31},{8,0},{9,1... | collective-permute-start | bytes 393224 | tf_op jit(solution)/shard_map/ppermute | solution.py:272
  22.5 7.9 %collective-permute-start.6 = (bf16[32,2048]{1,0:T(8,128)(2,1)}, bf16[32,2048]{1,0:T(8,128)(2,1)S(1)}, u32[]{:S(2)}, u32[]{:S(2)}) collective-permute-start(bf16[32,2048]{1,0:T(8,128)(2,1)} %get-tuple-element.39), channel_id=1, source_target_pairs={{0,26},{1,27},{2,28},{3,29},{4,30},{5,31},{6,24},{7,25},{8,2},{9,3... | collective-permute-start | bytes 393224 | tf_op jit(solution)/shard_map/ppermute | solution.py:272
  22.9 9.6 %collective-permute-start.7 = (bf16[128,2048]{1,0:T(8,128)(2,1)S(1)}, bf16[128,2048]{1,0:T(8,128)(2,1)S(1)}, u32[]{:S(2)}, u32[]{:S(2)}) collective-permute-start(bf16[128,2048]{1,0:T(8,128)(2,1)S(1)} %constant_dynamic-update-slice_fusion.refs_0_), channel_id=1, source_target_pairs={{0,1},{1,0},{2,3},{3,2},{4,5},{5,4},{6,7},{7,6},{8,9},{9,8},{10,11... | collective-permute-start | bytes 1572872 | tf_op jit(solution)/shard_map/ppermute | solution.py:278
  23.4 9.1 %collective-permute-start.8 = (bf16[64,2048]{1,0:T(8,128)(2,1)S(1)}, bf16[64,2048]{1,0:T(8,128)(2,1)S(1)}, u32[]{:S(2)}, u32[]{:S(2)}) collective-permute-start(bf16[64,2048]{1,0:T(8,128)(2,1)S(1)} %constant_dynamic-update-slice_fusion.4.refs_1_), channel_id=1, source_target_pairs={{0,1},{1,0},{2,3},{3,2},{4,5},{5,4},{6,7},{7,6},{8,9},{9,8},{10,11... | collective-permute-start | bytes 786440 | tf_op jit(solution)/shard_map/ppermute | solution.py:278
  30.4 2.1 %collective-permute-start.9 = (bf16[64,2048]{1,0:T(8,128)(2,1)S(1)}, bf16[64,2048]{1,0:T(8,128)(2,1)S(1)}, u32[]{:S(2)}, u32[]{:S(2)}) collective-permute-start(bf16[64,2048]{1,0:T(8,128)(2,1)S(1)} %constant_dynamic-update-slice_fusion.6.refs_2_), channel_id=1, source_target_pairs={{0,1},{1,0},{2,3},{3,2},{4,5},{5,4},{6,7},{7,6},{8,9},{9,8},{10,11... | collective-permute-start | bytes 786440 | tf_op jit(solution)/shard_map/ppermute | solution.py:278
  30.4 11.8 %collective-permute-start.14 = (bf16[64,2048]{1,0:T(8,128)(2,1)S(1)}, bf16[64,2048]{1,0:T(8,128)(2,1)S(1)}, u32[]{:S(2)}, u32[]{:S(2)}) collective-permute-start(bf16[64,2048]{1,0:T(8,128)(2,1)S(1)} %constant_dynamic-update-slice_fusion.4.refs_1_), channel_id=1, source_target_pairs={{0,2},{1,3},{2,4},{3,5},{4,6},{5,7},{6,0},{7,1},{8,10},{9,11},{10,... | collective-permute-start | bytes 786440 | tf_op jit(solution)/shard_map/ppermute | solution.py:275
  30.9 15.7 %collective-permute-start.16 = (bf16[64,2048]{1,0:T(8,128)(2,1)S(1)}, bf16[64,2048]{1,0:T(8,128)(2,1)S(1)}, u32[]{:S(2)}, u32[]{:S(2)}) collective-permute-start(bf16[64,2048]{1,0:T(8,128)(2,1)S(1)} %constant_dynamic-update-slice_fusion.6.refs_2_), channel_id=1, source_target_pairs={{0,2},{1,3},{2,4},{3,5},{4,6},{5,7},{6,0},{7,1},{8,10},{9,11},{10,... | collective-permute-start | bytes 786440 | tf_op jit(solution)/shard_map/ppermute | solution.py:275
  42.3 24.0 %copy-start = (f32[128,2048]{1,0:T(8,128)S(1)}, f32[128,2048]{1,0:T(8,128)}, u32[]{:S(2)}) copy-start(f32[128,2048]{1,0:T(8,128)} %get-tuple-element.40.refs_0_) | copy-start | bytes 3145732
  42.3 24.0 %collective-permute-start.10 = (bf16[128,2048]{1,0:T(8,128)(2,1)S(1)}, bf16[128,2048]{1,0:T(8,128)(2,1)S(1)}, u32[]{:S(2)}, u32[]{:S(2)}) collective-permute-start(bf16[128,2048]{1,0:T(8,128)(2,1)S(1)} %get-tuple-element.41), channel_id=1, source_target_pairs={{0,1},{1,0},{2,3},{3,2},{4,5},{5,4},{6,7},{7,6},{8,9},{9,8},{10,11... | collective-permute-start | bytes 1572872 | tf_op jit(solution)/shard_map/ppermute | solution.py:278
  42.3 11.0 %collective-permute-start.15 = (bf16[64,2048]{1,0:T(8,128)(2,1)S(1)}, bf16[64,2048]{1,0:T(8,128)(2,1)S(1)}, u32[]{:S(2)}, u32[]{:S(2)}) collective-permute-start(bf16[64,2048]{1,0:T(8,128)(2,1)S(1)} %collective-permute-done.14.refs_0_), channel_id=1, source_target_pairs={{0,2},{1,3},{2,4},{3,5},{4,6},{5,7},{6,0},{7,1},{8,10},{9,11},{10,... | collective-permute-start | bytes 786440 | tf_op jit(solution)/shard_map/ppermute | solution.py:275
  46.6 11.8 %collective-permute-start.17 = (bf16[64,2048]{1,0:T(8,128)(2,1)S(1)}, bf16[64,2048]{1,0:T(8,128)(2,1)S(1)}, u32[]{:S(2)}, u32[]{:S(2)}) collective-permute-start(bf16[64,2048]{1,0:T(8,128)(2,1)S(1)} %collective-permute-done.16.refs_1_), channel_id=1, source_target_pairs={{0,2},{1,3},{2,4},{3,5},{4,6},{5,7},{6,0},{7,1},{8,10},{9,11},{10,... | collective-permute-start | bytes 786440 | tf_op jit(solution)/shard_map/ppermute | solution.py:275
  46.6 11.8 %collective-permute-start.21 = (bf16[64,2048]{1,0:T(8,128)(2,1)S(1)}, bf16[64,2048]{1,0:T(8,128)(2,1)S(1)}, u32[]{:S(2)}, u32[]{:S(2)}) collective-permute-start(bf16[64,2048]{1,0:T(8,128)(2,1)S(1)} %collective-permute-done.14.refs_0_), channel_id=1, source_target_pairs={{0,1},{1,0},{2,3},{3,2},{4,5},{5,4},{6,7},{7,6},{8,9},{9,8},{10,11... | collective-permute-start | bytes 786440 | tf_op jit(solution)/shard_map/ppermute | solution.py:278
  46.6 11.8 %collective-permute-start.22 = (bf16[64,2048]{1,0:T(8,128)(2,1)S(1)}, bf16[64,2048]{1,0:T(8,128)(2,1)S(1)}, u32[]{:S(2)}, u32[]{:S(2)}) collective-permute-start(bf16[64,2048]{1,0:T(8,128)(2,1)S(1)} %collective-permute-done.16.refs_1_), channel_id=1, source_target_pairs={{0,1},{1,0},{2,3},{3,2},{4,5},{5,4},{6,7},{7,6},{8,9},{9,8},{10,11... | collective-permute-start | bytes 786440 | tf_op jit(solution)/shard_map/ppermute | solution.py:278
  53.2 13.2 %collective-permute-start.18 = (bf16[64,2048]{1,0:T(8,128)(2,1)S(1)}, bf16[64,2048]{1,0:T(8,128)(2,1)S(1)}, u32[]{:S(2)}, u32[]{:S(2)}) collective-permute-start(bf16[64,2048]{1,0:T(8,128)(2,1)S(1)} %collective-permute-done.15.refs_0_), channel_id=1, source_target_pairs={{0,1},{1,0},{2,3},{3,2},{4,5},{5,4},{6,7},{7,6},{8,9},{9,8},{10,11... | collective-permute-start | bytes 786440 | tf_op jit(solution)/shard_map/ppermute | solution.py:278
  58.4 8.0 %collective-permute-start.19 = (bf16[64,2048]{1,0:T(8,128)(2,1)S(1)}, bf16[64,2048]{1,0:T(8,128)(2,1)S(1)}, u32[]{:S(2)}, u32[]{:S(2)}) collective-permute-start(bf16[64,2048]{1,0:T(8,128)(2,1)S(1)} %collective-permute-done.17.refs_1_), channel_id=1, source_target_pairs={{0,1},{1,0},{2,3},{3,2},{4,5},{5,4},{6,7},{7,6},{8,9},{9,8},{10,11... | collective-permute-start | bytes 786440 | tf_op jit(solution)/shard_map/ppermute | solution.py:278
  65.7 8.1 %collective-permute-start.23 = (bf16[64,2048]{1,0:T(8,128)(2,1)S(1)}, bf16[64,2048]{1,0:T(8,128)(2,1)S(1)}, u32[]{:S(2)}, u32[]{:S(2)}) collective-permute-start(bf16[64,2048]{1,0:T(8,128)(2,1)S(1)} %get-tuple-element.49), channel_id=1, source_target_pairs={{0,1},{1,0},{2,3},{3,2},{4,5},{5,4},{6,7},{7,6},{8,9},{9,8},{10,11... | collective-permute-start | bytes 786440 | tf_op jit(solution)/shard_map/ppermute | solution.py:278
  66.3 10.1 %collective-permute-start.24 = (bf16[64,2048]{1,0:T(8,128)(2,1)S(1)}, bf16[64,2048]{1,0:T(8,128)(2,1)S(1)}, u32[]{:S(2)}, u32[]{:S(2)}) collective-permute-start(bf16[64,2048]{1,0:T(8,128)(2,1)S(1)} %get-tuple-element.50), channel_id=1, source_target_pairs={{0,2},{1,3},{2,4},{3,5},{4,6},{5,7},{6,0},{7,1},{8,10},{9,11},{10,... | collective-permute-start | bytes 786440 | tf_op jit(solution)/shard_map/ppermute | solution.py:275
  73.7 11.3 %collective-permute-start.20 = (bf16[64,2048]{1,0:T(8,128)(2,1)S(1)}, bf16[64,2048]{1,0:T(8,128)(2,1)S(1)}, u32[]{:S(2)}, u32[]{:S(2)}) collective-permute-start(bf16[64,2048]{1,0:T(8,128)(2,1)S(1)} %get-tuple-element.47), channel_id=1, source_target_pairs={{0,1},{1,0},{2,3},{3,2},{4,5},{5,4},{6,7},{7,6},{8,9},{9,8},{10,11... | collective-permute-start | bytes 786440 | tf_op jit(solution)/shard_map/ppermute | solution.py:278
  76.5 9.2 %collective-permute-start.25 = (bf16[64,2048]{1,0:T(8,128)(2,1)S(1)}, bf16[64,2048]{1,0:T(8,128)(2,1)S(1)}, u32[]{:S(2)}, u32[]{:S(2)}) collective-permute-start(bf16[64,2048]{1,0:T(8,128)(2,1)S(1)} %add_up.4), channel_id=1, source_target_pairs={{0,2},{1,3},{2,4},{3,5},{4,6},{5,7},{6,0},{7,1},{8,10},{9,11},{10,... | collective-permute-start | bytes 786440 | tf_op jit(solution)/shard_map/ppermute | solution.py:275
  76.6 12.7 %collective-permute-start.11 = (bf16[16,2048]{1,0:T(8,128)(2,1)S(1)}, bf16[16,2048]{1,0:T(8,128)(2,1)S(1)}, u32[]{:S(2)}, u32[]{:S(2)}) collective-permute-start(bf16[16,2048]{1,0:T(8,128)(2,1)S(1)} %get-tuple-element.43), channel_id=1, source_target_pairs={{0,24},{1,25},{2,26},{3,27},{4,28},{5,29},{6,30},{7,31},{8,0},{9,1... | collective-permute-start | bytes 196616 | tf_op jit(solution)/shard_map/ppermute | solution.py:272
  78.2 13.6 %collective-permute-start.12 = (bf16[16,2048]{1,0:T(8,128)(2,1)S(1)}, bf16[16,2048]{1,0:T(8,128)(2,1)S(1)}, u32[]{:S(2)}, u32[]{:S(2)}) collective-permute-start(bf16[16,2048]{1,0:T(8,128)(2,1)S(1)} %get-tuple-element.44), channel_id=1, source_target_pairs={{0,16},{1,17},{2,18},{3,19},{4,20},{5,21},{6,22},{7,23},{8,24},{9,... | collective-permute-start | bytes 196616 | tf_op jit(solution)/shard_map/ppermute | solution.py:272
  84.5 13.0 %collective-permute-start.13 = (bf16[16,2048]{1,0:T(8,128)(2,1)S(1)}, bf16[16,2048]{1,0:T(8,128)(2,1)S(1)}, u32[]{:S(2)}, u32[]{:S(2)}) collective-permute-start(bf16[16,2048]{1,0:T(8,128)(2,1)S(1)} %get-tuple-element.45), channel_id=1, source_target_pairs={{0,8},{1,9},{2,10},{3,11},{4,12},{5,13},{6,14},{7,15},{8,16},{9,17... | collective-permute-start | bytes 196616 | tf_op jit(solution)/shard_map/ppermute | solution.py:272
  85.8 11.7 %collective-permute-start.26 = (bf16[16,2048]{1,0:T(8,128)(2,1)S(1)}, bf16[16,2048]{1,0:T(8,128)(2,1)S(1)}, u32[]{:S(2)}, u32[]{:S(2)}) collective-permute-start(bf16[16,2048]{1,0:T(8,128)(2,1)S(1)} %get-tuple-element.51), channel_id=1, source_target_pairs={{0,2},{1,3},{2,4},{3,5},{4,6},{5,7},{6,0},{7,1},{8,10},{9,11},{10,... | collective-permute-start | bytes 196616 | tf_op jit(solution)/shard_map/ppermute | solution.py:272
  85.9 11.6 %collective-permute-start.27 = (bf16[16,2048]{1,0:T(8,128)(2,1)S(1)}, bf16[16,2048]{1,0:T(8,128)(2,1)S(1)}, u32[]{:S(2)}, u32[]{:S(2)}) collective-permute-start(bf16[16,2048]{1,0:T(8,128)(2,1)S(1)} %get-tuple-element.52), channel_id=1, source_target_pairs={{0,26},{1,27},{2,28},{3,29},{4,30},{5,31},{6,24},{7,25},{8,2},{9,3... | collective-permute-start | bytes 196616 | tf_op jit(solution)/shard_map/ppermute | solution.py:272
  89.2 8.3 %collective-permute-start.28 = (bf16[16,2048]{1,0:T(8,128)(2,1)S(1)}, bf16[16,2048]{1,0:T(8,128)(2,1)S(1)}, u32[]{:S(2)}, u32[]{:S(2)}) collective-permute-start(bf16[16,2048]{1,0:T(8,128)(2,1)S(1)} %get-tuple-element.53), channel_id=1, source_target_pairs={{0,18},{1,19},{2,20},{3,21},{4,22},{5,23},{6,16},{7,17},{8,26},{9,... | collective-permute-start | bytes 196616 | tf_op jit(solution)/shard_map/ppermute | solution.py:272
  91.9 7.9 %collective-permute-start.29 = (bf16[16,2048]{1,0:T(8,128)(2,1)S(1)}, bf16[16,2048]{1,0:T(8,128)(2,1)S(1)}, u32[]{:S(2)}, u32[]{:S(2)}) collective-permute-start(bf16[16,2048]{1,0:T(8,128)(2,1)S(1)} %get-tuple-element.54), channel_id=1, source_target_pairs={{0,10},{1,11},{2,12},{3,13},{4,14},{5,15},{6,8},{7,9},{8,18},{9,19... | collective-permute-start | bytes 196616 | tf_op jit(solution)/shard_map/ppermute | solution.py:272
  92.7 7.0 %copy-start.1 = (bf16[1024,128]{1,0:T(8,128)(2,1)S(1)}, bf16[1024,128]{1,0:T(8,128)(2,1)}, u32[]{:S(2)}) copy-start(bf16[1024,128]{1,0:T(8,128)(2,1)} %get-tuple-element.35.spot) | copy-start | bytes 786436

commit v3 on v0

v3 whole, which is shorter than its diff:
```python
import functools

import jax
import jax.numpy as jnp
from jax import lax
from jax.experimental import pallas as pl
from jax.experimental.pallas import tpu as pltpu
from jax.sharding import PartitionSpec as P

gelu_coef = 0.7978845608028654
both = ("group", "fsdp")


def gelu_parts(hidden):
    inner_arg = gelu_coef * (hidden + 0.044715 * hidden * hidden * hidden)
    tangent = jnp.tanh(inner_arg)
    activation = 0.5 * hidden * (1.0 + tangent)
    slope = 0.5 * (1.0 + tangent) + 0.5 * hidden * (1.0 - tangent * tangent) * gelu_coef * (
        1.0 + 3.0 * 0.044715 * hidden * hidden
    )
    return (activation, slope)


def params(limit=48 * 2**20):
    return pltpu.CompilerParams(vmem_limit_bytes=limit)


def cost(flops, moved, trans=0):
    return pl.CostEstimate(flops=flops, bytes_accessed=moved, transcendentals=trans)


def column_of(values, rows, dtype):
    at = lax.broadcasted_iota(jnp.int32, (8, 128), 0)
    tiles = []
    for base in range(0, rows, 8):
        tile = jnp.full((8, 128), values[base], dtype)
        for r in range(1, 8):
            tile = jnp.where(at == r, values[base + r], tile)
        tiles.append(tile)
    return jnp.concatenate(tiles, axis=0)


def pick_kernel(groups, slots, tiles, chosen_in, counts_in, gates_in, tokens_in, grads_in, *rest):
    outs, spot = rest[: 2 * groups], rest[2 * groups]
    chosen, counts, gates, tokens, grads, small, big = rest[2 * groups + 1 :]
    length, model = tokens.shape
    rows = groups * slots
    width = model // tiles
    scalars = [
        pltpu.make_async_copy(src, dst, small.at[i])
        for i, (src, dst) in enumerate(((chosen_in, chosen), (counts_in, counts), (gates_in, gates)))
    ]
    loads = []
    for i in range(tiles):
        some = slice(i * width, (i + 1) * width)
        for j, (src, dst) in enumerate(((tokens_in, tokens), (grads_in, grads))):
            loads.append(pltpu.make_async_copy(src.at[:, some], dst.at[:, some], big.at[2 * i + j]))
    for copy in scalars + loads:
        copy.start()
    for copy in scalars:
        copy.wait()

    me = lax.axis_index("group")
    owner = [lax.bitwise_xor(me, r) for r in range(groups)]
    where = [chosen[0, owner[r // slots], r % slots] for r in range(rows)]
    column = jnp.concatenate([column_of(where, rows, jnp.int32)] * (length // 128), axis=1)
    onehot = jnp.where(column == lax.broadcasted_iota(jnp.int32, (rows, length), 1), 1.0, 0.0).astype(
        jnp.bfloat16
    )
    live = []
    for r in range(rows):
        e, c = owner[r // slots], r % slots
        live.append(jnp.where(c < counts[0, e], gates[0, e, c], jnp.float32(0.0)))
    scale = jnp.concatenate([column_of(live, rows, jnp.float32)] * (width // 128), axis=1)
    lane = lax.rem(lax.broadcasted_iota(jnp.int32, (8, 2 * rows), 1), rows)
    line = jnp.full((8, 2 * rows), -1, jnp.int32)
    for r in range(rows):
        line = jnp.where(lane == r, where[r], line)
    line = jnp.concatenate([line] * (length // 8), axis=0)
    spot[...] = jnp.where(
        line == lax.broadcasted_iota(jnp.int32, (length, 2 * rows), 0), 1.0, 0.0
    ).astype(jnp.bfloat16)

    for i in range(tiles):
        some = slice(i * width, (i + 1) * width)
        loads[2 * i].wait()
        x = jnp.dot(onehot, tokens[:, some], preferred_element_type=jnp.float32).astype(jnp.bfloat16)
        loads[2 * i + 1].wait()
        g = jnp.dot(onehot, grads[:, some], preferred_element_type=jnp.float32)
        g = (g * scale).astype(jnp.bfloat16)
        for j, out in enumerate(outs):
            d = j % groups
            out[:slots, some] = x[d * slots : (d + 1) * slots]
            out[slots:, some] = g[d * slots : (d + 1) * slots]


def pick(tokens, grads, chosen, counts, gates, groups):
    slots = chosen.shape[2]
    length, model = tokens.shape
    tiles = max(1, model // 512)
    rows = groups * slots
    return pl.pallas_call(
        functools.partial(pick_kernel, groups, slots, tiles),
        in_specs=[anywhere()] * 5,
        out_specs=[vmem()] * (2 * groups + 1),
        out_shape=[jax.ShapeDtypeStruct((2 * slots, model), jnp.bfloat16)] * (2 * groups)
        + [jax.ShapeDtypeStruct((length, 2 * rows), jnp.bfloat16)],
        scratch_shapes=[
            pltpu.SMEM(chosen.shape, chosen.dtype),
            pltpu.SMEM(counts.shape, counts.dtype),
            pltpu.SMEM(gates.shape, gates.dtype),
            pltpu.VMEM((length, model), jnp.bfloat16),
            pltpu.VMEM((length, model), jnp.bfloat16),
            pltpu.SemaphoreType.DMA((3,)),
            pltpu.SemaphoreType.DMA((2 * tiles,)),
        ],
        compiler_params=params(60 * 2**20),
        cost_estimate=cost(4 * rows * length * model, 4 * length * model),
        name="pick",
    )(chosen, counts, gates, tokens, grads)


def vmem():
    return pl.BlockSpec(memory_space=pltpu.VMEM)


def anywhere():
    return pl.BlockSpec(memory_space=pl.ANY)


def join_kernel(n, *refs):
    out = refs[-1]
    at = 0
    for ref in refs[:n]:
        out[at : at + ref.shape[0]] = ref[...]
        at += ref.shape[0]


def join(ins, after):
    rows, model = sum(r.shape[0] for r in ins), ins[0].shape[1]
    return pl.pallas_call(
        functools.partial(join_kernel, len(ins)),
        in_specs=[vmem()] * len(ins) + [anywhere()] * len(after),
        out_specs=vmem(),
        out_shape=jax.ShapeDtypeStruct((rows, model), jnp.bfloat16),
        compiler_params=params(10 * 2**20),
        cost_estimate=cost(0, 4 * rows * model),
        name="join",
    )(*ins, *after)


def block_kernel(slots, tile, n_in, *refs):
    ins, (w_in, w_out) = refs[:n_in], refs[n_in : n_in + 2]
    x_t, act_t, hgrad, g_all, mine, theirs, x_all, g_t, total = refs[-9:]
    half = mine.shape[0]
    at = 0
    for ref in ins:
        for row in range(0, ref.shape[0], 2 * slots):
            x_all[at : at + slots] = ref[row : row + slots]
            g_all[at : at + slots] = ref[row + slots : row + 2 * slots]
            at += slots
    x_t[...] = x_all[...].T
    g_t[...] = g_all[...].T
    for unit in range(0, w_in.shape[2], tile):
        some = slice(unit, unit + tile)
        hidden = jnp.dot(x_all[...], w_in[0, :, some], preferred_element_type=jnp.float32).T
        activation, gelu_slope = gelu_parts(hidden)
        act_t[some] = activation.astype(jnp.bfloat16)
        back = jnp.dot(w_out[0, some], g_t[...], preferred_element_type=jnp.float32)
        hg_t = (back * gelu_slope).astype(jnp.bfloat16)
        hgrad[:, some] = hg_t.T
        part = jnp.dot(w_in[0, :, some], hg_t, preferred_element_type=jnp.float32)
        if unit == 0:
            total[...] = part
        else:
            total[...] += part
    slot_grad = total[...].T
    mine[...] = slot_grad[:half]
    theirs[...] = slot_grad[half:].astype(theirs.dtype)


def block(ins, w_in, w_out, slots, after):
    model, units = w_in.shape[1:]
    rows = sum(r.shape[0] for r in ins) // 2
    half = rows // 2
    bf = functools.partial(jax.ShapeDtypeStruct, dtype=jnp.bfloat16)
    return pl.pallas_call(
        functools.partial(block_kernel, slots, min(256, units), len(ins)),
        in_specs=[vmem()] * (len(ins) + 2) + [anywhere()] * len(after),
        out_specs=[vmem()] * 6,
        out_shape=[
            bf((model, rows)),
            bf((units, rows)),
            bf((rows, units)),
            bf((rows, model)),
            jax.ShapeDtypeStruct((half, model), jnp.float32),
            bf((half, model)),
        ],
        scratch_shapes=[
            pltpu.VMEM((rows, model), jnp.bfloat16),
            pltpu.VMEM((model, rows), jnp.bfloat16),
            pltpu.VMEM((model, rows), jnp.float32),
        ],
        compiler_params=params(20 * 2**20),
        cost_estimate=cost(6 * rows * model * units, 4 * model * units, rows * units),
        name="block",
    )(*ins, w_in, w_out, *after)


def outer_kernel(n, tiles, *refs):
    left_t, right = refs[:n], refs[n : 2 * n]
    out, buf, sems = refs[-3:]
    b = jnp.concatenate([r[...] for r in right], axis=0)
    size = buf.shape[0] // tiles
    copies = []
    for i in range(tiles):
        some = slice(i * size, (i + 1) * size)
        a = jnp.concatenate([r[some] for r in left_t], axis=1)
        buf[some] = jnp.dot(a, b, preferred_element_type=jnp.float32)
        copies.append(pltpu.make_async_copy(buf.at[some], out.at[0, some], sems.at[i]))
        copies[-1].start()
    for copy in copies:
        copy.wait()


def outer(left_ts, rights, after, name):
    n, m, k = len(rights), left_ts[0].shape[0], rights[0].shape[1]
    rows = sum(r.shape[0] for r in rights)
    tiles = 4
    return pl.pallas_call(
        functools.partial(outer_kernel, n, tiles),
        in_specs=[vmem()] * (2 * n) + [anywhere()] * len(after),
        out_specs=anywhere(),
        out_shape=jax.ShapeDtypeStruct((1, m, k), jnp.float32),
        scratch_shapes=[pltpu.VMEM((m, k), jnp.float32), pltpu.SemaphoreType.DMA((tiles,))],
        compiler_params=params(20 * 2**20),
        cost_estimate=cost(2 * rows * m * k, 4 * m * k),
        name=name,
    )(*left_ts, *rights, *after)


def add_kernel(n_in, *refs):
    ins, outs = refs[:n_in], refs[n_in:]
    total = ins[0][...].astype(jnp.float32)
    for ref in ins[1:]:
        total = total + ref[...].astype(jnp.float32)
    total = total.astype(jnp.bfloat16)
    at = 0
    for out in outs:
        out[...] = total[at : at + out.shape[0]]
        at += out.shape[0]


def add_up(ins, cuts):
    rows, model = sum(cuts), ins[0].shape[1]
    return pl.pallas_call(
        functools.partial(add_kernel, len(ins)),
        in_specs=[vmem()] * len(ins),
        out_specs=[vmem()] * len(cuts),
        out_shape=[jax.ShapeDtypeStruct((c, model), jnp.bfloat16) for c in cuts],
        compiler_params=params(10 * 2**20),
        cost_estimate=cost(rows * model, 12 * rows * model),
        name="add_up",
    )(*ins)


def place_kernel(tiles, spot, *rest):
    parts, (out, buf, sems) = rest[:-3], rest[-3:]
    values = jnp.concatenate([p[...] for p in parts], axis=0)
    size = buf.shape[0] // tiles
    copies = []
    for i in range(tiles):
        some = slice(i * size, (i + 1) * size)
        buf[some] = jnp.dot(spot[some], values, preferred_element_type=jnp.float32).astype(jnp.bfloat16)
        copies.append(pltpu.make_async_copy(buf.at[some], out.at[some], sems.at[i]))
        copies[-1].start()
    for copy in copies:
        copy.wait()


def place(parts, spot):
    model = parts[0].shape[1]
    length, rows = spot.shape
    tiles = 4
    return pl.pallas_call(
        functools.partial(place_kernel, tiles),
        in_specs=[vmem()] * (1 + len(parts)),
        out_specs=anywhere(),
        out_shape=jax.ShapeDtypeStruct((length, model), jnp.bfloat16),
        scratch_shapes=[pltpu.VMEM((length, model), jnp.bfloat16), pltpu.SemaphoreType.DMA((tiles,))],
        compiler_params=params(10 * 2**20),
        cost_estimate=cost(2 * rows * length * model, 2 * length * model),
        name="place",
    )(spot, *parts)


def shards(tokens_in, out_grad, w_in, w_out, chosen, counts, gates):
    groups = lax.axis_size("group")
    fsdp = lax.axis_size("fsdp")
    ring_len = fsdp // 2
    slots = chosen.shape[2]

    def send(x, group_step, to):
        pairs = [
            (g * fsdp + f, (g ^ group_step) * fsdp + to(f)) for g in range(groups) for f in range(fsdp)
        ]
        return lax.ppermute(x, both, pairs)

    def ring(x):
        return lax.ppermute(x, "fsdp", [(f, (f + 2) % fsdp) for f in range(fsdp)])

    def pair(x):
        return lax.ppermute(x, "fsdp", [(f, f ^ 1) for f in range(fsdp)])

    *picked, spot = pick(tokens_in, out_grad, chosen, counts, gates, groups)
    order = range(groups - 1, -1, -1)
    near = {d: send(picked[d], d, lambda f: f) if d else picked[d] for d in order}
    next_ = {d: send(picked[groups + d], d, lambda f: (f + 2) % fsdp) for d in order}
    rows = groups * slots
    first = join([near[d] for d in range(groups)], [])
    ours = join([next_[d] for d in range(groups)], [first])
    results, arrived, before = [], [], []
    for k in range(1, ring_len):
        last = k == ring_len - 1
        ahead = None if last else ring(ours)
        mixed = [first, ours, pair(first), pair(ours)] if k == 1 else [ours, pair(ours)]
        results.append(block(mixed, w_in, w_out, slots, before))
        mine, theirs = results[-1][4:]
        cuts = [slots] * groups if last else [rows]
        pieces = add_up([mine, pair(theirs)] + arrived, [slots] * groups + cuts if k == 1 else cuts)
        if k == 1:
            own = [pieces[0]] + [send(pieces[d], d, lambda f: f) for d in range(1, groups)]
            pieces = pieces[groups:]
        before, after = pieces[:1], [theirs] + arrived
        if not last:
            arrived = [ring(pieces[0])]
            ours = join([ahead], after + (own[1:] if k == 2 else []))
    parts = own + [send(pieces[d], d, lambda f: (f + 2) % fsdp) for d in range(groups)]

    x_ts, act_ts, hgrads, gs = list(zip(*results))[:4]
    grad_w_out = outer(act_ts, gs, [], "grad_w_out")
    grad_w_in = outer(x_ts, hgrads, pieces[:1], "grad_w_in")
    return place(parts, spot), grad_w_in, grad_w_out


def solution(mesh):
    placed = (
        P(("group", "fsdp"), None),
        P(("group", "fsdp"), None),
        P("group", None, "fsdp"),
        P("group", "fsdp", None),
        P(("group", "fsdp"), None, None),
        P(("group", "fsdp"), None),
        P(("group", "fsdp"), None, None),
    )
    return jax.shard_map(
        shards,
        mesh=mesh,
        in_specs=placed,
        out_specs=(P(("group", "fsdp"), None), P("group", None, "fsdp"), P("group", "fsdp", None)),
        check_vma=False,
    )
```

time: 171 us -> 92.5 us (0.54)
  waiting for transfers between devices: 81.6 us -> 31.2 us
  matrix products: 31.1 us -> 0 us
  Pallas kernels: 0 us -> 29.3 us
  starting transfers between devices: 3.77 us -> 25.4 us
  blocking collectives: 19.6 us -> 0 us
  between operations: 13.9 us -> 1.02 us
  other arithmetic: 11.5 us -> 0 us
  local copies, waits for them, and re-layouts: 9.14 us -> 5.29 us
    all_gather x2 -> x0, waiting for transfers between devices: 41 us -> none  [the longest x1 25.1 us: shards(): lax.all_gather(near_grad, 'fsdp', axis=0, tiled=True)]
    reduce_scatter x1 -> x0, waiting for transfers between devices: 40.6 us -> none  [shards(): lax.psum_scatter(partial_grad, 'fsdp', scatter_dimension=0, tiled=True)]
    ppermute x0 -> x25, waiting for transfers between devices: none -> 31.2 us  [the longest x4 19.1 us: ring(): return lax.ppermute(x, 'fsdp', [(f, (f + 2) % fsdp) for f in range(fsdp)])]
    dot_general x5 -> x0, matrix products: 31.1 us -> none  [the longest x1 8.33 us: shards(): lax.dot_general(activation, expert_grad, (((0,), (0,)), ((), ())), prefer...]
    pallas_call x0 -> x14, Pallas kernels: none -> 29.3 us  [the longest x3 13.4 us: block(): pl.pallas_call(functools.partial(block_kernel, slots, min(256, units), le...]
    ppermute x0 -> x25, starting transfers between devices: none -> 25.4 us  [the longest x14 23.4 us: send(): return lax.ppermute(x, both, pairs)]
    all_to_all x2 -> x0, blocking collectives: 19.6 us -> none  [the longest x1 10.8 us: shards(): lax.all_to_all(picked_x, 'group', split_axis=0, concat_axis=0, tiled=True)]
    gather x2 -> x0, local copies, waits for them, and re-layouts: 7.43 us -> none  [the longest x1 3.72 us: shards(): jnp.take(out_grad, slot_rows, axis=0).astype(jnp.float32)]
  transfers between devices with their start and end apart: 4 -> 25, of which waited for: 3 -> 11; matrix products, arithmetic and copies ran while one was open for 14% -> 0% of each run, Pallas kernels for 0% -> 24%
where the time goes in v3:
time: 92.5 us; the launch traced here: 92.3 us
  waiting for transfers between devices  31.2 us (34%)
  Pallas kernels  29.3 us (32%)
  starting transfers between devices  25.4 us (27%)
  local copies, waits for them, and re-layouts  5.29 us (6%)
  between operations  1.02 us (1%)
    ppermute x14, starting transfers between devices, send(): return lax.ppermute(x, both, pairs)  23.4 us
    ppermute x4, waiting for transfers between devices, ring(): return lax.ppermute(x, 'fsdp', [(f, (f + 2) % fsdp) for f in range(fsdp)])  19.1 us
    pallas_call x3, Pallas kernels, block(): pl.pallas_call(functools.partial(block_kernel, slots, min(256, units), le...  13.4 us
    ppermute x14, waiting for transfers between devices, send(): return lax.ppermute(x, both, pairs)  8.22 us
    pallas_call x2, Pallas kernels, outer(): pl.pallas_call(functools.partial(outer_kernel, n, tiles), in_specs=[vmem(...  8.15 us
    unnamed x12, local copies, waits for them, and re-layouts  5.29 us
    pallas_call x1, Pallas kernels, pick(): pl.pallas_call(functools.partial(pick_kernel, groups, slots, tiles), in_s...  4.9 us
    ppermute x7, waiting for transfers between devices, pair(): return lax.ppermute(x, 'fsdp', [(f, f ^ 1) for f in range(fsdp)])  3.93 us
  transfers between devices with their start and end apart: 25, of which 11 were waited for; matrix products, arithmetic and copies ran while one was open for 0% of the time, Pallas kernels for 24%

profile of v3, /device:TPU:0, one launch (start us, length us, event | category | flops | bytes accessed | tf_op | source)
XLA Modules:
  0.0 92.3 jit_solution(5179995477616668082)
XLA Ops:
  0.6 4.9 %pick.1 = (bf16[32,2048]{1,0:T(8,128)(2,1)}, bf16[32,2048]{1,0:T(8,128)(2,1)}, bf16[32,2048]{1,0:T(8,128)(2,1)}, bf16[32,2048]{1,0:T(8,128)(2,1)}, bf16[32,2048]...) custom-call(s32[1,4,16]{2,1,0:T(4,128)} %chosen_in.1, ...), custom_call_target="tpu_custom_call" | custom-call | flops 536870912 | bytes 8388608 | tf_op jit(solution)/shard_map/pick/pallas_call | solution.py:102
  5.5 3.0 %collective-permute-start = (bf16[32,2048]{1,0:T(8,128)(2,1)}, bf16[32,2048]{1,0:T(8,128)(2,1)S(1)}, u32[]{:S(2)}, u32[]{:S(2)}) collective-permute-start(bf16[32,2048]{1,0:T(8,128)(2,1)} %get-tuple-element.41), channel_id=1, source_target_pairs={{0,8},{1,9},{2,10},{3,11},{4,12},{5,13},{6,14},{7,15},{8,0},{9,1},... | collective-permute-start | bytes 393224 | tf_op jit(solution)/shard_map/ppermute | solution.py:307
  8.5 1.5 %collective-permute-start.1 = (bf16[32,2048]{1,0:T(8,128)(2,1)}, bf16[32,2048]{1,0:T(8,128)(2,1)S(1)}, u32[]{:S(2)}, u32[]{:S(2)}) collective-permute-start(bf16[32,2048]{1,0:T(8,128)(2,1)} %get-tuple-element.42), channel_id=1, source_target_pairs={{0,16},{1,17},{2,18},{3,19},{4,20},{5,21},{6,22},{7,23},{8,24},{9,... | collective-permute-start | bytes 393224 | tf_op jit(solution)/shard_map/ppermute | solution.py:307
  10.1 0.0 collective-permute-start.2
  10.1 2.0 %collective-permute-start.3 = (bf16[32,2048]{1,0:T(8,128)(2,1)}, bf16[32,2048]{1,0:T(8,128)(2,1)S(1)}, u32[]{:S(2)}, u32[]{:S(2)}) collective-permute-start(bf16[32,2048]{1,0:T(8,128)(2,1)} %get-tuple-element.44), channel_id=1, source_target_pairs={{0,2},{1,3},{2,4},{3,5},{4,6},{5,7},{6,0},{7,1},{8,10},{9,11},{10,... | collective-permute-start | bytes 393224 | tf_op jit(solution)/shard_map/ppermute | solution.py:307
  12.1 2.5 %collective-permute-start.4 = (bf16[32,2048]{1,0:T(8,128)(2,1)}, bf16[32,2048]{1,0:T(8,128)(2,1)S(1)}, u32[]{:S(2)}, u32[]{:S(2)}) collective-permute-start(bf16[32,2048]{1,0:T(8,128)(2,1)} %get-tuple-element.45), channel_id=1, source_target_pairs={{0,10},{1,11},{2,12},{3,13},{4,14},{5,15},{6,8},{7,9},{8,2},{9,3},... | collective-permute-start | bytes 393224 | tf_op jit(solution)/shard_map/ppermute | solution.py:307
  14.6 0.0 collective-permute-done.refs_1_
  14.6 2.5 %collective-permute-start.5 = (bf16[32,2048]{1,0:T(8,128)(2,1)}, bf16[32,2048]{1,0:T(8,128)(2,1)S(1)}, u32[]{:S(2)}, u32[]{:S(2)}) collective-permute-start(bf16[32,2048]{1,0:T(8,128)(2,1)} %get-tuple-element.46), channel_id=1, source_target_pairs={{0,18},{1,19},{2,20},{3,21},{4,22},{5,23},{6,16},{7,17},{8,26},{9,... | collective-permute-start | bytes 393224 | tf_op jit(solution)/shard_map/ppermute | solution.py:307
  17.2 0.0 collective-permute-done.1.refs_2_
  17.2 1.5 %collective-permute-start.6 = (bf16[32,2048]{1,0:T(8,128)(2,1)}, bf16[32,2048]{1,0:T(8,128)(2,1)S(1)}, u32[]{:S(2)}, u32[]{:S(2)}) collective-permute-start(bf16[32,2048]{1,0:T(8,128)(2,1)} %get-tuple-element.47), channel_id=1, source_target_pairs={{0,26},{1,27},{2,28},{3,29},{4,30},{5,31},{6,24},{7,25},{8,18},{9,... | collective-permute-start | bytes 393224 | tf_op jit(solution)/shard_map/ppermute | solution.py:307
  18.6 0.0 collective-permute-done.2.refs_3_
  18.6 0.9 copy-done.5
  19.6 0.0 collective-permute-done.3.refs_0_
  19.6 3.1 %collective-permute-done.4.refs_1_ = bf16[32,2048]{1,0:T(8,128)(2,1)S(1)} collective-permute-done((bf16[32,2048]{1,0:T(8,128)(2,1)}, bf16[32,2048]{1,0:T(8,128)(2,1)S(1)}, u32[]{:S(2)}, u32[]{:S(2)}) %collective-permute-start.4) | collective-permute-done | bytes 131104 | tf_op jit(solution)/shard_map/ppermute | solution.py:307
  22.7 2.7 %collective-permute-done.5.refs_2_ = bf16[32,2048]{1,0:T(8,128)(2,1)S(1)} collective-permute-done((bf16[32,2048]{1,0:T(8,128)(2,1)}, bf16[32,2048]{1,0:T(8,128)(2,1)S(1)}, u32[]{:S(2)}, u32[]{:S(2)}) %collective-permute-start.5) | collective-permute-done | bytes 131104 | tf_op jit(solution)/shard_map/ppermute | solution.py:307
  25.5 1.9 %collective-permute-done.6.refs_3_ = bf16[32,2048]{1,0:T(8,128)(2,1)S(1)} collective-permute-done((bf16[32,2048]{1,0:T(8,128)(2,1)}, bf16[32,2048]{1,0:T(8,128)(2,1)S(1)}, u32[]{:S(2)}, u32[]{:S(2)}) %collective-permute-start.6) | collective-permute-done | bytes 131104 | tf_op jit(solution)/shard_map/ppermute | solution.py:307
  27.4 0.1 collective-permute-start.8
  27.4 0.5 collective-permute-start.7
  27.9 0.0 collective-permute-start.13
  27.9 1.4 %collective-permute-done.8.refs_3_ = bf16[128,2048]{1,0:T(8,128)(2,1)S(1)} collective-permute-done((bf16[128,2048]{1,0:T(8,128)(2,1)S(1)}, bf16[128,2048]{1,0:T(8,128)(2,1)S(1)}, u32[]{:S(2)}, u32[]{:S(2)}) %collective-permute-start.8) | collective-permute-done | bytes 524320 | tf_op jit(solution)/shard_map/ppermute | solution.py:313
  29.3 0.7 collective-permute-done.7.refs_2_
  30.1 2.2 %copy-done = bf16[1,2048,1024]{2,1,0:T(8,128)(2,1)S(1)} copy-done((bf16[1,2048,1024]{2,1,0:T(8,128)(2,1)S(1)}, bf16[1,2048,1024]{2,1,0:T(8,128)(2,1)}, u32[]{:S(2)}) %copy-start) | copy-done | bytes 4194328
  32.3 2.2 %copy-done.2 = bf16[1,1024,2048]{2,1,0:T(8,128)(2,1)S(1)} copy-done((bf16[1,1024,2048]{2,1,0:T(8,128)(2,1)S(1)}, bf16[1,1024,2048]{2,1,0:T(8,128)(2,1)}, u32[]{:S(2)}) %copy-start.2) | copy-done | bytes 4194328
  34.5 5.3 %block.3 = (bf16[2048,256]{1,0:T(8,128)(2,1)S(1)}, bf16[1024,256]{1,0:T(8,128)(2,1)S(1)}, bf16[256,1024]{1,0:T(8,128)(2,1)S(1)}, bf16[256,2048]{1,0:T(8,128)(2,1...) custom-call(bf16[128,2048]{1,0:T(8,128)(2,1)S(1)} %join.4.refs_4_.refs_0_, ...), custom_call_target="tpu_custom_call" | custom-call | flops 3221225472 | bytes 8388608 | tf_op jit(solution)/shard_map/block/pallas_call | solution.py:187
  39.7 0.2 collective-permute-start.9
  39.9 3.7 %collective-permute-done.13.refs_0_ = bf16[128,2048]{1,0:T(8,128)(2,1)S(1)} collective-permute-done((bf16[128,2048]{1,0:T(8,128)(2,1)S(1)}, bf16[128,2048]{1,0:T(8,128)(2,1)S(1)}, u32[]{:S(2)}, u32[]{:S(2)}) %collective-permute-start.13) | collective-permute-done | bytes 524320 | tf_op jit(solution)/shard_map/ppermute | solution.py:310
  43.7 0.1 collective-permute-start.15
  43.8 0.1 collective-permute-start.14
  43.8 0.0 collective-permute-done.9.refs_1_
  43.8 0.1 add_up.3
  43.9 0.2 collective-permute-start.16
  44.2 1.3 %collective-permute-start.10 = (bf16[16,2048]{1,0:T(8,128)(2,1)S(1)}, bf16[16,2048]{1,0:T(8,128)(2,1)S(1)}, u32[]{:S(2)}, u32[]{:S(2)}) collective-permute-start(bf16[16,2048]{1,0:T(8,128)(2,1)S(1)} %get-tuple-element.51), channel_id=1, source_target_pairs={{0,8},{1,9},{2,10},{3,11},{4,12},{5,13},{6,14},{7,15},{8,0},{9,1},... | collective-permute-start | bytes 196616 | tf_op jit(solution)/shard_map/ppermute | solution.py:307
  45.5 0.3 collective-permute-start.11
  45.7 0.0 collective-permute-done.15.refs_1_
  45.7 2.0 %collective-permute-start.12 = (bf16[16,2048]{1,0:T(8,128)(2,1)S(1)}, bf16[16,2048]{1,0:T(8,128)(2,1)S(1)}, u32[]{:S(2)}, u32[]{:S(2)}) collective-permute-start(bf16[16,2048]{1,0:T(8,128)(2,1)S(1)} %get-tuple-element.53), channel_id=1, source_target_pairs={{0,24},{1,25},{2,26},{3,27},{4,28},{5,29},{6,30},{7,31},{8,16},{9,... | collective-permute-start | bytes 196616 | tf_op jit(solution)/shard_map/ppermute | solution.py:307
  47.7 4.1 %block.4 = (bf16[2048,128]{1,0:T(8,128)(2,1)S(1)}, bf16[1024,128]{1,0:T(8,128)(2,1)S(1)}, bf16[128,1024]{1,0:T(8,128)(2,1)S(1)}, bf16[128,2048]{1,0:T(8,128)(2,1...) custom-call(bf16[128,2048]{1,0:T(8,128)(2,1)S(1)} %join.6.refs_0_, ...), custom_call_target="tpu_custom_call" | custom-call | flops 1610612736 | bytes 8388608 | tf_op jit(solution)/shard_map/block/pallas_call | solution.py:187
  51.8 8.5 %collective-permute-done.14.refs_0_ = bf16[128,2048]{1,0:T(8,128)(2,1)S(1)} collective-permute-done((bf16[128,2048]{1,0:T(8,128)(2,1)S(1)}, bf16[128,2048]{1,0:T(8,128)(2,1)S(1)}, u32[]{:S(2)}, u32[]{:S(2)}) %collective-permute-start.14) | collective-permute-done | bytes 524320 | tf_op jit(solution)/shard_map/ppermute | solution.py:310
  60.3 0.0 collective-permute-done.10.refs_3_.rest_1_
  60.3 0.0 collective-permute-done.11.refs_4_.rest_2_
  60.3 0.0 collective-permute-done.12.refs_5_.rest_3_
  60.3 5.2 %collective-permute-done.16.refs_2_ = bf16[64,2048]{1,0:T(8,128)(2,1)S(1)} collective-permute-done((bf16[64,2048]{1,0:T(8,128)(2,1)S(1)}, bf16[64,2048]{1,0:T(8,128)(2,1)S(1)}, u32[]{:S(2)}, u32[]{:S(2)}) %collective-permute-start.16) | collective-permute-done | bytes 262176 | tf_op jit(solution)/shard_map/ppermute | solution.py:310
  65.5 0.1 collective-permute-start.17
  65.6 0.5 collective-permute-start.18
  66.1 1.8 %collective-permute-done.18.refs_1_ = bf16[64,2048]{1,0:T(8,128)(2,1)S(1)} collective-permute-done((bf16[64,2048]{1,0:T(8,128)(2,1)S(1)}, bf16[64,2048]{1,0:T(8,128)(2,1)S(1)}, u32[]{:S(2)}, u32[]{:S(2)}) %collective-permute-start.18) | collective-permute-done | bytes 262176 | tf_op jit(solution)/shard_map/ppermute | solution.py:313
  67.9 0.1 add_up.4.refs_4_
  68.0 0.1 collective-permute-start.20
  68.0 0.0 collective-permute-done.17.refs_1_
  68.0 4.1 %block.5 = (bf16[2048,128]{1,0:T(8,128)(2,1)S(1)}, bf16[1024,128]{1,0:T(8,128)(2,1)S(1)}, bf16[128,1024]{1,0:T(8,128)(2,1)S(1)}, bf16[128,2048]{1,0:T(8,128)(2,1...) custom-call(bf16[128,2048]{1,0:T(8,128)(2,1)S(1)} %join.7.refs_0_, ...), custom_call_target="tpu_custom_call" | custom-call | flops 1610612736 | bytes 8388608 | tf_op jit(solution)/shard_map/block/pallas_call | solution.py:187
  72.2 0.2 collective-permute-start.19
  72.4 4.1 %grad_w_out.1 = f32[1,1024,2048]{2,1,0:T(8,128)} custom-call(bf16[1024,256]{1,0:T(8,128)(2,1)S(1)} %get-tuple-element.69.refs_0_, bf16[1024,128]{1,0:T(8,128)(2,1)S(1)} %get-tuple-element.70.refs_1_, bf16[1024,128]{1,0:T(8,128)(2,1)S(1)} %get-tuple-element.71.refs_2_, bf16[256,2048]{1,0:T(8,128)(2,1)S(1)} %get-tuple-element.72.refs_3_, ...), custom_call_target="tpu_custom_call" | custom-call | flops 2147483648 | bytes 8388608 | tf_op jit(solution)/shard_map/grad_w_out/pallas_call | solution.py:230
  76.4 1.7 %collective-permute-done.20.refs_2_ = bf16[64,2048]{1,0:T(8,128)(2,1)S(1)} collective-permute-done((bf16[64,2048]{1,0:T(8,128)(2,1)S(1)}, bf16[64,2048]{1,0:T(8,128)(2,1)S(1)}, u32[]{:S(2)}, u32[]{:S(2)}) %collective-permute-start.20) | collective-permute-done | bytes 262176 | tf_op jit(solution)/shard_map/ppermute | solution.py:310
  78.2 0.0 collective-permute-done.19.refs_1_
  78.2 0.1 add_up.5
  78.3 0.1 collective-permute-start.21
  78.3 0.1 collective-permute-start.22
  78.4 3.4 %collective-permute-start.23 = (bf16[16,2048]{1,0:T(8,128)(2,1)S(1)}, bf16[16,2048]{1,0:T(8,128)(2,1)S(1)}, u32[]{:S(2)}, u32[]{:S(2)}) collective-permute-start(bf16[16,2048]{1,0:T(8,128)(2,1)S(1)} %get-tuple-element.61), channel_id=1, source_target_pairs={{0,18},{1,19},{2,20},{3,21},{4,22},{5,23},{6,16},{7,17},{8,26},{9,... | collective-permute-start | bytes 196616 | tf_op jit(solution)/shard_map/ppermute | solution.py:307
  81.8 3.3 %collective-permute-start.24 = (bf16[16,2048]{1,0:T(8,128)(2,1)S(1)}, bf16[16,2048]{1,0:T(8,128)(2,1)S(1)}, u32[]{:S(2)}, u32[]{:S(2)}) collective-permute-start(bf16[16,2048]{1,0:T(8,128)(2,1)S(1)} %get-tuple-element.62), channel_id=1, source_target_pairs={{0,26},{1,27},{2,28},{3,29},{4,30},{5,31},{6,24},{7,25},{8,18},{9,... | collective-permute-start | bytes 196616 | tf_op jit(solution)/shard_map/ppermute | solution.py:307
  85.1 4.1 %grad_w_in.1 = f32[1,2048,1024]{2,1,0:T(8,128)} custom-call(bf16[2048,256]{1,0:T(8,128)(2,1)S(1)} %get-tuple-element.63.refs_0_, bf16[2048,128]{1,0:T(8,128)(2,1)S(1)} %get-tuple-element.64.refs_1_, bf16[2048,128]{1,0:T(8,128)(2,1)S(1)} %get-tuple-element.65.refs_2_, bf16[256,1024]{1,0:T(8,128)(2,1)S(1)} %get-tuple-element.66.refs_3_, ...), custom_call_target="tpu_custom_call" | custom-call | flops 2147483648 | bytes 8388608 | tf_op jit(solution)/shard_map/grad_w_in/pallas_call | solution.py:230
  89.1 0.0 collective-permute-done.21.rest_4_
  89.2 0.0 collective-permute-done.22.rest_5_
  89.2 0.0 collective-permute-done.23.rest_6_
  89.2 0.5 collective-permute-done.24.rest_7_
  89.6 0.0 copy-done.4
  89.7 2.5 %place.1 = bf16[1024,2048]{1,0:T(8,128)(2,1)} custom-call(bf16[1024,128]{1,0:T(8,128)(2,1)S(1)} %copy-done.4, bf16[16,2048]{1,0:T(8,128)(2,1)S(1)} %get-tuple-element.50.rest_0_, bf16[16,2048]{1,0:T(8,128)(2,1)S(1)} %collective-permute-done.10.refs_3_.rest_1_, bf16[16,2048]{1,0:T(8,128)(2,1)S(1)} %collective-permute-done.11.refs_4_.rest_2_, ...), custom_call_target="tpu_custom_call" | custom-call | flops 536870912 | bytes 4194304 | tf_op jit(solution)/shard_map/place/pallas_call | solution.py:285
  (12 shorter events, 0.2 us)
Async XLA Ops:
  5.5 9.1 %collective-permute-start = (bf16[32,2048]{1,0:T(8,128)(2,1)}, bf16[32,2048]{1,0:T(8,128)(2,1)S(1)}, u32[]{:S(2)}, u32[]{:S(2)}) collective-permute-start(bf16[32,2048]{1,0:T(8,128)(2,1)} %get-tuple-element.41), channel_id=1, source_target_pairs={{0,8},{1,9},{2,10},{3,11},{4,12},{5,13},{6,14},{7,15},{8,0},{9,1},... | collective-permute-start | bytes 393224 | tf_op jit(solution)/shard_map/ppermute | solution.py:307
  8.5 8.6 %collective-permute-start.1 = (bf16[32,2048]{1,0:T(8,128)(2,1)}, bf16[32,2048]{1,0:T(8,128)(2,1)S(1)}, u32[]{:S(2)}, u32[]{:S(2)}) collective-permute-start(bf16[32,2048]{1,0:T(8,128)(2,1)} %get-tuple-element.42), channel_id=1, source_target_pairs={{0,16},{1,17},{2,18},{3,19},{4,20},{5,21},{6,22},{7,23},{8,24},{9,... | collective-permute-start | bytes 393224 | tf_op jit(solution)/shard_map/ppermute | solution.py:307
  10.1 8.6 %collective-permute-start.2 = (bf16[32,2048]{1,0:T(8,128)(2,1)}, bf16[32,2048]{1,0:T(8,128)(2,1)S(1)}, u32[]{:S(2)}, u32[]{:S(2)}) collective-permute-start(bf16[32,2048]{1,0:T(8,128)(2,1)} %get-tuple-element.43), channel_id=1, source_target_pairs={{0,24},{1,25},{2,26},{3,27},{4,28},{5,29},{6,30},{7,31},{8,16},{9,... | collective-permute-start | bytes 393224 | tf_op jit(solution)/shard_map/ppermute | solution.py:307
  10.1 9.5 %collective-permute-start.3 = (bf16[32,2048]{1,0:T(8,128)(2,1)}, bf16[32,2048]{1,0:T(8,128)(2,1)S(1)}, u32[]{:S(2)}, u32[]{:S(2)}) collective-permute-start(bf16[32,2048]{1,0:T(8,128)(2,1)} %get-tuple-element.44), channel_id=1, source_target_pairs={{0,2},{1,3},{2,4},{3,5},{4,6},{5,7},{6,0},{7,1},{8,10},{9,11},{10,... | collective-permute-start | bytes 393224 | tf_op jit(solution)/shard_map/ppermute | solution.py:307
  12.1 10.6 %collective-permute-start.4 = (bf16[32,2048]{1,0:T(8,128)(2,1)}, bf16[32,2048]{1,0:T(8,128)(2,1)S(1)}, u32[]{:S(2)}, u32[]{:S(2)}) collective-permute-start(bf16[32,2048]{1,0:T(8,128)(2,1)} %get-tuple-element.45), channel_id=1, source_target_pairs={{0,10},{1,11},{2,12},{3,13},{4,14},{5,15},{6,8},{7,9},{8,2},{9,3},... | collective-permute-start | bytes 393224 | tf_op jit(solution)/shard_map/ppermute | solution.py:307
  14.6 10.8 %collective-permute-start.5 = (bf16[32,2048]{1,0:T(8,128)(2,1)}, bf16[32,2048]{1,0:T(8,128)(2,1)S(1)}, u32[]{:S(2)}, u32[]{:S(2)}) collective-permute-start(bf16[32,2048]{1,0:T(8,128)(2,1)} %get-tuple-element.46), channel_id=1, source_target_pairs={{0,18},{1,19},{2,20},{3,21},{4,22},{5,23},{6,16},{7,17},{8,26},{9,... | collective-permute-start | bytes 393224 | tf_op jit(solution)/shard_map/ppermute | solution.py:307
  17.2 10.2 %collective-permute-start.6 = (bf16[32,2048]{1,0:T(8,128)(2,1)}, bf16[32,2048]{1,0:T(8,128)(2,1)S(1)}, u32[]{:S(2)}, u32[]{:S(2)}) collective-permute-start(bf16[32,2048]{1,0:T(8,128)(2,1)} %get-tuple-element.47), channel_id=1, source_target_pairs={{0,26},{1,27},{2,28},{3,29},{4,30},{5,31},{6,24},{7,25},{8,18},{9,... | collective-permute-start | bytes 393224 | tf_op jit(solution)/shard_map/ppermute | solution.py:307
  18.6 0.9 copy-start.5
  27.4 2.0 %collective-permute-start.8 = (bf16[128,2048]{1,0:T(8,128)(2,1)S(1)}, bf16[128,2048]{1,0:T(8,128)(2,1)S(1)}, u32[]{:S(2)}, u32[]{:S(2)}) collective-permute-start(bf16[128,2048]{1,0:T(8,128)(2,1)S(1)} %join.5.refs_1_), channel_id=1, source_target_pairs={{0,1},{1,0},{2,3},{3,2},{4,5},{5,4},{6,7},{7,6},{8,9},{9,8},{10,11... | collective-permute-start | bytes 1572872 | tf_op jit(solution)/shard_map/ppermute | solution.py:313
  27.4 2.6 %collective-permute-start.7 = (bf16[128,2048]{1,0:T(8,128)(2,1)S(1)}, bf16[128,2048]{1,0:T(8,128)(2,1)S(1)}, u32[]{:S(2)}, u32[]{:S(2)}) collective-permute-start(bf16[128,2048]{1,0:T(8,128)(2,1)S(1)} %join.4.refs_4_.refs_0_), channel_id=1, source_target_pairs={{0,1},{1,0},{2,3},{3,2},{4,5},{5,4},{6,7},{7,6},{8,9},{9,8},{10,11... | collective-permute-start | bytes 1572872 | tf_op jit(solution)/shard_map/ppermute | solution.py:313
  27.9 15.7 %collective-permute-start.13 = (bf16[128,2048]{1,0:T(8,128)(2,1)S(1)}, bf16[128,2048]{1,0:T(8,128)(2,1)S(1)}, u32[]{:S(2)}, u32[]{:S(2)}) collective-permute-start(bf16[128,2048]{1,0:T(8,128)(2,1)S(1)} %join.5.refs_1_), channel_id=1, source_target_pairs={{0,2},{1,3},{2,4},{3,5},{4,6},{5,7},{6,0},{7,1},{8,10},{9,11},{10,... | collective-permute-start | bytes 1572872 | tf_op jit(solution)/shard_map/ppermute | solution.py:310
  30.1 2.2 %copy-start = (bf16[1,2048,1024]{2,1,0:T(8,128)(2,1)S(1)}, bf16[1,2048,1024]{2,1,0:T(8,128)(2,1)}, u32[]{:S(2)}) copy-start(bf16[1,2048,1024]{2,1,0:T(8,128)(2,1)} %refs_2_.3) | copy-start | bytes 12582916
  32.3 2.2 %copy-start.2 = (bf16[1,1024,2048]{2,1,0:T(8,128)(2,1)S(1)}, bf16[1,1024,2048]{2,1,0:T(8,128)(2,1)}, u32[]{:S(2)}) copy-start(bf16[1,1024,2048]{2,1,0:T(8,128)(2,1)} %refs_3_.3) | copy-start | bytes 12582916
  34.5 13.3 %copy-start.1 = (bf16[1,2048,1024]{2,1,0:T(8,128)(2,1)S(1)}, bf16[1,2048,1024]{2,1,0:T(8,128)(2,1)}, u32[]{:S(2)}) copy-start(bf16[1,2048,1024]{2,1,0:T(8,128)(2,1)} %refs_2_.3) | copy-start | bytes 12582916
  34.5 13.3 %copy-start.3 = (bf16[1,1024,2048]{2,1,0:T(8,128)(2,1)S(1)}, bf16[1,1024,2048]{2,1,0:T(8,128)(2,1)}, u32[]{:S(2)}) copy-start(bf16[1,1024,2048]{2,1,0:T(8,128)(2,1)} %refs_3_.3) | copy-start | bytes 12582916
  39.7 4.1 %collective-permute-start.9 = (bf16[128,2048]{1,0:T(8,128)(2,1)S(1)}, bf16[128,2048]{1,0:T(8,128)(2,1)S(1)}, u32[]{:S(2)}, u32[]{:S(2)}) collective-permute-start(bf16[128,2048]{1,0:T(8,128)(2,1)S(1)} %get-tuple-element.49.refs_1_), channel_id=1, source_target_pairs={{0,1},{1,0},{2,3},{3,2},{4,5},{5,4},{6,7},{7,6},{8,9},{9,8},{10,11... | collective-permute-start | bytes 1572872 | tf_op jit(solution)/shard_map/ppermute | solution.py:313
  43.7 2.1 %collective-permute-start.15 = (bf16[128,2048]{1,0:T(8,128)(2,1)S(1)}, bf16[128,2048]{1,0:T(8,128)(2,1)S(1)}, u32[]{:S(2)}, u32[]{:S(2)}) collective-permute-start(bf16[128,2048]{1,0:T(8,128)(2,1)S(1)} %join.6.refs_0_), channel_id=1, source_target_pairs={{0,1},{1,0},{2,3},{3,2},{4,5},{5,4},{6,7},{7,6},{8,9},{9,8},{10,11... | collective-permute-start | bytes 1572872 | tf_op jit(solution)/shard_map/ppermute | solution.py:313
  43.8 16.6 %collective-permute-start.14 = (bf16[128,2048]{1,0:T(8,128)(2,1)S(1)}, bf16[128,2048]{1,0:T(8,128)(2,1)S(1)}, u32[]{:S(2)}, u32[]{:S(2)}) collective-permute-start(bf16[128,2048]{1,0:T(8,128)(2,1)S(1)} %join.6.refs_0_), channel_id=1, source_target_pairs={{0,2},{1,3},{2,4},{3,5},{4,6},{5,7},{6,0},{7,1},{8,10},{9,11},{10,... | collective-permute-start | bytes 1572872 | tf_op jit(solution)/shard_map/ppermute | solution.py:310
  43.9 21.6 %collective-permute-start.16 = (bf16[64,2048]{1,0:T(8,128)(2,1)S(1)}, bf16[64,2048]{1,0:T(8,128)(2,1)S(1)}, u32[]{:S(2)}, u32[]{:S(2)}) collective-permute-start(bf16[64,2048]{1,0:T(8,128)(2,1)S(1)} %get-tuple-element.54.refs_4_), channel_id=1, source_target_pairs={{0,2},{1,3},{2,4},{3,5},{4,6},{5,7},{6,0},{7,1},{8,10},{9,11},{10,... | collective-permute-start | bytes 786440 | tf_op jit(solution)/shard_map/ppermute | solution.py:310
  44.2 16.2 %collective-permute-start.10 = (bf16[16,2048]{1,0:T(8,128)(2,1)S(1)}, bf16[16,2048]{1,0:T(8,128)(2,1)S(1)}, u32[]{:S(2)}, u32[]{:S(2)}) collective-permute-start(bf16[16,2048]{1,0:T(8,128)(2,1)S(1)} %get-tuple-element.51), channel_id=1, source_target_pairs={{0,8},{1,9},{2,10},{3,11},{4,12},{5,13},{6,14},{7,15},{8,0},{9,1},... | collective-permute-start | bytes 196616 | tf_op jit(solution)/shard_map/ppermute | solution.py:307
  45.5 14.9 %collective-permute-start.11 = (bf16[16,2048]{1,0:T(8,128)(2,1)S(1)}, bf16[16,2048]{1,0:T(8,128)(2,1)S(1)}, u32[]{:S(2)}, u32[]{:S(2)}) collective-permute-start(bf16[16,2048]{1,0:T(8,128)(2,1)S(1)} %get-tuple-element.52), channel_id=1, source_target_pairs={{0,16},{1,17},{2,18},{3,19},{4,20},{5,21},{6,22},{7,23},{8,24},{9,... | collective-permute-start | bytes 196616 | tf_op jit(solution)/shard_map/ppermute | solution.py:307
  45.7 14.6 %collective-permute-start.12 = (bf16[16,2048]{1,0:T(8,128)(2,1)S(1)}, bf16[16,2048]{1,0:T(8,128)(2,1)S(1)}, u32[]{:S(2)}, u32[]{:S(2)}) collective-permute-start(bf16[16,2048]{1,0:T(8,128)(2,1)S(1)} %get-tuple-element.53), channel_id=1, source_target_pairs={{0,24},{1,25},{2,26},{3,27},{4,28},{5,29},{6,30},{7,31},{8,16},{9,... | collective-permute-start | bytes 196616 | tf_op jit(solution)/shard_map/ppermute | solution.py:307
  65.5 2.5 %collective-permute-start.17 = (bf16[128,2048]{1,0:T(8,128)(2,1)S(1)}, bf16[128,2048]{1,0:T(8,128)(2,1)S(1)}, u32[]{:S(2)}, u32[]{:S(2)}) collective-permute-start(bf16[128,2048]{1,0:T(8,128)(2,1)S(1)} %join.7.refs_0_), channel_id=1, source_target_pairs={{0,1},{1,0},{2,3},{3,2},{4,5},{5,4},{6,7},{7,6},{8,9},{9,8},{10,11... | collective-permute-start | bytes 1572872 | tf_op jit(solution)/shard_map/ppermute | solution.py:313
  65.6 2.3 %collective-permute-start.18 = (bf16[64,2048]{1,0:T(8,128)(2,1)S(1)}, bf16[64,2048]{1,0:T(8,128)(2,1)S(1)}, u32[]{:S(2)}, u32[]{:S(2)}) collective-permute-start(bf16[64,2048]{1,0:T(8,128)(2,1)S(1)} %get-tuple-element.55.refs_1_), channel_id=1, source_target_pairs={{0,1},{1,0},{2,3},{3,2},{4,5},{5,4},{6,7},{7,6},{8,9},{9,8},{10,11... | collective-permute-start | bytes 786440 | tf_op jit(solution)/shard_map/ppermute | solution.py:313
  68.0 10.2 %collective-permute-start.20 = (bf16[64,2048]{1,0:T(8,128)(2,1)S(1)}, bf16[64,2048]{1,0:T(8,128)(2,1)S(1)}, u32[]{:S(2)}, u32[]{:S(2)}) collective-permute-start(bf16[64,2048]{1,0:T(8,128)(2,1)S(1)} %add_up.4.refs_4_), channel_id=1, source_target_pairs={{0,2},{1,3},{2,4},{3,5},{4,6},{5,7},{6,0},{7,1},{8,10},{9,11},{10,... | collective-permute-start | bytes 786440 | tf_op jit(solution)/shard_map/ppermute | solution.py:310
  72.2 6.0 %collective-permute-start.19 = (bf16[64,2048]{1,0:T(8,128)(2,1)S(1)}, bf16[64,2048]{1,0:T(8,128)(2,1)S(1)}, u32[]{:S(2)}, u32[]{:S(2)}) collective-permute-start(bf16[64,2048]{1,0:T(8,128)(2,1)S(1)} %get-tuple-element.58), channel_id=1, source_target_pairs={{0,1},{1,0},{2,3},{3,2},{4,5},{5,4},{6,7},{7,6},{8,9},{9,8},{10,11... | collective-permute-start | bytes 786440 | tf_op jit(solution)/shard_map/ppermute | solution.py:313
  78.3 10.9 %collective-permute-start.21 = (bf16[16,2048]{1,0:T(8,128)(2,1)S(1)}, bf16[16,2048]{1,0:T(8,128)(2,1)S(1)}, u32[]{:S(2)}, u32[]{:S(2)}) collective-permute-start(bf16[16,2048]{1,0:T(8,128)(2,1)S(1)} %get-tuple-element.59.refs_6_), channel_id=1, source_target_pairs={{0,2},{1,3},{2,4},{3,5},{4,6},{5,7},{6,0},{7,1},{8,10},{9,11},{10,... | collective-permute-start | bytes 196616 | tf_op jit(solution)/shard_map/ppermute | solution.py:307
  78.3 10.8 %collective-permute-start.22 = (bf16[16,2048]{1,0:T(8,128)(2,1)S(1)}, bf16[16,2048]{1,0:T(8,128)(2,1)S(1)}, u32[]{:S(2)}, u32[]{:S(2)}) collective-permute-start(bf16[16,2048]{1,0:T(8,128)(2,1)S(1)} %get-tuple-element.60), channel_id=1, source_target_pairs={{0,10},{1,11},{2,12},{3,13},{4,14},{5,15},{6,8},{7,9},{8,2},{9,3},... | collective-permute-start | bytes 196616 | tf_op jit(solution)/shard_map/ppermute | solution.py:307
  78.4 10.8 %collective-permute-start.23 = (bf16[16,2048]{1,0:T(8,128)(2,1)S(1)}, bf16[16,2048]{1,0:T(8,128)(2,1)S(1)}, u32[]{:S(2)}, u32[]{:S(2)}) collective-permute-start(bf16[16,2048]{1,0:T(8,128)(2,1)S(1)} %get-tuple-element.61), channel_id=1, source_target_pairs={{0,18},{1,19},{2,20},{3,21},{4,22},{5,23},{6,16},{7,17},{8,26},{9,... | collective-permute-start | bytes 196616 | tf_op jit(solution)/shard_map/ppermute | solution.py:307
  81.8 7.9 %collective-permute-start.24 = (bf16[16,2048]{1,0:T(8,128)(2,1)S(1)}, bf16[16,2048]{1,0:T(8,128)(2,1)S(1)}, u32[]{:S(2)}, u32[]{:S(2)}) collective-permute-start(bf16[16,2048]{1,0:T(8,128)(2,1)S(1)} %get-tuple-element.62), channel_id=1, source_target_pairs={{0,26},{1,27},{2,28},{3,29},{4,30},{5,31},{6,24},{7,25},{8,18},{9,... | collective-permute-start | bytes 196616 | tf_op jit(solution)/shard_map/ppermute | solution.py:307
  85.1 4.6 %copy-start.4 = (bf16[1024,128]{1,0:T(8,128)(2,1)S(1)}, bf16[1024,128]{1,0:T(8,128)(2,1)}, u32[]{:S(2)}) copy-start(bf16[1024,128]{1,0:T(8,128)(2,1)} %get-tuple-element.39.spot) | copy-start | bytes 786436

commit v4 on v3

--- a/solution.py
+++ b/solution.py
@@ -239,11 +239,12 @@
     )(*left_ts, *rights, *after)
 
 
-def add_kernel(n_in, *refs):
+def add_kernel(n_in, at, rows, *refs):
     ins, outs = refs[:n_in], refs[n_in:]
-    total = ins[0][...].astype(jnp.float32)
-    for ref in ins[1:]:
-        total = total + ref[...].astype(jnp.float32)
+    total = None
+    for ref in ins:
+        part = (ref[...] if ref.shape[0] == rows else ref[at : at + rows]).astype(jnp.float32)
+        total = part if total is None else total + part
     total = total.astype(jnp.bfloat16)
     at = 0
     for out in outs:
@@ -251,10 +252,10 @@
         at += out.shape[0]
 
 
-def add_up(ins, cuts):
+def add_up(ins, cuts, at=0):
     rows, model = sum(cuts), ins[0].shape[1]
     return pl.pallas_call(
-        functools.partial(add_kernel, len(ins)),
+        functools.partial(add_kernel, len(ins), at, rows),
         in_specs=[vmem()] * len(ins),
         out_specs=[vmem()] * len(cuts),
         out_shape=[jax.ShapeDtypeStruct((c, model), jnp.bfloat16) for c in cuts],
@@ -306,36 +307,46 @@
         ]
         return lax.ppermute(x, both, pairs)
 
+    places = [0] + list(range(1, ring_len, 2)) + list(range(2, ring_len, 2))[::-1]
+    onward = {p: places[(i + 1) % ring_len] for i, p in enumerate(places)}
+
+    def next_chip(f):
+        return 2 * onward[f // 2] + f % 2
+
     def ring(x):
-        return lax.ppermute(x, "fsdp", [(f, (f + 2) % fsdp) for f in range(fsdp)])
+        return lax.ppermute(x, "fsdp", [(f, next_chip(f)) for f in range(fsdp)])
+
+    def back(x):
+        return lax.ppermute(x, "fsdp", [(next_chip(f), f) for f in range(fsdp)])
 
     def pair(x):
         return lax.ppermute(x, "fsdp", [(f, f ^ 1) for f in range(fsdp)])
 
     *picked, spot = pick(tokens_in, out_grad, chosen, counts, gates, groups)
-    order = range(groups - 1, -1, -1)
-    near = {d: send(picked[d], d, lambda f: f) if d else picked[d] for d in order}
-    next_ = {d: send(picked[groups + d], d, lambda f: (f + 2) % fsdp) for d in order}
     rows = groups * slots
-    first = join([near[d] for d in range(groups)], [])
-    ours = join([next_[d] for d in range(groups)], [first])
+    near = [picked[0]] + [send(picked[d], d, lambda f: f) for d in range(1, groups)]
+    ours = join([send(picked[groups + d], d, next_chip) for d in range(groups)], [])
     results, arrived, before = [], [], []
     for k in range(1, ring_len):
         last = k == ring_len - 1
         ahead = None if last else ring(ours)
-        mixed = [first, ours, pair(first), pair(ours)] if k == 1 else [ours, pair(ours)]
+        mixed = [ours, first, pair(ours), pair(first)] if k == 2 else [ours, pair(ours)]
         results.append(block(mixed, w_in, w_out, slots, before))
         mine, theirs = results[-1][4:]
-        cuts = [slots] * groups if last else [rows]
-        pieces = add_up([mine, pair(theirs)] + arrived, [slots] * groups + cuts if k == 1 else cuts)
+        total = [mine, pair(theirs)]
+        pieces = add_up(total + arrived, [slots] * groups if last else [rows])
         if k == 1:
-            own = [pieces[0]] + [send(pieces[d], d, lambda f: f) for d in range(1, groups)]
-            pieces = pieces[groups:]
-        before, after = pieces[:1], [theirs] + arrived
+            returned = back(pieces[0])
+            first = join(near, [theirs])
+        elif not last:
+            arrived = [ring(pieces[0])]
+        if k == 2:
+            own = add_up(total + [returned], [slots] * groups, rows)
+        before = pieces[:1]
         if not last:
-            arrived = [ring(pieces[0])]
-            ours = join([ahead], after + (own[1:] if k == 2 else []))
-    parts = own + [send(pieces[d], d, lambda f: (f + 2) % fsdp) for d in range(groups)]
+            ours = join([ahead], [theirs] + ([first] if k == 1 else []))
+    parts = [own[0]] + [send(own[d], d, lambda f: f) for d in range(1, groups)]
+    parts += [send(pieces[d], d, next_chip) for d in range(groups)]
 
     x_ts, act_ts, hgrads, gs = list(zip(*results))[:4]
     grad_w_out = outer(act_ts, gs, [], "grad_w_out")

time: 92.5 us -> 86.3 us (0.933)
  waiting for transfers between devices: 31.2 us -> 23.9 us
  starting transfers between devices: 25.4 us -> 27.4 us
    ppermute x4, waiting for transfers between devices: 19.1 us -> 11.3 us  [the longest x3 9.57 us: ring(): return lax.ppermute(x, 'fsdp', [(f, next_chip(f)) for f in range(fsdp)])]
    ppermute x4, starting transfers between devices: 0.36 us -> 4.36 us  [the longest x3 2.62 us: ring(): return lax.ppermute(x, 'fsdp', [(f, next_chip(f)) for f in range(fsdp)])]
    ppermute x14, waiting for transfers between devices: 8.22 us -> 11.1 us  [send(): return lax.ppermute(x, both, pairs)]
    ppermute x7, waiting for transfers between devices: 3.93 us -> 1.48 us  [pair(): return lax.ppermute(x, 'fsdp', [(f, f ^ 1) for f in range(fsdp)])]
    ppermute x14, starting transfers between devices: 23.4 us -> 21.8 us  [send(): return lax.ppermute(x, both, pairs)]
  transfers between devices with their start and end apart: 25 -> 25, of which waited for: 11 -> 10; matrix products, arithmetic and copies ran while one was open for 0% -> 0% of each run, Pallas kernels for 24% -> 25%
where the time goes in v4:
time: 86.3 us; the launch traced here: 86.1 us
  Pallas kernels  29.4 us (34%)
  starting transfers between devices  27.4 us (32%)
  waiting for transfers between devices  23.9 us (28%)
  local copies, waits for them, and re-layouts  4.39 us (5%)
  between operations  1.04 us (1%)
    ppermute x14, starting transfers between devices, send(): return lax.ppermute(x, both, pairs)  21.8 us
    pallas_call x3, Pallas kernels, block(): pl.pallas_call(functools.partial(block_kernel, slots, min(256, units), le...  13.5 us
    ppermute x14, waiting for transfers between devices, send(): return lax.ppermute(x, both, pairs)  11.1 us
    ppermute x3, waiting for transfers between devices, ring(): return lax.ppermute(x, 'fsdp', [(f, next_chip(f)) for f in range(fsdp)])  9.57 us
    pallas_call x2, Pallas kernels, outer(): pl.pallas_call(functools.partial(outer_kernel, n, tiles), in_specs=[vmem(...  8.15 us
    pallas_call x1, Pallas kernels, pick(): pl.pallas_call(functools.partial(pick_kernel, groups, slots, tiles), in_s...  4.9 us
    unnamed x12, local copies, waits for them, and re-layouts  4.39 us
    ppermute x3, starting transfers between devices, ring(): return lax.ppermute(x, 'fsdp', [(f, next_chip(f)) for f in range(fsdp)])  2.62 us
  transfers between devices with their start and end apart: 25, of which 10 were waited for; matrix products, arithmetic and copies ran while one was open for 0% of the time, Pallas kernels for 25%

profile of v4, /device:TPU:0, one launch (start us, length us, event | category | flops | bytes accessed | tf_op | source)
XLA Modules:
  0.0 86.1 jit_solution(17597611270957530938)
XLA Ops:
  0.6 4.9 %pick.1 = (bf16[32,2048]{1,0:T(8,128)(2,1)}, bf16[32,2048]{1,0:T(8,128)(2,1)}, bf16[32,2048]{1,0:T(8,128)(2,1)}, bf16[32,2048]{1,0:T(8,128)(2,1)}, bf16[32,2048]...) custom-call(s32[1,4,16]{2,1,0:T(4,128)} %chosen_in.1, ...), custom_call_target="tpu_custom_call" | custom-call | flops 536870912 | bytes 8388608 | tf_op jit(solution)/shard_map/pick/pallas_call | solution.py:102
  5.5 3.1 %collective-permute-start = (bf16[32,2048]{1,0:T(8,128)(2,1)}, bf16[32,2048]{1,0:T(8,128)(2,1)S(1)}, u32[]{:S(2)}, u32[]{:S(2)}) collective-permute-start(bf16[32,2048]{1,0:T(8,128)(2,1)} %get-tuple-element.39), channel_id=1, source_target_pairs={{0,2},{1,3},{2,6},{3,7},{4,0},{5,1},{6,4},{7,5},{8,10},{9,11},{10,... | collective-permute-start | bytes 393224 | tf_op jit(solution)/shard_map/ppermute | solution.py:308
  8.6 3.5 %collective-permute-start.1 = (bf16[32,2048]{1,0:T(8,128)(2,1)}, bf16[32,2048]{1,0:T(8,128)(2,1)S(1)}, u32[]{:S(2)}, u32[]{:S(2)}) collective-permute-start(bf16[32,2048]{1,0:T(8,128)(2,1)} %get-tuple-element.40), channel_id=1, source_target_pairs={{0,10},{1,11},{2,14},{3,15},{4,8},{5,9},{6,12},{7,13},{8,2},{9,3},... | collective-permute-start | bytes 393224 | tf_op jit(solution)/shard_map/ppermute | solution.py:308
  12.1 1.4 %collective-permute-start.2 = (bf16[32,2048]{1,0:T(8,128)(2,1)}, bf16[32,2048]{1,0:T(8,128)(2,1)S(1)}, u32[]{:S(2)}, u32[]{:S(2)}) collective-permute-start(bf16[32,2048]{1,0:T(8,128)(2,1)} %get-tuple-element.41), channel_id=1, source_target_pairs={{0,18},{1,19},{2,22},{3,23},{4,16},{5,17},{6,20},{7,21},{8,26},{9,... | collective-permute-start | bytes 393224 | tf_op jit(solution)/shard_map/ppermute | solution.py:308
  13.5 0.0 collective-permute-start.3
  13.5 0.3 collective-permute-done.refs_0_
  13.8 4.3 %collective-permute-done.1.refs_1_ = bf16[32,2048]{1,0:T(8,128)(2,1)S(1)} collective-permute-done((bf16[32,2048]{1,0:T(8,128)(2,1)}, bf16[32,2048]{1,0:T(8,128)(2,1)S(1)}, u32[]{:S(2)}, u32[]{:S(2)}) %collective-permute-start.1) | collective-permute-done | bytes 131104 | tf_op jit(solution)/shard_map/ppermute | solution.py:308
  18.1 2.7 %collective-permute-done.2.refs_2_ = bf16[32,2048]{1,0:T(8,128)(2,1)S(1)} collective-permute-done((bf16[32,2048]{1,0:T(8,128)(2,1)}, bf16[32,2048]{1,0:T(8,128)(2,1)S(1)}, u32[]{:S(2)}, u32[]{:S(2)}) %collective-permute-start.2) | collective-permute-done | bytes 131104 | tf_op jit(solution)/shard_map/ppermute | solution.py:308
  20.8 2.9 %collective-permute-done.3.refs_3_ = bf16[32,2048]{1,0:T(8,128)(2,1)S(1)} collective-permute-done((bf16[32,2048]{1,0:T(8,128)(2,1)}, bf16[32,2048]{1,0:T(8,128)(2,1)S(1)}, u32[]{:S(2)}, u32[]{:S(2)}) %collective-permute-start.3) | collective-permute-done | bytes 131104 | tf_op jit(solution)/shard_map/ppermute | solution.py:308
  23.7 0.1 collective-permute-start.5
  23.8 0.7 collective-permute-start.4
  24.6 0.9 %collective-permute-start.6 = (bf16[32,2048]{1,0:T(8,128)(2,1)}, bf16[32,2048]{1,0:T(8,128)(2,1)S(1)}, u32[]{:S(2)}, u32[]{:S(2)}) collective-permute-start(bf16[32,2048]{1,0:T(8,128)(2,1)} %get-tuple-element.45), channel_id=1, source_target_pairs={{0,8},{1,9},{2,10},{3,11},{4,12},{5,13},{6,14},{7,15},{8,0},{9,1},... | collective-permute-start | bytes 393224 | tf_op jit(solution)/shard_map/ppermute | solution.py:308
  25.5 0.5 collective-permute-start.7
  26.0 2.0 %collective-permute-start.8 = (bf16[32,2048]{1,0:T(8,128)(2,1)}, bf16[32,2048]{1,0:T(8,128)(2,1)S(1)}, u32[]{:S(2)}, u32[]{:S(2)}) collective-permute-start(bf16[32,2048]{1,0:T(8,128)(2,1)} %get-tuple-element.47), channel_id=1, source_target_pairs={{0,24},{1,25},{2,26},{3,27},{4,28},{5,29},{6,30},{7,31},{8,16},{9,... | collective-permute-start | bytes 393224 | tf_op jit(solution)/shard_map/ppermute | solution.py:308
  28.1 0.0 collective-permute-done.5.refs_1_
  28.1 2.2 %copy-done = bf16[1,2048,1024]{2,1,0:T(8,128)(2,1)S(1)} copy-done((bf16[1,2048,1024]{2,1,0:T(8,128)(2,1)S(1)}, bf16[1,2048,1024]{2,1,0:T(8,128)(2,1)}, u32[]{:S(2)}) %copy-start) | copy-done | bytes 4194328
  30.2 2.2 %copy-done.2 = bf16[1,1024,2048]{2,1,0:T(8,128)(2,1)S(1)} copy-done((bf16[1,1024,2048]{2,1,0:T(8,128)(2,1)S(1)}, bf16[1,1024,2048]{2,1,0:T(8,128)(2,1)}, u32[]{:S(2)}) %copy-start.2) | copy-done | bytes 4194328
  32.4 4.1 %block.3 = (bf16[2048,128]{1,0:T(8,128)(2,1)S(1)}, bf16[1024,128]{1,0:T(8,128)(2,1)S(1)}, bf16[128,1024]{1,0:T(8,128)(2,1)S(1)}, bf16[128,2048]{1,0:T(8,128)(2,1...) custom-call(bf16[128,2048]{1,0:T(8,128)(2,1)S(1)} %join.4.refs_0_, ...), custom_call_target="tpu_custom_call" | custom-call | flops 1610612736 | bytes 8388608 | tf_op jit(solution)/shard_map/block/pallas_call | solution.py:187
  36.5 0.0 copy-start.1
  36.5 0.0 collective-permute-done.6.refs_1_
  36.6 0.0 collective-permute-done.7.refs_2_
  36.6 0.0 collective-permute-done.8.refs_3_
  36.6 0.0 copy-done.5
  36.6 2.4 %collective-permute-done.4.refs_0_ = bf16[128,2048]{1,0:T(8,128)(2,1)S(1)} collective-permute-done((bf16[128,2048]{1,0:T(8,128)(2,1)S(1)}, bf16[128,2048]{1,0:T(8,128)(2,1)S(1)}, u32[]{:S(2)}, u32[]{:S(2)}) %collective-permute-start.4) | collective-permute-done | bytes 524320 | tf_op jit(solution)/shard_map/ppermute | solution.py:317
  39.1 0.1 collective-permute-start.9
  39.2 0.5 collective-permute-start.10
  39.7 0.1 collective-permute-start.11
  39.7 1.1 %collective-permute-start.17 = (bf16[128,2048]{1,0:T(8,128)(2,1)S(1)}, bf16[128,2048]{1,0:T(8,128)(2,1)S(1)}, u32[]{:S(2)}, u32[]{:S(2)}) collective-permute-start(bf16[128,2048]{1,0:T(8,128)(2,1)S(1)} %join.6.refs_0_), channel_id=1, source_target_pairs={{0,2},{1,3},{2,6},{3,7},{4,0},{5,1},{6,4},{7,5},{8,10},{9,11},{10,... | collective-permute-start | bytes 1572872 | tf_op jit(solution)/shard_map/ppermute | solution.py:317
  40.8 1.4 %collective-permute-done.11.refs_1_ = bf16[64,2048]{1,0:T(8,128)(2,1)S(1)} collective-permute-done((bf16[64,2048]{1,0:T(8,128)(2,1)S(1)}, bf16[64,2048]{1,0:T(8,128)(2,1)S(1)}, u32[]{:S(2)}, u32[]{:S(2)}) %collective-permute-start.11) | collective-permute-done | bytes 262176 | tf_op jit(solution)/shard_map/ppermute | solution.py:323
  42.2 0.0 collective-permute-done.9.refs_2_
  42.2 0.0 collective-permute-done.10.refs_3_
  42.3 0.0 copy-done.3
  42.3 5.3 %block.4 = (bf16[2048,256]{1,0:T(8,128)(2,1)S(1)}, bf16[1024,256]{1,0:T(8,128)(2,1)S(1)}, bf16[256,1024]{1,0:T(8,128)(2,1)S(1)}, bf16[256,2048]{1,0:T(8,128)(2,1...) custom-call(bf16[128,2048]{1,0:T(8,128)(2,1)S(1)} %join.6.refs_0_, ...), custom_call_target="tpu_custom_call" | custom-call | flops 3221225472 | bytes 8388608 | tf_op jit(solution)/shard_map/block/pallas_call | solution.py:187
  47.5 0.2 collective-permute-start.12
  47.7 7.2 %collective-permute-done.17.refs_0_ = bf16[128,2048]{1,0:T(8,128)(2,1)S(1)} collective-permute-done((bf16[128,2048]{1,0:T(8,128)(2,1)S(1)}, bf16[128,2048]{1,0:T(8,128)(2,1)S(1)}, u32[]{:S(2)}, u32[]{:S(2)}) %collective-permute-start.17) | collective-permute-done | bytes 524320 | tf_op jit(solution)/shard_map/ppermute | solution.py:317
  54.9 0.1 collective-permute-start.18
  55.0 1.7 %collective-permute-start.13 = (bf16[64,2048]{1,0:T(8,128)(2,1)S(1)}, bf16[64,2048]{1,0:T(8,128)(2,1)S(1)}, u32[]{:S(2)}, u32[]{:S(2)}) collective-permute-start(bf16[64,2048]{1,0:T(8,128)(2,1)S(1)} %add_up.4.refs_6_), channel_id=1, source_target_pairs={{2,0},{3,1},{6,2},{7,3},{0,4},{1,5},{4,6},{5,7},{10,8},{11,9},{14,... | collective-permute-start | bytes 786440 | tf_op jit(solution)/shard_map/ppermute | solution.py:320
  56.8 0.0 collective-permute-done.12.refs_1_
  56.8 0.1 collective-permute-done.18.refs_1_
  56.9 4.1 %block.5 = (bf16[2048,128]{1,0:T(8,128)(2,1)S(1)}, bf16[1024,128]{1,0:T(8,128)(2,1)S(1)}, bf16[128,1024]{1,0:T(8,128)(2,1)S(1)}, bf16[128,2048]{1,0:T(8,128)(2,1...) custom-call(bf16[128,2048]{1,0:T(8,128)(2,1)S(1)} %join.7.refs_0_, ...), custom_call_target="tpu_custom_call" | custom-call | flops 1610612736 | bytes 8388608 | tf_op jit(solution)/shard_map/block/pallas_call | solution.py:187
  61.0 0.2 collective-permute-start.19
  61.2 0.8 collective-permute-start.20
  62.0 1.7 %collective-permute-done.13.refs_2_ = bf16[64,2048]{1,0:T(8,128)(2,1)S(1)} collective-permute-done((bf16[64,2048]{1,0:T(8,128)(2,1)S(1)}, bf16[64,2048]{1,0:T(8,128)(2,1)S(1)}, u32[]{:S(2)}, u32[]{:S(2)}) %collective-permute-start.13) | collective-permute-done | bytes 262176 | tf_op jit(solution)/shard_map/ppermute | solution.py:320
  63.7 0.1 add_up.5
  63.8 0.7 collective-permute-start.14
  64.6 0.4 collective-permute-start.15
  65.0 2.4 %collective-permute-start.16 = (bf16[16,2048]{1,0:T(8,128)(2,1)S(1)}, bf16[16,2048]{1,0:T(8,128)(2,1)S(1)}, u32[]{:S(2)}, u32[]{:S(2)}) collective-permute-start(bf16[16,2048]{1,0:T(8,128)(2,1)S(1)} %get-tuple-element.54), channel_id=1, source_target_pairs={{0,24},{1,25},{2,26},{3,27},{4,28},{5,29},{6,30},{7,31},{8,16},{9,... | collective-permute-start | bytes 196616 | tf_op jit(solution)/shard_map/ppermute | solution.py:308
  67.4 4.1 %grad_w_out.1 = f32[1,1024,2048]{2,1,0:T(8,128)} custom-call(bf16[1024,128]{1,0:T(8,128)(2,1)S(1)} %get-tuple-element.67.refs_0_, bf16[1024,256]{1,0:T(8,128)(2,1)S(1)} %get-tuple-element.68.refs_1_, bf16[1024,128]{1,0:T(8,128)(2,1)S(1)} %get-tuple-element.69.refs_2_, bf16[128,2048]{1,0:T(8,128)(2,1)S(1)} %get-tuple-element.70.refs_3_, ...), custom_call_target="tpu_custom_call" | custom-call | flops 2147483648 | bytes 8388608 | tf_op jit(solution)/shard_map/grad_w_out/pallas_call | solution.py:230
  71.5 0.0 collective-permute-done.19.refs_1_
  71.5 0.0 collective-permute-done.20.refs_2_
  71.5 0.1 add_up.7
  71.6 2.5 %collective-permute-start.21 = (bf16[16,2048]{1,0:T(8,128)(2,1)S(1)}, bf16[16,2048]{1,0:T(8,128)(2,1)S(1)}, u32[]{:S(2)}, u32[]{:S(2)}) collective-permute-start(bf16[16,2048]{1,0:T(8,128)(2,1)S(1)} %get-tuple-element.57.refs_6_), channel_id=1, source_target_pairs={{0,2},{1,3},{2,6},{3,7},{4,0},{5,1},{6,4},{7,5},{8,10},{9,11},{10,... | collective-permute-start | bytes 196616 | tf_op jit(solution)/shard_map/ppermute | solution.py:308
  74.1 1.7 %collective-permute-start.22 = (bf16[16,2048]{1,0:T(8,128)(2,1)S(1)}, bf16[16,2048]{1,0:T(8,128)(2,1)S(1)}, u32[]{:S(2)}, u32[]{:S(2)}) collective-permute-start(bf16[16,2048]{1,0:T(8,128)(2,1)S(1)} %get-tuple-element.58), channel_id=1, source_target_pairs={{0,10},{1,11},{2,14},{3,15},{4,8},{5,9},{6,12},{7,13},{8,2},{9,3},... | collective-permute-start | bytes 196616 | tf_op jit(solution)/shard_map/ppermute | solution.py:308
  75.8 0.0 collective-permute-done.14.rest_1_
  75.8 0.4 collective-permute-start.23
  76.2 0.0 collective-permute-done.15.rest_2_
  76.2 2.2 %collective-permute-start.24 = (bf16[16,2048]{1,0:T(8,128)(2,1)S(1)}, bf16[16,2048]{1,0:T(8,128)(2,1)S(1)}, u32[]{:S(2)}, u32[]{:S(2)}) collective-permute-start(bf16[16,2048]{1,0:T(8,128)(2,1)S(1)} %get-tuple-element.60), channel_id=1, source_target_pairs={{0,26},{1,27},{2,30},{3,31},{4,24},{5,25},{6,28},{7,29},{8,18},{9,... | collective-permute-start | bytes 196616 | tf_op jit(solution)/shard_map/ppermute | solution.py:308
  78.4 4.1 %grad_w_in.1 = f32[1,2048,1024]{2,1,0:T(8,128)} custom-call(bf16[2048,128]{1,0:T(8,128)(2,1)S(1)} %get-tuple-element.61.refs_0_, bf16[2048,256]{1,0:T(8,128)(2,1)S(1)} %get-tuple-element.62.refs_1_, bf16[2048,128]{1,0:T(8,128)(2,1)S(1)} %get-tuple-element.63.refs_2_, bf16[128,1024]{1,0:T(8,128)(2,1)S(1)} %get-tuple-element.64.refs_3_, ...), custom_call_target="tpu_custom_call" | custom-call | flops 2147483648 | bytes 8388608 | tf_op jit(solution)/shard_map/grad_w_in/pallas_call | solution.py:230
  82.5 0.0 collective-permute-done.16.rest_3_
  82.5 0.0 collective-permute-done.21.rest_4_
  82.5 0.0 collective-permute-done.22.rest_5_
  82.5 0.0 collective-permute-done.23.rest_6_
  82.5 0.9 %collective-permute-done.24.rest_7_ = bf16[16,2048]{1,0:T(8,128)(2,1)S(1)} collective-permute-done((bf16[16,2048]{1,0:T(8,128)(2,1)S(1)}, bf16[16,2048]{1,0:T(8,128)(2,1)S(1)}, u32[]{:S(2)}, u32[]{:S(2)}) %collective-permute-start.24) | collective-permute-done | bytes 65568 | tf_op jit(solution)/shard_map/ppermute | solution.py:308
  83.5 2.5 %place.1 = bf16[1024,2048]{1,0:T(8,128)(2,1)} custom-call(bf16[1024,128]{1,0:T(8,128)(2,1)S(1)} %copy-done.4, bf16[16,2048]{1,0:T(8,128)(2,1)S(1)} %get-tuple-element.51.rest_0_, bf16[16,2048]{1,0:T(8,128)(2,1)S(1)} %collective-permute-done.14.rest_1_, bf16[16,2048]{1,0:T(8,128)(2,1)S(1)} %collective-permute-done.15.rest_2_, ...), custom_call_target="tpu_custom_call" | custom-call | flops 536870912 | bytes 4194304 | tf_op jit(solution)/shard_map/place/pallas_call | solution.py:286
  (13 shorter events, 0.2 us)
Async XLA Ops:
  5.5 8.3 %collective-permute-start = (bf16[32,2048]{1,0:T(8,128)(2,1)}, bf16[32,2048]{1,0:T(8,128)(2,1)S(1)}, u32[]{:S(2)}, u32[]{:S(2)}) collective-permute-start(bf16[32,2048]{1,0:T(8,128)(2,1)} %get-tuple-element.39), channel_id=1, source_target_pairs={{0,2},{1,3},{2,6},{3,7},{4,0},{5,1},{6,4},{7,5},{8,10},{9,11},{10,... | collective-permute-start | bytes 393224 | tf_op jit(solution)/shard_map/ppermute | solution.py:308
  8.6 9.5 %collective-permute-start.1 = (bf16[32,2048]{1,0:T(8,128)(2,1)}, bf16[32,2048]{1,0:T(8,128)(2,1)S(1)}, u32[]{:S(2)}, u32[]{:S(2)}) collective-permute-start(bf16[32,2048]{1,0:T(8,128)(2,1)} %get-tuple-element.40), channel_id=1, source_target_pairs={{0,10},{1,11},{2,14},{3,15},{4,8},{5,9},{6,12},{7,13},{8,2},{9,3},... | collective-permute-start | bytes 393224 | tf_op jit(solution)/shard_map/ppermute | solution.py:308
  12.1 8.7 %collective-permute-start.2 = (bf16[32,2048]{1,0:T(8,128)(2,1)}, bf16[32,2048]{1,0:T(8,128)(2,1)S(1)}, u32[]{:S(2)}, u32[]{:S(2)}) collective-permute-start(bf16[32,2048]{1,0:T(8,128)(2,1)} %get-tuple-element.41), channel_id=1, source_target_pairs={{0,18},{1,19},{2,22},{3,23},{4,16},{5,17},{6,20},{7,21},{8,26},{9,... | collective-permute-start | bytes 393224 | tf_op jit(solution)/shard_map/ppermute | solution.py:308
  13.5 10.2 %collective-permute-start.3 = (bf16[32,2048]{1,0:T(8,128)(2,1)}, bf16[32,2048]{1,0:T(8,128)(2,1)S(1)}, u32[]{:S(2)}, u32[]{:S(2)}) collective-permute-start(bf16[32,2048]{1,0:T(8,128)(2,1)} %get-tuple-element.42), channel_id=1, source_target_pairs={{0,26},{1,27},{2,30},{3,31},{4,24},{5,25},{6,28},{7,29},{8,18},{9,... | collective-permute-start | bytes 393224 | tf_op jit(solution)/shard_map/ppermute | solution.py:308
  23.7 4.3 %collective-permute-start.5 = (bf16[128,2048]{1,0:T(8,128)(2,1)S(1)}, bf16[128,2048]{1,0:T(8,128)(2,1)S(1)}, u32[]{:S(2)}, u32[]{:S(2)}) collective-permute-start(bf16[128,2048]{1,0:T(8,128)(2,1)S(1)} %join.4.refs_0_), channel_id=1, source_target_pairs={{0,1},{1,0},{2,3},{3,2},{4,5},{5,4},{6,7},{7,6},{8,9},{9,8},{10,11... | collective-permute-start | bytes 1572872 | tf_op jit(solution)/shard_map/ppermute | solution.py:323
  23.8 15.2 %collective-permute-start.4 = (bf16[128,2048]{1,0:T(8,128)(2,1)S(1)}, bf16[128,2048]{1,0:T(8,128)(2,1)S(1)}, u32[]{:S(2)}, u32[]{:S(2)}) collective-permute-start(bf16[128,2048]{1,0:T(8,128)(2,1)S(1)} %join.4.refs_0_), channel_id=1, source_target_pairs={{0,2},{1,3},{2,6},{3,7},{4,0},{5,1},{6,4},{7,5},{8,10},{9,11},{10,... | collective-permute-start | bytes 1572872 | tf_op jit(solution)/shard_map/ppermute | solution.py:317
  24.6 12.0 %collective-permute-start.6 = (bf16[32,2048]{1,0:T(8,128)(2,1)}, bf16[32,2048]{1,0:T(8,128)(2,1)S(1)}, u32[]{:S(2)}, u32[]{:S(2)}) collective-permute-start(bf16[32,2048]{1,0:T(8,128)(2,1)} %get-tuple-element.45), channel_id=1, source_target_pairs={{0,8},{1,9},{2,10},{3,11},{4,12},{5,13},{6,14},{7,15},{8,0},{9,1},... | collective-permute-start | bytes 393224 | tf_op jit(solution)/shard_map/ppermute | solution.py:308
  25.5 11.1 %collective-permute-start.7 = (bf16[32,2048]{1,0:T(8,128)(2,1)}, bf16[32,2048]{1,0:T(8,128)(2,1)S(1)}, u32[]{:S(2)}, u32[]{:S(2)}) collective-permute-start(bf16[32,2048]{1,0:T(8,128)(2,1)} %get-tuple-element.46), channel_id=1, source_target_pairs={{0,16},{1,17},{2,18},{3,19},{4,20},{5,21},{6,22},{7,23},{8,24},{9,... | collective-permute-start | bytes 393224 | tf_op jit(solution)/shard_map/ppermute | solution.py:308
  26.0 10.6 %collective-permute-start.8 = (bf16[32,2048]{1,0:T(8,128)(2,1)}, bf16[32,2048]{1,0:T(8,128)(2,1)S(1)}, u32[]{:S(2)}, u32[]{:S(2)}) collective-permute-start(bf16[32,2048]{1,0:T(8,128)(2,1)} %get-tuple-element.47), channel_id=1, source_target_pairs={{0,24},{1,25},{2,26},{3,27},{4,28},{5,29},{6,30},{7,31},{8,16},{9,... | collective-permute-start | bytes 393224 | tf_op jit(solution)/shard_map/ppermute | solution.py:308
  28.1 2.2 %copy-start = (bf16[1,2048,1024]{2,1,0:T(8,128)(2,1)S(1)}, bf16[1,2048,1024]{2,1,0:T(8,128)(2,1)}, u32[]{:S(2)}) copy-start(bf16[1,2048,1024]{2,1,0:T(8,128)(2,1)} %refs_2_.3) | copy-start | bytes 12582916
  30.2 2.2 %copy-start.2 = (bf16[1,1024,2048]{2,1,0:T(8,128)(2,1)S(1)}, bf16[1,1024,2048]{2,1,0:T(8,128)(2,1)}, u32[]{:S(2)}) copy-start(bf16[1,1024,2048]{2,1,0:T(8,128)(2,1)} %refs_3_.3) | copy-start | bytes 12582916
  32.4 4.2 %copy-start.5 = (bf16[32,2048]{1,0:T(8,128)(2,1)S(1)}, bf16[32,2048]{1,0:T(8,128)(2,1)}, u32[]{:S(2)}) copy-start(bf16[32,2048]{1,0:T(8,128)(2,1)} %get-tuple-element.44.refs_0_) | copy-start | bytes 393220
  32.4 9.8 %copy-start.3 = (bf16[1,1024,2048]{2,1,0:T(8,128)(2,1)S(1)}, bf16[1,1024,2048]{2,1,0:T(8,128)(2,1)}, u32[]{:S(2)}) copy-start(bf16[1,1024,2048]{2,1,0:T(8,128)(2,1)} %refs_3_.3) | copy-start | bytes 12582916
  36.5 5.7 %copy-start.1 = (bf16[1,2048,1024]{2,1,0:T(8,128)(2,1)S(1)}, bf16[1,2048,1024]{2,1,0:T(8,128)(2,1)}, u32[]{:S(2)}) copy-start(bf16[1,2048,1024]{2,1,0:T(8,128)(2,1)} %refs_2_.3) | copy-start | bytes 12582916
  39.1 3.2 %collective-permute-start.9 = (bf16[128,2048]{1,0:T(8,128)(2,1)S(1)}, bf16[128,2048]{1,0:T(8,128)(2,1)S(1)}, u32[]{:S(2)}, u32[]{:S(2)}) collective-permute-start(bf16[128,2048]{1,0:T(8,128)(2,1)S(1)} %join.6.refs_0_), channel_id=1, source_target_pairs={{0,1},{1,0},{2,3},{3,2},{4,5},{5,4},{6,7},{7,6},{8,9},{9,8},{10,11... | collective-permute-start | bytes 1572872 | tf_op jit(solution)/shard_map/ppermute | solution.py:323
  39.2 3.1 %collective-permute-start.10 = (bf16[128,2048]{1,0:T(8,128)(2,1)S(1)}, bf16[128,2048]{1,0:T(8,128)(2,1)S(1)}, u32[]{:S(2)}, u32[]{:S(2)}) collective-permute-start(bf16[128,2048]{1,0:T(8,128)(2,1)S(1)} %join.5.refs_2_.refs_1_), channel_id=1, source_target_pairs={{0,1},{1,0},{2,3},{3,2},{4,5},{5,4},{6,7},{7,6},{8,9},{9,8},{10,11... | collective-permute-start | bytes 1572872 | tf_op jit(solution)/shard_map/ppermute | solution.py:323
  39.7 2.5 %collective-permute-start.11 = (bf16[64,2048]{1,0:T(8,128)(2,1)S(1)}, bf16[64,2048]{1,0:T(8,128)(2,1)S(1)}, u32[]{:S(2)}, u32[]{:S(2)}) collective-permute-start(bf16[64,2048]{1,0:T(8,128)(2,1)S(1)} %get-tuple-element.43.refs_4_.refs_1_), channel_id=1, source_target_pairs={{0,1},{1,0},{2,3},{3,2},{4,5},{5,4},{6,7},{7,6},{8,9},{9,8},{10,11... | collective-permute-start | bytes 786440 | tf_op jit(solution)/shard_map/ppermute | solution.py:323
  39.7 15.2 %collective-permute-start.17 = (bf16[128,2048]{1,0:T(8,128)(2,1)S(1)}, bf16[128,2048]{1,0:T(8,128)(2,1)S(1)}, u32[]{:S(2)}, u32[]{:S(2)}) collective-permute-start(bf16[128,2048]{1,0:T(8,128)(2,1)S(1)} %join.6.refs_0_), channel_id=1, source_target_pairs={{0,2},{1,3},{2,6},{3,7},{4,0},{5,1},{6,4},{7,5},{8,10},{9,11},{10,... | collective-permute-start | bytes 1572872 | tf_op jit(solution)/shard_map/ppermute | solution.py:317
  47.5 9.2 %collective-permute-start.12 = (bf16[128,2048]{1,0:T(8,128)(2,1)S(1)}, bf16[128,2048]{1,0:T(8,128)(2,1)S(1)}, u32[]{:S(2)}, u32[]{:S(2)}) collective-permute-start(bf16[128,2048]{1,0:T(8,128)(2,1)S(1)} %get-tuple-element.50.refs_1_), channel_id=1, source_target_pairs={{0,1},{1,0},{2,3},{3,2},{4,5},{5,4},{6,7},{7,6},{8,9},{9,8},{10,11... | collective-permute-start | bytes 1572872 | tf_op jit(solution)/shard_map/ppermute | solution.py:323
  54.9 2.0 %collective-permute-start.18 = (bf16[128,2048]{1,0:T(8,128)(2,1)S(1)}, bf16[128,2048]{1,0:T(8,128)(2,1)S(1)}, u32[]{:S(2)}, u32[]{:S(2)}) collective-permute-start(bf16[128,2048]{1,0:T(8,128)(2,1)S(1)} %join.7.refs_0_), channel_id=1, source_target_pairs={{0,1},{1,0},{2,3},{3,2},{4,5},{5,4},{6,7},{7,6},{8,9},{9,8},{10,11... | collective-permute-start | bytes 1572872 | tf_op jit(solution)/shard_map/ppermute | solution.py:323
  55.0 8.7 %collective-permute-start.13 = (bf16[64,2048]{1,0:T(8,128)(2,1)S(1)}, bf16[64,2048]{1,0:T(8,128)(2,1)S(1)}, u32[]{:S(2)}, u32[]{:S(2)}) collective-permute-start(bf16[64,2048]{1,0:T(8,128)(2,1)S(1)} %add_up.4.refs_6_), channel_id=1, source_target_pairs={{2,0},{3,1},{6,2},{7,3},{0,4},{1,5},{4,6},{5,7},{10,8},{11,9},{14,... | collective-permute-start | bytes 786440 | tf_op jit(solution)/shard_map/ppermute | solution.py:320
  61.0 10.4 %collective-permute-start.19 = (bf16[64,2048]{1,0:T(8,128)(2,1)S(1)}, bf16[64,2048]{1,0:T(8,128)(2,1)S(1)}, u32[]{:S(2)}, u32[]{:S(2)}) collective-permute-start(bf16[64,2048]{1,0:T(8,128)(2,1)S(1)} %get-tuple-element.56), channel_id=1, source_target_pairs={{0,1},{1,0},{2,3},{3,2},{4,5},{5,4},{6,7},{7,6},{8,9},{9,8},{10,11... | collective-permute-start | bytes 786440 | tf_op jit(solution)/shard_map/ppermute | solution.py:323
  61.2 10.2 %collective-permute-start.20 = (bf16[64,2048]{1,0:T(8,128)(2,1)S(1)}, bf16[64,2048]{1,0:T(8,128)(2,1)S(1)}, u32[]{:S(2)}, u32[]{:S(2)}) collective-permute-start(bf16[64,2048]{1,0:T(8,128)(2,1)S(1)} %add_up.6.refs_4_), channel_id=1, source_target_pairs={{0,2},{1,3},{2,6},{3,7},{4,0},{5,1},{6,4},{7,5},{8,10},{9,11},{10,... | collective-permute-start | bytes 786440 | tf_op jit(solution)/shard_map/ppermute | solution.py:317
  63.8 12.0 %collective-permute-start.14 = (bf16[16,2048]{1,0:T(8,128)(2,1)S(1)}, bf16[16,2048]{1,0:T(8,128)(2,1)S(1)}, u32[]{:S(2)}, u32[]{:S(2)}) collective-permute-start(bf16[16,2048]{1,0:T(8,128)(2,1)S(1)} %get-tuple-element.52), channel_id=1, source_target_pairs={{0,8},{1,9},{2,10},{3,11},{4,12},{5,13},{6,14},{7,15},{8,0},{9,1},... | collective-permute-start | bytes 196616 | tf_op jit(solution)/shard_map/ppermute | solution.py:308
  64.6 11.6 %collective-permute-start.15 = (bf16[16,2048]{1,0:T(8,128)(2,1)S(1)}, bf16[16,2048]{1,0:T(8,128)(2,1)S(1)}, u32[]{:S(2)}, u32[]{:S(2)}) collective-permute-start(bf16[16,2048]{1,0:T(8,128)(2,1)S(1)} %get-tuple-element.53), channel_id=1, source_target_pairs={{0,16},{1,17},{2,18},{3,19},{4,20},{5,21},{6,22},{7,23},{8,24},{9,... | collective-permute-start | bytes 196616 | tf_op jit(solution)/shard_map/ppermute | solution.py:308
  65.0 17.5 %collective-permute-start.16 = (bf16[16,2048]{1,0:T(8,128)(2,1)S(1)}, bf16[16,2048]{1,0:T(8,128)(2,1)S(1)}, u32[]{:S(2)}, u32[]{:S(2)}) collective-permute-start(bf16[16,2048]{1,0:T(8,128)(2,1)S(1)} %get-tuple-element.54), channel_id=1, source_target_pairs={{0,24},{1,25},{2,26},{3,27},{4,28},{5,29},{6,30},{7,31},{8,16},{9,... | collective-permute-start | bytes 196616 | tf_op jit(solution)/shard_map/ppermute | solution.py:308
  71.6 10.9 %collective-permute-start.21 = (bf16[16,2048]{1,0:T(8,128)(2,1)S(1)}, bf16[16,2048]{1,0:T(8,128)(2,1)S(1)}, u32[]{:S(2)}, u32[]{:S(2)}) collective-permute-start(bf16[16,2048]{1,0:T(8,128)(2,1)S(1)} %get-tuple-element.57.refs_6_), channel_id=1, source_target_pairs={{0,2},{1,3},{2,6},{3,7},{4,0},{5,1},{6,4},{7,5},{8,10},{9,11},{10,... | collective-permute-start | bytes 196616 | tf_op jit(solution)/shard_map/ppermute | solution.py:308
  74.1 8.4 %collective-permute-start.22 = (bf16[16,2048]{1,0:T(8,128)(2,1)S(1)}, bf16[16,2048]{1,0:T(8,128)(2,1)S(1)}, u32[]{:S(2)}, u32[]{:S(2)}) collective-permute-start(bf16[16,2048]{1,0:T(8,128)(2,1)S(1)} %get-tuple-element.58), channel_id=1, source_target_pairs={{0,10},{1,11},{2,14},{3,15},{4,8},{5,9},{6,12},{7,13},{8,2},{9,3},... | collective-permute-start | bytes 196616 | tf_op jit(solution)/shard_map/ppermute | solution.py:308
  75.8 6.7 %collective-permute-start.23 = (bf16[16,2048]{1,0:T(8,128)(2,1)S(1)}, bf16[16,2048]{1,0:T(8,128)(2,1)S(1)}, u32[]{:S(2)}, u32[]{:S(2)}) collective-permute-start(bf16[16,2048]{1,0:T(8,128)(2,1)S(1)} %get-tuple-element.59), channel_id=1, source_target_pairs={{0,18},{1,19},{2,22},{3,23},{4,16},{5,17},{6,20},{7,21},{8,26},{9,... | collective-permute-start | bytes 196616 | tf_op jit(solution)/shard_map/ppermute | solution.py:308
  76.2 7.3 %collective-permute-start.24 = (bf16[16,2048]{1,0:T(8,128)(2,1)S(1)}, bf16[16,2048]{1,0:T(8,128)(2,1)S(1)}, u32[]{:S(2)}, u32[]{:S(2)}) collective-permute-start(bf16[16,2048]{1,0:T(8,128)(2,1)S(1)} %get-tuple-element.60), channel_id=1, source_target_pairs={{0,26},{1,27},{2,30},{3,31},{4,24},{5,25},{6,28},{7,29},{8,18},{9,... | collective-permute-start | bytes 196616 | tf_op jit(solution)/shard_map/ppermute | solution.py:308
  78.4 5.1 %copy-start.4 = (bf16[1024,128]{1,0:T(8,128)(2,1)S(1)}, bf16[1024,128]{1,0:T(8,128)(2,1)}, u32[]{:S(2)}) copy-start(bf16[1024,128]{1,0:T(8,128)(2,1)} %get-tuple-element.38.spot) | copy-start | bytes 786436

commit v5 on v4

--- a/solution.py
+++ b/solution.py
@@ -151,7 +151,7 @@
 
 def block_kernel(slots, tile, n_in, *refs):
     ins, (w_in, w_out) = refs[:n_in], refs[n_in : n_in + 2]
-    x_t, act_t, hgrad, g_all, mine, theirs, x_all, g_t, total = refs[-9:]
+    x_all, act_t, hgrad, g_all, mine, theirs, g_t, total = refs[-8:]
     half = mine.shape[0]
     at = 0
     for ref in ins:
@@ -159,7 +159,6 @@
             x_all[at : at + slots] = ref[row : row + slots]
             g_all[at : at + slots] = ref[row + slots : row + 2 * slots]
             at += slots
-    x_t[...] = x_all[...].T
     g_t[...] = g_all[...].T
     for unit in range(0, w_in.shape[2], tile):
         some = slice(unit, unit + tile)
@@ -189,7 +188,7 @@
         in_specs=[vmem()] * (len(ins) + 2) + [anywhere()] * len(after),
         out_specs=[vmem()] * 6,
         out_shape=[
-            bf((model, rows)),
+            bf((rows, model)),
             bf((units, rows)),
             bf((rows, units)),
             bf((rows, model)),
@@ -197,25 +196,24 @@
             bf((half, model)),
         ],
         scratch_shapes=[
-            pltpu.VMEM((rows, model), jnp.bfloat16),
             pltpu.VMEM((model, rows), jnp.bfloat16),
             pltpu.VMEM((model, rows), jnp.float32),
         ],
         compiler_params=params(20 * 2**20),
-        cost_estimate=cost(6 * rows * model * units, 4 * model * units, rows * units),
+        cost_estimate=cost(3 * rows * model * units, 2 * model * units, rows * units),
         name="block",
     )(*ins, w_in, w_out, *after)
 
 
-def outer_kernel(n, tiles, *refs):
-    left_t, right = refs[:n], refs[n : 2 * n]
+def outer_kernel(n, tiles, turn, *refs):
+    left, right = refs[:n], refs[n : 2 * n]
     out, buf, sems = refs[-3:]
     b = jnp.concatenate([r[...] for r in right], axis=0)
     size = buf.shape[0] // tiles
     copies = []
     for i in range(tiles):
         some = slice(i * size, (i + 1) * size)
-        a = jnp.concatenate([r[some] for r in left_t], axis=1)
+        a = jnp.concatenate([r[:, some].T if turn else r[some] for r in left], axis=1)
         buf[some] = jnp.dot(a, b, preferred_element_type=jnp.float32)
         copies.append(pltpu.make_async_copy(buf.at[some], out.at[0, some], sems.at[i]))
         copies[-1].start()
@@ -223,12 +221,12 @@
         copy.wait()
 
 
-def outer(left_ts, rights, after, name):
-    n, m, k = len(rights), left_ts[0].shape[0], rights[0].shape[1]
+def outer(lefts, rights, after, turn, name):
+    n, m, k = len(rights), lefts[0].shape[1 if turn else 0], rights[0].shape[1]
     rows = sum(r.shape[0] for r in rights)
-    tiles = 4
-    return pl.pallas_call(
-        functools.partial(outer_kernel, n, tiles),
+    tiles = 8
+    return pl.pallas_call(
+        functools.partial(outer_kernel, n, tiles, turn),
         in_specs=[vmem()] * (2 * n) + [anywhere()] * len(after),
         out_specs=anywhere(),
         out_shape=jax.ShapeDtypeStruct((1, m, k), jnp.float32),
@@ -236,7 +234,7 @@
         compiler_params=params(20 * 2**20),
         cost_estimate=cost(2 * rows * m * k, 4 * m * k),
         name=name,
-    )(*left_ts, *rights, *after)
+    )(*lefts, *rights, *after)
 
 
 def add_kernel(n_in, at, rows, *refs):
@@ -282,7 +280,7 @@
 def place(parts, spot):
     model = parts[0].shape[1]
     length, rows = spot.shape
-    tiles = 4
+    tiles = 8
     return pl.pallas_call(
         functools.partial(place_kernel, tiles),
         in_specs=[vmem()] * (1 + len(parts)),
@@ -348,9 +346,9 @@
     parts = [own[0]] + [send(own[d], d, lambda f: f) for d in range(1, groups)]
     parts += [send(pieces[d], d, next_chip) for d in range(groups)]
 
-    x_ts, act_ts, hgrads, gs = list(zip(*results))[:4]
-    grad_w_out = outer(act_ts, gs, [], "grad_w_out")
-    grad_w_in = outer(x_ts, hgrads, pieces[:1], "grad_w_in")
+    xs, act_ts, hgrads, gs = list(zip(*results))[:4]
+    grad_w_out = outer(act_ts, gs, [], False, "grad_w_out")
+    grad_w_in = outer(xs, hgrads, pieces[:1], True, "grad_w_in")
     return place(parts, spot), grad_w_in, grad_w_out
 
 

time: 86.3 us -> 85.5 us (level)
  no operation moved by 1% of the time
where the time goes in v5:
time: 85.5 us; the launch traced here: 85.3 us
  Pallas kernels  28.9 us (34%)
  starting transfers between devices  27.3 us (32%)
  waiting for transfers between devices  23.6 us (28%)
  local copies, waits for them, and re-layouts  4.39 us (5%)
  between operations  1.04 us (1%)
    ppermute x14, starting transfers between devices, send(): return lax.ppermute(x, both, pairs)  21.8 us
    pallas_call x3, Pallas kernels, block(): pl.pallas_call(functools.partial(block_kernel, slots, min(256, units), le...  13.6 us
    ppermute x14, waiting for transfers between devices, send(): return lax.ppermute(x, both, pairs)  11.4 us
    ppermute x3, waiting for transfers between devices, ring(): return lax.ppermute(x, 'fsdp', [(f, next_chip(f)) for f in range(fsdp)])  8.92 us
    pallas_call x2, Pallas kernels, outer(): pl.pallas_call(functools.partial(outer_kernel, n, tiles, turn), in_specs=...  7.65 us
    pallas_call x1, Pallas kernels, pick(): pl.pallas_call(functools.partial(pick_kernel, groups, slots, tiles), in_s...  4.9 us
    unnamed x12, local copies, waits for them, and re-layouts  4.39 us
    ppermute x3, starting transfers between devices, ring(): return lax.ppermute(x, 'fsdp', [(f, next_chip(f)) for f in range(fsdp)])  2.64 us
  transfers between devices with their start and end apart: 25, of which 10 were waited for; matrix products, arithmetic and copies ran while one was open for 0% of the time, Pallas kernels for 25%

profile of v5, /device:TPU:0, one launch (start us, length us, event | category | flops | bytes accessed | tf_op | source)
XLA Modules:
  0.0 85.3 jit_solution(1705576230859904509)
XLA Ops:
  0.6 4.9 %pick.1 = (bf16[32,2048]{1,0:T(8,128)(2,1)}, bf16[32,2048]{1,0:T(8,128)(2,1)}, bf16[32,2048]{1,0:T(8,128)(2,1)}, bf16[32,2048]{1,0:T(8,128)(2,1)}, bf16[32,2048]...) custom-call(s32[1,4,16]{2,1,0:T(4,128)} %chosen_in.1, ...), custom_call_target="tpu_custom_call" | custom-call | flops 536870912 | bytes 8388608 | tf_op jit(solution)/shard_map/pick/pallas_call | solution.py:102
  5.5 3.1 %collective-permute-start = (bf16[32,2048]{1,0:T(8,128)(2,1)}, bf16[32,2048]{1,0:T(8,128)(2,1)S(1)}, u32[]{:S(2)}, u32[]{:S(2)}) collective-permute-start(bf16[32,2048]{1,0:T(8,128)(2,1)} %get-tuple-element.39), channel_id=1, source_target_pairs={{0,2},{1,3},{2,6},{3,7},{4,0},{5,1},{6,4},{7,5},{8,10},{9,11},{10,... | collective-permute-start | bytes 393224 | tf_op jit(solution)/shard_map/ppermute | solution.py:306
  8.6 3.5 %collective-permute-start.1 = (bf16[32,2048]{1,0:T(8,128)(2,1)}, bf16[32,2048]{1,0:T(8,128)(2,1)S(1)}, u32[]{:S(2)}, u32[]{:S(2)}) collective-permute-start(bf16[32,2048]{1,0:T(8,128)(2,1)} %get-tuple-element.40), channel_id=1, source_target_pairs={{0,10},{1,11},{2,14},{3,15},{4,8},{5,9},{6,12},{7,13},{8,2},{9,3},... | collective-permute-start | bytes 393224 | tf_op jit(solution)/shard_map/ppermute | solution.py:306
  12.1 1.4 %collective-permute-start.2 = (bf16[32,2048]{1,0:T(8,128)(2,1)}, bf16[32,2048]{1,0:T(8,128)(2,1)S(1)}, u32[]{:S(2)}, u32[]{:S(2)}) collective-permute-start(bf16[32,2048]{1,0:T(8,128)(2,1)} %get-tuple-element.41), channel_id=1, source_target_pairs={{0,18},{1,19},{2,22},{3,23},{4,16},{5,17},{6,20},{7,21},{8,26},{9,... | collective-permute-start | bytes 393224 | tf_op jit(solution)/shard_map/ppermute | solution.py:306
  13.5 0.0 collective-permute-start.3
  13.5 0.3 collective-permute-done.refs_0_
  13.8 4.3 %collective-permute-done.1.refs_1_ = bf16[32,2048]{1,0:T(8,128)(2,1)S(1)} collective-permute-done((bf16[32,2048]{1,0:T(8,128)(2,1)}, bf16[32,2048]{1,0:T(8,128)(2,1)S(1)}, u32[]{:S(2)}, u32[]{:S(2)}) %collective-permute-start.1) | collective-permute-done | bytes 131104 | tf_op jit(solution)/shard_map/ppermute | solution.py:306
  18.1 2.7 %collective-permute-done.2.refs_2_ = bf16[32,2048]{1,0:T(8,128)(2,1)S(1)} collective-permute-done((bf16[32,2048]{1,0:T(8,128)(2,1)}, bf16[32,2048]{1,0:T(8,128)(2,1)S(1)}, u32[]{:S(2)}, u32[]{:S(2)}) %collective-permute-start.2) | collective-permute-done | bytes 131104 | tf_op jit(solution)/shard_map/ppermute | solution.py:306
  20.8 2.9 %collective-permute-done.3.refs_3_ = bf16[32,2048]{1,0:T(8,128)(2,1)S(1)} collective-permute-done((bf16[32,2048]{1,0:T(8,128)(2,1)}, bf16[32,2048]{1,0:T(8,128)(2,1)S(1)}, u32[]{:S(2)}, u32[]{:S(2)}) %collective-permute-start.3) | collective-permute-done | bytes 131104 | tf_op jit(solution)/shard_map/ppermute | solution.py:306
  23.7 0.1 collective-permute-start.5
  23.8 0.7 collective-permute-start.4
  24.6 0.9 %collective-permute-start.6 = (bf16[32,2048]{1,0:T(8,128)(2,1)}, bf16[32,2048]{1,0:T(8,128)(2,1)S(1)}, u32[]{:S(2)}, u32[]{:S(2)}) collective-permute-start(bf16[32,2048]{1,0:T(8,128)(2,1)} %get-tuple-element.45), channel_id=1, source_target_pairs={{0,8},{1,9},{2,10},{3,11},{4,12},{5,13},{6,14},{7,15},{8,0},{9,1},... | collective-permute-start | bytes 393224 | tf_op jit(solution)/shard_map/ppermute | solution.py:306
  25.5 0.5 collective-permute-start.7
  26.0 2.0 %collective-permute-start.8 = (bf16[32,2048]{1,0:T(8,128)(2,1)}, bf16[32,2048]{1,0:T(8,128)(2,1)S(1)}, u32[]{:S(2)}, u32[]{:S(2)}) collective-permute-start(bf16[32,2048]{1,0:T(8,128)(2,1)} %get-tuple-element.47), channel_id=1, source_target_pairs={{0,24},{1,25},{2,26},{3,27},{4,28},{5,29},{6,30},{7,31},{8,16},{9,... | collective-permute-start | bytes 393224 | tf_op jit(solution)/shard_map/ppermute | solution.py:306
  28.1 0.0 collective-permute-done.5.refs_1_
  28.1 2.2 %copy-done = bf16[1,2048,1024]{2,1,0:T(8,128)(2,1)S(1)} copy-done((bf16[1,2048,1024]{2,1,0:T(8,128)(2,1)S(1)}, bf16[1,2048,1024]{2,1,0:T(8,128)(2,1)}, u32[]{:S(2)}) %copy-start) | copy-done | bytes 4194328
  30.2 2.2 %copy-done.2 = bf16[1,1024,2048]{2,1,0:T(8,128)(2,1)S(1)} copy-done((bf16[1,1024,2048]{2,1,0:T(8,128)(2,1)S(1)}, bf16[1,1024,2048]{2,1,0:T(8,128)(2,1)}, u32[]{:S(2)}) %copy-start.2) | copy-done | bytes 4194328
  32.4 4.1 %block.3 = (bf16[128,2048]{1,0:T(8,128)(2,1)S(1)}, bf16[1024,128]{1,0:T(8,128)(2,1)S(1)}, bf16[128,1024]{1,0:T(8,128)(2,1)S(1)}, bf16[128,2048]{1,0:T(8,128)(2,1...) custom-call(bf16[128,2048]{1,0:T(8,128)(2,1)S(1)} %join.4.refs_0_, ...), custom_call_target="tpu_custom_call" | custom-call | flops 805306368 | bytes 4194304 | tf_op jit(solution)/shard_map/block/pallas_call | solution.py:186
  36.5 0.0 copy-start.1
  36.6 0.0 collective-permute-done.6.refs_1_
  36.6 0.0 collective-permute-done.7.refs_2_
  36.6 0.0 collective-permute-done.8.refs_3_
  36.6 0.0 copy-done.5
  36.6 2.4 %collective-permute-done.4.refs_0_ = bf16[128,2048]{1,0:T(8,128)(2,1)S(1)} collective-permute-done((bf16[128,2048]{1,0:T(8,128)(2,1)S(1)}, bf16[128,2048]{1,0:T(8,128)(2,1)S(1)}, u32[]{:S(2)}, u32[]{:S(2)}) %collective-permute-start.4) | collective-permute-done | bytes 524320 | tf_op jit(solution)/shard_map/ppermute | solution.py:315
  39.1 0.1 collective-permute-start.9
  39.2 0.5 collective-permute-start.10
  39.7 1.1 %collective-permute-start.17 = (bf16[128,2048]{1,0:T(8,128)(2,1)S(1)}, bf16[128,2048]{1,0:T(8,128)(2,1)S(1)}, u32[]{:S(2)}, u32[]{:S(2)}) collective-permute-start(bf16[128,2048]{1,0:T(8,128)(2,1)S(1)} %join.6.refs_0_), channel_id=1, source_target_pairs={{0,2},{1,3},{2,6},{3,7},{4,0},{5,1},{6,4},{7,5},{8,10},{9,11},{10,... | collective-permute-start | bytes 1572872 | tf_op jit(solution)/shard_map/ppermute | solution.py:315
  40.7 0.0 collective-permute-start.11
  40.7 1.5 %collective-permute-done.11.refs_1_ = bf16[64,2048]{1,0:T(8,128)(2,1)S(1)} collective-permute-done((bf16[64,2048]{1,0:T(8,128)(2,1)S(1)}, bf16[64,2048]{1,0:T(8,128)(2,1)S(1)}, u32[]{:S(2)}, u32[]{:S(2)}) %collective-permute-start.11) | collective-permute-done | bytes 262176 | tf_op jit(solution)/shard_map/ppermute | solution.py:321
  42.3 0.0 collective-permute-done.9.refs_2_
  42.3 0.0 collective-permute-done.10.refs_3_
  42.4 0.0 copy-done.3
  42.4 5.4 %block.4 = (bf16[256,2048]{1,0:T(8,128)(2,1)S(1)}, bf16[1024,256]{1,0:T(8,128)(2,1)S(1)}, bf16[256,1024]{1,0:T(8,128)(2,1)S(1)}, bf16[256,2048]{1,0:T(8,128)(2,1...) custom-call(bf16[128,2048]{1,0:T(8,128)(2,1)S(1)} %join.6.refs_0_, ...), custom_call_target="tpu_custom_call" | custom-call | flops 1610612736 | bytes 4194304 | tf_op jit(solution)/shard_map/block/pallas_call | solution.py:186
  47.7 0.2 collective-permute-start.12
  47.9 6.5 %collective-permute-done.17.refs_0_ = bf16[128,2048]{1,0:T(8,128)(2,1)S(1)} collective-permute-done((bf16[128,2048]{1,0:T(8,128)(2,1)S(1)}, bf16[128,2048]{1,0:T(8,128)(2,1)S(1)}, u32[]{:S(2)}, u32[]{:S(2)}) %collective-permute-start.17) | collective-permute-done | bytes 524320 | tf_op jit(solution)/shard_map/ppermute | solution.py:315
  54.5 0.1 collective-permute-start.18
  54.6 1.8 %collective-permute-start.13 = (bf16[64,2048]{1,0:T(8,128)(2,1)S(1)}, bf16[64,2048]{1,0:T(8,128)(2,1)S(1)}, u32[]{:S(2)}, u32[]{:S(2)}) collective-permute-start(bf16[64,2048]{1,0:T(8,128)(2,1)S(1)} %add_up.4.refs_6_), channel_id=1, source_target_pairs={{2,0},{3,1},{6,2},{7,3},{0,4},{1,5},{4,6},{5,7},{10,8},{11,9},{14,... | collective-permute-start | bytes 786440 | tf_op jit(solution)/shard_map/ppermute | solution.py:318
  56.3 0.0 collective-permute-done.12.refs_1_
  56.4 0.1 collective-permute-done.18.refs_1_
  56.5 4.1 %block.5 = (bf16[128,2048]{1,0:T(8,128)(2,1)S(1)}, bf16[1024,128]{1,0:T(8,128)(2,1)S(1)}, bf16[128,1024]{1,0:T(8,128)(2,1)S(1)}, bf16[128,2048]{1,0:T(8,128)(2,1...) custom-call(bf16[128,2048]{1,0:T(8,128)(2,1)S(1)} %join.7.refs_0_, ...), custom_call_target="tpu_custom_call" | custom-call | flops 805306368 | bytes 4194304 | tf_op jit(solution)/shard_map/block/pallas_call | solution.py:186
  60.6 0.2 collective-permute-start.19
  60.8 0.8 collective-permute-start.20
  61.6 1.7 %collective-permute-done.13.refs_2_ = bf16[64,2048]{1,0:T(8,128)(2,1)S(1)} collective-permute-done((bf16[64,2048]{1,0:T(8,128)(2,1)S(1)}, bf16[64,2048]{1,0:T(8,128)(2,1)S(1)}, u32[]{:S(2)}, u32[]{:S(2)}) %collective-permute-start.13) | collective-permute-done | bytes 262176 | tf_op jit(solution)/shard_map/ppermute | solution.py:318
  63.3 0.1 add_up.5
  63.4 0.7 collective-permute-start.14
  64.1 0.4 collective-permute-start.15
  64.5 2.4 %collective-permute-start.16 = (bf16[16,2048]{1,0:T(8,128)(2,1)S(1)}, bf16[16,2048]{1,0:T(8,128)(2,1)S(1)}, u32[]{:S(2)}, u32[]{:S(2)}) collective-permute-start(bf16[16,2048]{1,0:T(8,128)(2,1)S(1)} %get-tuple-element.54), channel_id=1, source_target_pairs={{0,24},{1,25},{2,26},{3,27},{4,28},{5,29},{6,30},{7,31},{8,16},{9,... | collective-permute-start | bytes 196616 | tf_op jit(solution)/shard_map/ppermute | solution.py:306
  66.9 3.8 %grad_w_out.1 = f32[1,1024,2048]{2,1,0:T(8,128)} custom-call(bf16[1024,128]{1,0:T(8,128)(2,1)S(1)} %get-tuple-element.67.refs_0_, bf16[1024,256]{1,0:T(8,128)(2,1)S(1)} %get-tuple-element.68.refs_1_, bf16[1024,128]{1,0:T(8,128)(2,1)S(1)} %get-tuple-element.69.refs_2_, bf16[128,2048]{1,0:T(8,128)(2,1)S(1)} %get-tuple-element.70.refs_3_, ...), custom_call_target="tpu_custom_call" | custom-call | flops 2147483648 | bytes 8388608 | tf_op jit(solution)/shard_map/grad_w_out/pallas_call | solution.py:228
  70.8 0.0 collective-permute-done.19.refs_1_
  70.8 0.0 collective-permute-done.20.refs_2_
  70.8 0.1 add_up.7
  70.9 2.5 %collective-permute-start.21 = (bf16[16,2048]{1,0:T(8,128)(2,1)S(1)}, bf16[16,2048]{1,0:T(8,128)(2,1)S(1)}, u32[]{:S(2)}, u32[]{:S(2)}) collective-permute-start(bf16[16,2048]{1,0:T(8,128)(2,1)S(1)} %get-tuple-element.57.refs_6_), channel_id=1, source_target_pairs={{0,2},{1,3},{2,6},{3,7},{4,0},{5,1},{6,4},{7,5},{8,10},{9,11},{10,... | collective-permute-start | bytes 196616 | tf_op jit(solution)/shard_map/ppermute | solution.py:306
  73.4 1.7 %collective-permute-start.22 = (bf16[16,2048]{1,0:T(8,128)(2,1)S(1)}, bf16[16,2048]{1,0:T(8,128)(2,1)S(1)}, u32[]{:S(2)}, u32[]{:S(2)}) collective-permute-start(bf16[16,2048]{1,0:T(8,128)(2,1)S(1)} %get-tuple-element.58), channel_id=1, source_target_pairs={{0,10},{1,11},{2,14},{3,15},{4,8},{5,9},{6,12},{7,13},{8,2},{9,3},... | collective-permute-start | bytes 196616 | tf_op jit(solution)/shard_map/ppermute | solution.py:306
  75.1 0.0 collective-permute-done.14.rest_1_
  75.1 0.4 collective-permute-start.23
  75.5 0.0 collective-permute-done.15.rest_2_
  75.5 2.2 %collective-permute-start.24 = (bf16[16,2048]{1,0:T(8,128)(2,1)S(1)}, bf16[16,2048]{1,0:T(8,128)(2,1)S(1)}, u32[]{:S(2)}, u32[]{:S(2)}) collective-permute-start(bf16[16,2048]{1,0:T(8,128)(2,1)S(1)} %get-tuple-element.60), channel_id=1, source_target_pairs={{0,26},{1,27},{2,30},{3,31},{4,24},{5,25},{6,28},{7,29},{8,18},{9,... | collective-permute-start | bytes 196616 | tf_op jit(solution)/shard_map/ppermute | solution.py:306
  77.7 3.8 %grad_w_in.1 = f32[1,2048,1024]{2,1,0:T(8,128)} custom-call(bf16[128,2048]{1,0:T(8,128)(2,1)S(1)} %get-tuple-element.61.refs_0_, bf16[256,2048]{1,0:T(8,128)(2,1)S(1)} %get-tuple-element.62.refs_1_, bf16[128,2048]{1,0:T(8,128)(2,1)S(1)} %get-tuple-element.63.refs_2_, bf16[128,1024]{1,0:T(8,128)(2,1)S(1)} %get-tuple-element.64.refs_3_, ...), custom_call_target="tpu_custom_call" | custom-call | flops 2147483648 | bytes 8388608 | tf_op jit(solution)/shard_map/grad_w_in/pallas_call | solution.py:228
  81.5 0.0 collective-permute-done.16.rest_3_
  81.5 0.0 collective-permute-done.21.rest_4_
  81.5 0.0 collective-permute-done.22.rest_5_
  81.6 0.0 collective-permute-done.23.rest_6_
  81.6 1.2 %collective-permute-done.24.rest_7_ = bf16[16,2048]{1,0:T(8,128)(2,1)S(1)} collective-permute-done((bf16[16,2048]{1,0:T(8,128)(2,1)S(1)}, bf16[16,2048]{1,0:T(8,128)(2,1)S(1)}, u32[]{:S(2)}, u32[]{:S(2)}) %collective-permute-start.24) | collective-permute-done | bytes 65568 | tf_op jit(solution)/shard_map/ppermute | solution.py:306
  82.8 2.4 %place.1 = bf16[1024,2048]{1,0:T(8,128)(2,1)} custom-call(bf16[1024,128]{1,0:T(8,128)(2,1)S(1)} %copy-done.4, bf16[16,2048]{1,0:T(8,128)(2,1)S(1)} %get-tuple-element.51.rest_0_, bf16[16,2048]{1,0:T(8,128)(2,1)S(1)} %collective-permute-done.14.rest_1_, bf16[16,2048]{1,0:T(8,128)(2,1)S(1)} %collective-permute-done.15.rest_2_, ...), custom_call_target="tpu_custom_call" | custom-call | flops 536870912 | bytes 4194304 | tf_op jit(solution)/shard_map/place/pallas_call | solution.py:284
  (13 shorter events, 0.2 us)
Async XLA Ops:
  5.5 8.3 %collective-permute-start = (bf16[32,2048]{1,0:T(8,128)(2,1)}, bf16[32,2048]{1,0:T(8,128)(2,1)S(1)}, u32[]{:S(2)}, u32[]{:S(2)}) collective-permute-start(bf16[32,2048]{1,0:T(8,128)(2,1)} %get-tuple-element.39), channel_id=1, source_target_pairs={{0,2},{1,3},{2,6},{3,7},{4,0},{5,1},{6,4},{7,5},{8,10},{9,11},{10,... | collective-permute-start | bytes 393224 | tf_op jit(solution)/shard_map/ppermute | solution.py:306
  8.6 9.5 %collective-permute-start.1 = (bf16[32,2048]{1,0:T(8,128)(2,1)}, bf16[32,2048]{1,0:T(8,128)(2,1)S(1)}, u32[]{:S(2)}, u32[]{:S(2)}) collective-permute-start(bf16[32,2048]{1,0:T(8,128)(2,1)} %get-tuple-element.40), channel_id=1, source_target_pairs={{0,10},{1,11},{2,14},{3,15},{4,8},{5,9},{6,12},{7,13},{8,2},{9,3},... | collective-permute-start | bytes 393224 | tf_op jit(solution)/shard_map/ppermute | solution.py:306
  12.1 8.7 %collective-permute-start.2 = (bf16[32,2048]{1,0:T(8,128)(2,1)}, bf16[32,2048]{1,0:T(8,128)(2,1)S(1)}, u32[]{:S(2)}, u32[]{:S(2)}) collective-permute-start(bf16[32,2048]{1,0:T(8,128)(2,1)} %get-tuple-element.41), channel_id=1, source_target_pairs={{0,18},{1,19},{2,22},{3,23},{4,16},{5,17},{6,20},{7,21},{8,26},{9,... | collective-permute-start | bytes 393224 | tf_op jit(solution)/shard_map/ppermute | solution.py:306
  13.5 10.2 %collective-permute-start.3 = (bf16[32,2048]{1,0:T(8,128)(2,1)}, bf16[32,2048]{1,0:T(8,128)(2,1)S(1)}, u32[]{:S(2)}, u32[]{:S(2)}) collective-permute-start(bf16[32,2048]{1,0:T(8,128)(2,1)} %get-tuple-element.42), channel_id=1, source_target_pairs={{0,26},{1,27},{2,30},{3,31},{4,24},{5,25},{6,28},{7,29},{8,18},{9,... | collective-permute-start | bytes 393224 | tf_op jit(solution)/shard_map/ppermute | solution.py:306
  23.7 4.3 %collective-permute-start.5 = (bf16[128,2048]{1,0:T(8,128)(2,1)S(1)}, bf16[128,2048]{1,0:T(8,128)(2,1)S(1)}, u32[]{:S(2)}, u32[]{:S(2)}) collective-permute-start(bf16[128,2048]{1,0:T(8,128)(2,1)S(1)} %join.4.refs_0_), channel_id=1, source_target_pairs={{0,1},{1,0},{2,3},{3,2},{4,5},{5,4},{6,7},{7,6},{8,9},{9,8},{10,11... | collective-permute-start | bytes 1572872 | tf_op jit(solution)/shard_map/ppermute | solution.py:321
  23.8 15.2 %collective-permute-start.4 = (bf16[128,2048]{1,0:T(8,128)(2,1)S(1)}, bf16[128,2048]{1,0:T(8,128)(2,1)S(1)}, u32[]{:S(2)}, u32[]{:S(2)}) collective-permute-start(bf16[128,2048]{1,0:T(8,128)(2,1)S(1)} %join.4.refs_0_), channel_id=1, source_target_pairs={{0,2},{1,3},{2,6},{3,7},{4,0},{5,1},{6,4},{7,5},{8,10},{9,11},{10,... | collective-permute-start | bytes 1572872 | tf_op jit(solution)/shard_map/ppermute | solution.py:315
  24.6 12.0 %collective-permute-start.6 = (bf16[32,2048]{1,0:T(8,128)(2,1)}, bf16[32,2048]{1,0:T(8,128)(2,1)S(1)}, u32[]{:S(2)}, u32[]{:S(2)}) collective-permute-start(bf16[32,2048]{1,0:T(8,128)(2,1)} %get-tuple-element.45), channel_id=1, source_target_pairs={{0,8},{1,9},{2,10},{3,11},{4,12},{5,13},{6,14},{7,15},{8,0},{9,1},... | collective-permute-start | bytes 393224 | tf_op jit(solution)/shard_map/ppermute | solution.py:306
  25.5 11.1 %collective-permute-start.7 = (bf16[32,2048]{1,0:T(8,128)(2,1)}, bf16[32,2048]{1,0:T(8,128)(2,1)S(1)}, u32[]{:S(2)}, u32[]{:S(2)}) collective-permute-start(bf16[32,2048]{1,0:T(8,128)(2,1)} %get-tuple-element.46), channel_id=1, source_target_pairs={{0,16},{1,17},{2,18},{3,19},{4,20},{5,21},{6,22},{7,23},{8,24},{9,... | collective-permute-start | bytes 393224 | tf_op jit(solution)/shard_map/ppermute | solution.py:306
  26.0 10.6 %collective-permute-start.8 = (bf16[32,2048]{1,0:T(8,128)(2,1)}, bf16[32,2048]{1,0:T(8,128)(2,1)S(1)}, u32[]{:S(2)}, u32[]{:S(2)}) collective-permute-start(bf16[32,2048]{1,0:T(8,128)(2,1)} %get-tuple-element.47), channel_id=1, source_target_pairs={{0,24},{1,25},{2,26},{3,27},{4,28},{5,29},{6,30},{7,31},{8,16},{9,... | collective-permute-start | bytes 393224 | tf_op jit(solution)/shard_map/ppermute | solution.py:306
  28.1 2.2 %copy-start = (bf16[1,2048,1024]{2,1,0:T(8,128)(2,1)S(1)}, bf16[1,2048,1024]{2,1,0:T(8,128)(2,1)}, u32[]{:S(2)}) copy-start(bf16[1,2048,1024]{2,1,0:T(8,128)(2,1)} %refs_2_.3) | copy-start | bytes 12582916
  30.2 2.2 %copy-start.2 = (bf16[1,1024,2048]{2,1,0:T(8,128)(2,1)S(1)}, bf16[1,1024,2048]{2,1,0:T(8,128)(2,1)}, u32[]{:S(2)}) copy-start(bf16[1,1024,2048]{2,1,0:T(8,128)(2,1)} %refs_3_.3) | copy-start | bytes 12582916
  32.4 4.2 %copy-start.5 = (bf16[32,2048]{1,0:T(8,128)(2,1)S(1)}, bf16[32,2048]{1,0:T(8,128)(2,1)}, u32[]{:S(2)}) copy-start(bf16[32,2048]{1,0:T(8,128)(2,1)} %get-tuple-element.44.refs_0_) | copy-start | bytes 393220
  32.4 9.9 %copy-start.3 = (bf16[1,1024,2048]{2,1,0:T(8,128)(2,1)S(1)}, bf16[1,1024,2048]{2,1,0:T(8,128)(2,1)}, u32[]{:S(2)}) copy-start(bf16[1,1024,2048]{2,1,0:T(8,128)(2,1)} %refs_3_.3) | copy-start | bytes 12582916
  36.5 5.8 %copy-start.1 = (bf16[1,2048,1024]{2,1,0:T(8,128)(2,1)S(1)}, bf16[1,2048,1024]{2,1,0:T(8,128)(2,1)}, u32[]{:S(2)}) copy-start(bf16[1,2048,1024]{2,1,0:T(8,128)(2,1)} %refs_2_.3) | copy-start | bytes 12582916
  39.1 3.3 %collective-permute-start.9 = (bf16[128,2048]{1,0:T(8,128)(2,1)S(1)}, bf16[128,2048]{1,0:T(8,128)(2,1)S(1)}, u32[]{:S(2)}, u32[]{:S(2)}) collective-permute-start(bf16[128,2048]{1,0:T(8,128)(2,1)S(1)} %join.6.refs_0_), channel_id=1, source_target_pairs={{0,1},{1,0},{2,3},{3,2},{4,5},{5,4},{6,7},{7,6},{8,9},{9,8},{10,11... | collective-permute-start | bytes 1572872 | tf_op jit(solution)/shard_map/ppermute | solution.py:321
  39.2 3.2 %collective-permute-start.10 = (bf16[128,2048]{1,0:T(8,128)(2,1)S(1)}, bf16[128,2048]{1,0:T(8,128)(2,1)S(1)}, u32[]{:S(2)}, u32[]{:S(2)}) collective-permute-start(bf16[128,2048]{1,0:T(8,128)(2,1)S(1)} %join.5.refs_2_.refs_1_), channel_id=1, source_target_pairs={{0,1},{1,0},{2,3},{3,2},{4,5},{5,4},{6,7},{7,6},{8,9},{9,8},{10,11... | collective-permute-start | bytes 1572872 | tf_op jit(solution)/shard_map/ppermute | solution.py:321
  39.7 14.8 %collective-permute-start.17 = (bf16[128,2048]{1,0:T(8,128)(2,1)S(1)}, bf16[128,2048]{1,0:T(8,128)(2,1)S(1)}, u32[]{:S(2)}, u32[]{:S(2)}) collective-permute-start(bf16[128,2048]{1,0:T(8,128)(2,1)S(1)} %join.6.refs_0_), channel_id=1, source_target_pairs={{0,2},{1,3},{2,6},{3,7},{4,0},{5,1},{6,4},{7,5},{8,10},{9,11},{10,... | collective-permute-start | bytes 1572872 | tf_op jit(solution)/shard_map/ppermute | solution.py:315
  40.7 1.5 %collective-permute-start.11 = (bf16[64,2048]{1,0:T(8,128)(2,1)S(1)}, bf16[64,2048]{1,0:T(8,128)(2,1)S(1)}, u32[]{:S(2)}, u32[]{:S(2)}) collective-permute-start(bf16[64,2048]{1,0:T(8,128)(2,1)S(1)} %get-tuple-element.43.refs_4_.refs_1_), channel_id=1, source_target_pairs={{0,1},{1,0},{2,3},{3,2},{4,5},{5,4},{6,7},{7,6},{8,9},{9,8},{10,11... | collective-permute-start | bytes 786440 | tf_op jit(solution)/shard_map/ppermute | solution.py:321
  47.7 8.6 %collective-permute-start.12 = (bf16[128,2048]{1,0:T(8,128)(2,1)S(1)}, bf16[128,2048]{1,0:T(8,128)(2,1)S(1)}, u32[]{:S(2)}, u32[]{:S(2)}) collective-permute-start(bf16[128,2048]{1,0:T(8,128)(2,1)S(1)} %get-tuple-element.50.refs_1_), channel_id=1, source_target_pairs={{0,1},{1,0},{2,3},{3,2},{4,5},{5,4},{6,7},{7,6},{8,9},{9,8},{10,11... | collective-permute-start | bytes 1572872 | tf_op jit(solution)/shard_map/ppermute | solution.py:321
  54.5 2.0 %collective-permute-start.18 = (bf16[128,2048]{1,0:T(8,128)(2,1)S(1)}, bf16[128,2048]{1,0:T(8,128)(2,1)S(1)}, u32[]{:S(2)}, u32[]{:S(2)}) collective-permute-start(bf16[128,2048]{1,0:T(8,128)(2,1)S(1)} %join.7.refs_0_), channel_id=1, source_target_pairs={{0,1},{1,0},{2,3},{3,2},{4,5},{5,4},{6,7},{7,6},{8,9},{9,8},{10,11... | collective-permute-start | bytes 1572872 | tf_op jit(solution)/shard_map/ppermute | solution.py:321
  54.6 8.7 %collective-permute-start.13 = (bf16[64,2048]{1,0:T(8,128)(2,1)S(1)}, bf16[64,2048]{1,0:T(8,128)(2,1)S(1)}, u32[]{:S(2)}, u32[]{:S(2)}) collective-permute-start(bf16[64,2048]{1,0:T(8,128)(2,1)S(1)} %add_up.4.refs_6_), channel_id=1, source_target_pairs={{2,0},{3,1},{6,2},{7,3},{0,4},{1,5},{4,6},{5,7},{10,8},{11,9},{14,... | collective-permute-start | bytes 786440 | tf_op jit(solution)/shard_map/ppermute | solution.py:318
  60.6 10.2 %collective-permute-start.19 = (bf16[64,2048]{1,0:T(8,128)(2,1)S(1)}, bf16[64,2048]{1,0:T(8,128)(2,1)S(1)}, u32[]{:S(2)}, u32[]{:S(2)}) collective-permute-start(bf16[64,2048]{1,0:T(8,128)(2,1)S(1)} %get-tuple-element.56), channel_id=1, source_target_pairs={{0,1},{1,0},{2,3},{3,2},{4,5},{5,4},{6,7},{7,6},{8,9},{9,8},{10,11... | collective-permute-start | bytes 786440 | tf_op jit(solution)/shard_map/ppermute | solution.py:321
  60.8 10.0 %collective-permute-start.20 = (bf16[64,2048]{1,0:T(8,128)(2,1)S(1)}, bf16[64,2048]{1,0:T(8,128)(2,1)S(1)}, u32[]{:S(2)}, u32[]{:S(2)}) collective-permute-start(bf16[64,2048]{1,0:T(8,128)(2,1)S(1)} %add_up.6.refs_4_), channel_id=1, source_target_pairs={{0,2},{1,3},{2,6},{3,7},{4,0},{5,1},{6,4},{7,5},{8,10},{9,11},{10,... | collective-permute-start | bytes 786440 | tf_op jit(solution)/shard_map/ppermute | solution.py:315
  63.4 11.7 %collective-permute-start.14 = (bf16[16,2048]{1,0:T(8,128)(2,1)S(1)}, bf16[16,2048]{1,0:T(8,128)(2,1)S(1)}, u32[]{:S(2)}, u32[]{:S(2)}) collective-permute-start(bf16[16,2048]{1,0:T(8,128)(2,1)S(1)} %get-tuple-element.52), channel_id=1, source_target_pairs={{0,8},{1,9},{2,10},{3,11},{4,12},{5,13},{6,14},{7,15},{8,0},{9,1},... | collective-permute-start | bytes 196616 | tf_op jit(solution)/shard_map/ppermute | solution.py:306
  64.1 11.4 %collective-permute-start.15 = (bf16[16,2048]{1,0:T(8,128)(2,1)S(1)}, bf16[16,2048]{1,0:T(8,128)(2,1)S(1)}, u32[]{:S(2)}, u32[]{:S(2)}) collective-permute-start(bf16[16,2048]{1,0:T(8,128)(2,1)S(1)} %get-tuple-element.53), channel_id=1, source_target_pairs={{0,16},{1,17},{2,18},{3,19},{4,20},{5,21},{6,22},{7,23},{8,24},{9,... | collective-permute-start | bytes 196616 | tf_op jit(solution)/shard_map/ppermute | solution.py:306
  64.5 17.0 %collective-permute-start.16 = (bf16[16,2048]{1,0:T(8,128)(2,1)S(1)}, bf16[16,2048]{1,0:T(8,128)(2,1)S(1)}, u32[]{:S(2)}, u32[]{:S(2)}) collective-permute-start(bf16[16,2048]{1,0:T(8,128)(2,1)S(1)} %get-tuple-element.54), channel_id=1, source_target_pairs={{0,24},{1,25},{2,26},{3,27},{4,28},{5,29},{6,30},{7,31},{8,16},{9,... | collective-permute-start | bytes 196616 | tf_op jit(solution)/shard_map/ppermute | solution.py:306
  70.9 10.7 %collective-permute-start.21 = (bf16[16,2048]{1,0:T(8,128)(2,1)S(1)}, bf16[16,2048]{1,0:T(8,128)(2,1)S(1)}, u32[]{:S(2)}, u32[]{:S(2)}) collective-permute-start(bf16[16,2048]{1,0:T(8,128)(2,1)S(1)} %get-tuple-element.57.refs_6_), channel_id=1, source_target_pairs={{0,2},{1,3},{2,6},{3,7},{4,0},{5,1},{6,4},{7,5},{8,10},{9,11},{10,... | collective-permute-start | bytes 196616 | tf_op jit(solution)/shard_map/ppermute | solution.py:306
  73.4 8.2 %collective-permute-start.22 = (bf16[16,2048]{1,0:T(8,128)(2,1)S(1)}, bf16[16,2048]{1,0:T(8,128)(2,1)S(1)}, u32[]{:S(2)}, u32[]{:S(2)}) collective-permute-start(bf16[16,2048]{1,0:T(8,128)(2,1)S(1)} %get-tuple-element.58), channel_id=1, source_target_pairs={{0,10},{1,11},{2,14},{3,15},{4,8},{5,9},{6,12},{7,13},{8,2},{9,3},... | collective-permute-start | bytes 196616 | tf_op jit(solution)/shard_map/ppermute | solution.py:306
  75.1 6.5 %collective-permute-start.23 = (bf16[16,2048]{1,0:T(8,128)(2,1)S(1)}, bf16[16,2048]{1,0:T(8,128)(2,1)S(1)}, u32[]{:S(2)}, u32[]{:S(2)}) collective-permute-start(bf16[16,2048]{1,0:T(8,128)(2,1)S(1)} %get-tuple-element.59), channel_id=1, source_target_pairs={{0,18},{1,19},{2,22},{3,23},{4,16},{5,17},{6,20},{7,21},{8,26},{9,... | collective-permute-start | bytes 196616 | tf_op jit(solution)/shard_map/ppermute | solution.py:306
  75.5 7.2 %collective-permute-start.24 = (bf16[16,2048]{1,0:T(8,128)(2,1)S(1)}, bf16[16,2048]{1,0:T(8,128)(2,1)S(1)}, u32[]{:S(2)}, u32[]{:S(2)}) collective-permute-start(bf16[16,2048]{1,0:T(8,128)(2,1)S(1)} %get-tuple-element.60), channel_id=1, source_target_pairs={{0,26},{1,27},{2,30},{3,31},{4,24},{5,25},{6,28},{7,29},{8,18},{9,... | collective-permute-start | bytes 196616 | tf_op jit(solution)/shard_map/ppermute | solution.py:306
  77.7 5.1 %copy-start.4 = (bf16[1024,128]{1,0:T(8,128)(2,1)S(1)}, bf16[1024,128]{1,0:T(8,128)(2,1)}, u32[]{:S(2)}) copy-start(bf16[1024,128]{1,0:T(8,128)(2,1)} %get-tuple-element.38.spot) | copy-start | bytes 786436

commit v6 on v5

--- a/solution.py
+++ b/solution.py
@@ -344,7 +344,7 @@
         if not last:
             ours = join([ahead], [theirs] + ([first] if k == 1 else []))
     parts = [own[0]] + [send(own[d], d, lambda f: f) for d in range(1, groups)]
-    parts += [send(pieces[d], d, next_chip) for d in range(groups)]
+    parts += [send(pieces[d], d, next_chip) for d in range(groups - 1, -1, -1)][::-1]
 
     xs, act_ts, hgrads, gs = list(zip(*results))[:4]
     grad_w_out = outer(act_ts, gs, [], False, "grad_w_out")

time: 85.5 us -> 85.5 us (level)
  no operation moved by 1% of the time
where the time goes in v6:
time: 85.5 us; the launch traced here: 85.3 us
  Pallas kernels  28.9 us (34%)
  starting transfers between devices  27.3 us (32%)
  waiting for transfers between devices  23.6 us (28%)
  local copies, waits for them, and re-layouts  4.39 us (5%)
  between operations  1.04 us (1%)
    ppermute x14, starting transfers between devices, send(): return lax.ppermute(x, both, pairs)  21.8 us
    pallas_call x3, Pallas kernels, block(): pl.pallas_call(functools.partial(block_kernel, slots, min(256, units), le...  13.6 us
    ppermute x14, waiting for transfers between devices, send(): return lax.ppermute(x, both, pairs)  11.4 us
    ppermute x3, waiting for transfers between devices, ring(): return lax.ppermute(x, 'fsdp', [(f, next_chip(f)) for f in range(fsdp)])  8.92 us
    pallas_call x2, Pallas kernels, outer(): pl.pallas_call(functools.partial(outer_kernel, n, tiles, turn), in_specs=...  7.65 us
    pallas_call x1, Pallas kernels, pick(): pl.pallas_call(functools.partial(pick_kernel, groups, slots, tiles), in_s...  4.9 us
    unnamed x12, local copies, waits for them, and re-layouts  4.39 us
    ppermute x3, starting transfers between devices, ring(): return lax.ppermute(x, 'fsdp', [(f, next_chip(f)) for f in range(fsdp)])  2.64 us
  transfers between devices with their start and end apart: 25, of which 10 were waited for; matrix products, arithmetic and copies ran while one was open for 0% of the time, Pallas kernels for 25%

profile of v6, /device:TPU:0, one launch (start us, length us, event | category | flops | bytes accessed | tf_op | source)
XLA Modules:
  0.0 85.3 jit_solution(1705576230859904509)
XLA Ops:
  0.6 4.9 %pick.1 = (bf16[32,2048]{1,0:T(8,128)(2,1)}, bf16[32,2048]{1,0:T(8,128)(2,1)}, bf16[32,2048]{1,0:T(8,128)(2,1)}, bf16[32,2048]{1,0:T(8,128)(2,1)}, bf16[32,2048]...) custom-call(s32[1,4,16]{2,1,0:T(4,128)} %chosen_in.1, ...), custom_call_target="tpu_custom_call" | custom-call | flops 536870912 | bytes 8388608 | tf_op jit(solution)/shard_map/pick/pallas_call | solution.py:102
  5.5 3.1 %collective-permute-start = (bf16[32,2048]{1,0:T(8,128)(2,1)}, bf16[32,2048]{1,0:T(8,128)(2,1)S(1)}, u32[]{:S(2)}, u32[]{:S(2)}) collective-permute-start(bf16[32,2048]{1,0:T(8,128)(2,1)} %get-tuple-element.39), channel_id=1, source_target_pairs={{0,2},{1,3},{2,6},{3,7},{4,0},{5,1},{6,4},{7,5},{8,10},{9,11},{10,... | collective-permute-start | bytes 393224 | tf_op jit(solution)/shard_map/ppermute | solution.py:306
  8.6 3.5 %collective-permute-start.1 = (bf16[32,2048]{1,0:T(8,128)(2,1)}, bf16[32,2048]{1,0:T(8,128)(2,1)S(1)}, u32[]{:S(2)}, u32[]{:S(2)}) collective-permute-start(bf16[32,2048]{1,0:T(8,128)(2,1)} %get-tuple-element.40), channel_id=1, source_target_pairs={{0,10},{1,11},{2,14},{3,15},{4,8},{5,9},{6,12},{7,13},{8,2},{9,3},... | collective-permute-start | bytes 393224 | tf_op jit(solution)/shard_map/ppermute | solution.py:306
  12.1 1.4 %collective-permute-start.2 = (bf16[32,2048]{1,0:T(8,128)(2,1)}, bf16[32,2048]{1,0:T(8,128)(2,1)S(1)}, u32[]{:S(2)}, u32[]{:S(2)}) collective-permute-start(bf16[32,2048]{1,0:T(8,128)(2,1)} %get-tuple-element.41), channel_id=1, source_target_pairs={{0,18},{1,19},{2,22},{3,23},{4,16},{5,17},{6,20},{7,21},{8,26},{9,... | collective-permute-start | bytes 393224 | tf_op jit(solution)/shard_map/ppermute | solution.py:306
  13.5 0.0 collective-permute-start.3
  13.5 0.3 collective-permute-done.refs_0_
  13.8 4.3 %collective-permute-done.1.refs_1_ = bf16[32,2048]{1,0:T(8,128)(2,1)S(1)} collective-permute-done((bf16[32,2048]{1,0:T(8,128)(2,1)}, bf16[32,2048]{1,0:T(8,128)(2,1)S(1)}, u32[]{:S(2)}, u32[]{:S(2)}) %collective-permute-start.1) | collective-permute-done | bytes 131104 | tf_op jit(solution)/shard_map/ppermute | solution.py:306
  18.1 2.7 %collective-permute-done.2.refs_2_ = bf16[32,2048]{1,0:T(8,128)(2,1)S(1)} collective-permute-done((bf16[32,2048]{1,0:T(8,128)(2,1)}, bf16[32,2048]{1,0:T(8,128)(2,1)S(1)}, u32[]{:S(2)}, u32[]{:S(2)}) %collective-permute-start.2) | collective-permute-done | bytes 131104 | tf_op jit(solution)/shard_map/ppermute | solution.py:306
  20.8 2.9 %collective-permute-done.3.refs_3_ = bf16[32,2048]{1,0:T(8,128)(2,1)S(1)} collective-permute-done((bf16[32,2048]{1,0:T(8,128)(2,1)}, bf16[32,2048]{1,0:T(8,128)(2,1)S(1)}, u32[]{:S(2)}, u32[]{:S(2)}) %collective-permute-start.3) | collective-permute-done | bytes 131104 | tf_op jit(solution)/shard_map/ppermute | solution.py:306
  23.7 0.1 collective-permute-start.5
  23.8 0.7 collective-permute-start.4
  24.6 0.9 %collective-permute-start.6 = (bf16[32,2048]{1,0:T(8,128)(2,1)}, bf16[32,2048]{1,0:T(8,128)(2,1)S(1)}, u32[]{:S(2)}, u32[]{:S(2)}) collective-permute-start(bf16[32,2048]{1,0:T(8,128)(2,1)} %get-tuple-element.45), channel_id=1, source_target_pairs={{0,8},{1,9},{2,10},{3,11},{4,12},{5,13},{6,14},{7,15},{8,0},{9,1},... | collective-permute-start | bytes 393224 | tf_op jit(solution)/shard_map/ppermute | solution.py:306
  25.5 0.5 collective-permute-start.7
  26.0 2.0 %collective-permute-start.8 = (bf16[32,2048]{1,0:T(8,128)(2,1)}, bf16[32,2048]{1,0:T(8,128)(2,1)S(1)}, u32[]{:S(2)}, u32[]{:S(2)}) collective-permute-start(bf16[32,2048]{1,0:T(8,128)(2,1)} %get-tuple-element.47), channel_id=1, source_target_pairs={{0,24},{1,25},{2,26},{3,27},{4,28},{5,29},{6,30},{7,31},{8,16},{9,... | collective-permute-start | bytes 393224 | tf_op jit(solution)/shard_map/ppermute | solution.py:306
  28.1 0.0 collective-permute-done.5.refs_1_
  28.1 2.2 %copy-done = bf16[1,2048,1024]{2,1,0:T(8,128)(2,1)S(1)} copy-done((bf16[1,2048,1024]{2,1,0:T(8,128)(2,1)S(1)}, bf16[1,2048,1024]{2,1,0:T(8,128)(2,1)}, u32[]{:S(2)}) %copy-start) | copy-done | bytes 4194328
  30.2 2.2 %copy-done.2 = bf16[1,1024,2048]{2,1,0:T(8,128)(2,1)S(1)} copy-done((bf16[1,1024,2048]{2,1,0:T(8,128)(2,1)S(1)}, bf16[1,1024,2048]{2,1,0:T(8,128)(2,1)}, u32[]{:S(2)}) %copy-start.2) | copy-done | bytes 4194328
  32.4 4.1 %block.3 = (bf16[128,2048]{1,0:T(8,128)(2,1)S(1)}, bf16[1024,128]{1,0:T(8,128)(2,1)S(1)}, bf16[128,1024]{1,0:T(8,128)(2,1)S(1)}, bf16[128,2048]{1,0:T(8,128)(2,1...) custom-call(bf16[128,2048]{1,0:T(8,128)(2,1)S(1)} %join.4.refs_0_, ...), custom_call_target="tpu_custom_call" | custom-call | flops 805306368 | bytes 4194304 | tf_op jit(solution)/shard_map/block/pallas_call | solution.py:186
  36.5 0.0 copy-start.1
  36.6 0.0 collective-permute-done.6.refs_1_
  36.6 0.0 collective-permute-done.7.refs_2_
  36.6 0.0 collective-permute-done.8.refs_3_
  36.6 0.0 copy-done.5
  36.6 2.4 %collective-permute-done.4.refs_0_ = bf16[128,2048]{1,0:T(8,128)(2,1)S(1)} collective-permute-done((bf16[128,2048]{1,0:T(8,128)(2,1)S(1)}, bf16[128,2048]{1,0:T(8,128)(2,1)S(1)}, u32[]{:S(2)}, u32[]{:S(2)}) %collective-permute-start.4) | collective-permute-done | bytes 524320 | tf_op jit(solution)/shard_map/ppermute | solution.py:315
  39.1 0.1 collective-permute-start.9
  39.2 0.5 collective-permute-start.10
  39.7 1.1 %collective-permute-start.17 = (bf16[128,2048]{1,0:T(8,128)(2,1)S(1)}, bf16[128,2048]{1,0:T(8,128)(2,1)S(1)}, u32[]{:S(2)}, u32[]{:S(2)}) collective-permute-start(bf16[128,2048]{1,0:T(8,128)(2,1)S(1)} %join.6.refs_0_), channel_id=1, source_target_pairs={{0,2},{1,3},{2,6},{3,7},{4,0},{5,1},{6,4},{7,5},{8,10},{9,11},{10,... | collective-permute-start | bytes 1572872 | tf_op jit(solution)/shard_map/ppermute | solution.py:315
  40.7 0.0 collective-permute-start.11
  40.7 1.5 %collective-permute-done.11.refs_1_ = bf16[64,2048]{1,0:T(8,128)(2,1)S(1)} collective-permute-done((bf16[64,2048]{1,0:T(8,128)(2,1)S(1)}, bf16[64,2048]{1,0:T(8,128)(2,1)S(1)}, u32[]{:S(2)}, u32[]{:S(2)}) %collective-permute-start.11) | collective-permute-done | bytes 262176 | tf_op jit(solution)/shard_map/ppermute | solution.py:321
  42.3 0.0 collective-permute-done.9.refs_2_
  42.3 0.0 collective-permute-done.10.refs_3_
  42.4 0.0 copy-done.3
  42.4 5.4 %block.4 = (bf16[256,2048]{1,0:T(8,128)(2,1)S(1)}, bf16[1024,256]{1,0:T(8,128)(2,1)S(1)}, bf16[256,1024]{1,0:T(8,128)(2,1)S(1)}, bf16[256,2048]{1,0:T(8,128)(2,1...) custom-call(bf16[128,2048]{1,0:T(8,128)(2,1)S(1)} %join.6.refs_0_, ...), custom_call_target="tpu_custom_call" | custom-call | flops 1610612736 | bytes 4194304 | tf_op jit(solution)/shard_map/block/pallas_call | solution.py:186
  47.7 0.2 collective-permute-start.12
  47.9 6.5 %collective-permute-done.17.refs_0_ = bf16[128,2048]{1,0:T(8,128)(2,1)S(1)} collective-permute-done((bf16[128,2048]{1,0:T(8,128)(2,1)S(1)}, bf16[128,2048]{1,0:T(8,128)(2,1)S(1)}, u32[]{:S(2)}, u32[]{:S(2)}) %collective-permute-start.17) | collective-permute-done | bytes 524320 | tf_op jit(solution)/shard_map/ppermute | solution.py:315
  54.5 0.1 collective-permute-start.18
  54.6 1.8 %collective-permute-start.13 = (bf16[64,2048]{1,0:T(8,128)(2,1)S(1)}, bf16[64,2048]{1,0:T(8,128)(2,1)S(1)}, u32[]{:S(2)}, u32[]{:S(2)}) collective-permute-start(bf16[64,2048]{1,0:T(8,128)(2,1)S(1)} %add_up.4.refs_6_), channel_id=1, source_target_pairs={{2,0},{3,1},{6,2},{7,3},{0,4},{1,5},{4,6},{5,7},{10,8},{11,9},{14,... | collective-permute-start | bytes 786440 | tf_op jit(solution)/shard_map/ppermute | solution.py:318
  56.3 0.0 collective-permute-done.12.refs_1_
  56.4 0.1 collective-permute-done.18.refs_1_
  56.5 4.1 %block.5 = (bf16[128,2048]{1,0:T(8,128)(2,1)S(1)}, bf16[1024,128]{1,0:T(8,128)(2,1)S(1)}, bf16[128,1024]{1,0:T(8,128)(2,1)S(1)}, bf16[128,2048]{1,0:T(8,128)(2,1...) custom-call(bf16[128,2048]{1,0:T(8,128)(2,1)S(1)} %join.7.refs_0_, ...), custom_call_target="tpu_custom_call" | custom-call | flops 805306368 | bytes 4194304 | tf_op jit(solution)/shard_map/block/pallas_call | solution.py:186
  60.6 0.2 collective-permute-start.19
  60.8 0.8 collective-permute-start.20
  61.6 1.7 %collective-permute-done.13.refs_2_ = bf16[64,2048]{1,0:T(8,128)(2,1)S(1)} collective-permute-done((bf16[64,2048]{1,0:T(8,128)(2,1)S(1)}, bf16[64,2048]{1,0:T(8,128)(2,1)S(1)}, u32[]{:S(2)}, u32[]{:S(2)}) %collective-permute-start.13) | collective-permute-done | bytes 262176 | tf_op jit(solution)/shard_map/ppermute | solution.py:318
  63.3 0.1 add_up.5
  63.4 0.7 collective-permute-start.14
  64.1 0.4 collective-permute-start.15
  64.5 2.4 %collective-permute-start.16 = (bf16[16,2048]{1,0:T(8,128)(2,1)S(1)}, bf16[16,2048]{1,0:T(8,128)(2,1)S(1)}, u32[]{:S(2)}, u32[]{:S(2)}) collective-permute-start(bf16[16,2048]{1,0:T(8,128)(2,1)S(1)} %get-tuple-element.54), channel_id=1, source_target_pairs={{0,24},{1,25},{2,26},{3,27},{4,28},{5,29},{6,30},{7,31},{8,16},{9,... | collective-permute-start | bytes 196616 | tf_op jit(solution)/shard_map/ppermute | solution.py:306
  66.9 3.8 %grad_w_out.1 = f32[1,1024,2048]{2,1,0:T(8,128)} custom-call(bf16[1024,128]{1,0:T(8,128)(2,1)S(1)} %get-tuple-element.67.refs_0_, bf16[1024,256]{1,0:T(8,128)(2,1)S(1)} %get-tuple-element.68.refs_1_, bf16[1024,128]{1,0:T(8,128)(2,1)S(1)} %get-tuple-element.69.refs_2_, bf16[128,2048]{1,0:T(8,128)(2,1)S(1)} %get-tuple-element.70.refs_3_, ...), custom_call_target="tpu_custom_call" | custom-call | flops 2147483648 | bytes 8388608 | tf_op jit(solution)/shard_map/grad_w_out/pallas_call | solution.py:228
  70.8 0.0 collective-permute-done.19.refs_1_
  70.8 0.0 collective-permute-done.20.refs_2_
  70.8 0.1 add_up.7
  70.9 2.5 %collective-permute-start.21 = (bf16[16,2048]{1,0:T(8,128)(2,1)S(1)}, bf16[16,2048]{1,0:T(8,128)(2,1)S(1)}, u32[]{:S(2)}, u32[]{:S(2)}) collective-permute-start(bf16[16,2048]{1,0:T(8,128)(2,1)S(1)} %get-tuple-element.57.refs_6_), channel_id=1, source_target_pairs={{0,2},{1,3},{2,6},{3,7},{4,0},{5,1},{6,4},{7,5},{8,10},{9,11},{10,... | collective-permute-start | bytes 196616 | tf_op jit(solution)/shard_map/ppermute | solution.py:306
  73.4 1.7 %collective-permute-start.22 = (bf16[16,2048]{1,0:T(8,128)(2,1)S(1)}, bf16[16,2048]{1,0:T(8,128)(2,1)S(1)}, u32[]{:S(2)}, u32[]{:S(2)}) collective-permute-start(bf16[16,2048]{1,0:T(8,128)(2,1)S(1)} %get-tuple-element.58), channel_id=1, source_target_pairs={{0,10},{1,11},{2,14},{3,15},{4,8},{5,9},{6,12},{7,13},{8,2},{9,3},... | collective-permute-start | bytes 196616 | tf_op jit(solution)/shard_map/ppermute | solution.py:306
  75.1 0.0 collective-permute-done.14.rest_1_
  75.1 0.4 collective-permute-start.23
  75.5 0.0 collective-permute-done.15.rest_2_
  75.5 2.2 %collective-permute-start.24 = (bf16[16,2048]{1,0:T(8,128)(2,1)S(1)}, bf16[16,2048]{1,0:T(8,128)(2,1)S(1)}, u32[]{:S(2)}, u32[]{:S(2)}) collective-permute-start(bf16[16,2048]{1,0:T(8,128)(2,1)S(1)} %get-tuple-element.60), channel_id=1, source_target_pairs={{0,26},{1,27},{2,30},{3,31},{4,24},{5,25},{6,28},{7,29},{8,18},{9,... | collective-permute-start | bytes 196616 | tf_op jit(solution)/shard_map/ppermute | solution.py:306
  77.7 3.8 %grad_w_in.1 = f32[1,2048,1024]{2,1,0:T(8,128)} custom-call(bf16[128,2048]{1,0:T(8,128)(2,1)S(1)} %get-tuple-element.61.refs_0_, bf16[256,2048]{1,0:T(8,128)(2,1)S(1)} %get-tuple-element.62.refs_1_, bf16[128,2048]{1,0:T(8,128)(2,1)S(1)} %get-tuple-element.63.refs_2_, bf16[128,1024]{1,0:T(8,128)(2,1)S(1)} %get-tuple-element.64.refs_3_, ...), custom_call_target="tpu_custom_call" | custom-call | flops 2147483648 | bytes 8388608 | tf_op jit(solution)/shard_map/grad_w_in/pallas_call | solution.py:228
  81.5 0.0 collective-permute-done.16.rest_3_
  81.5 0.0 collective-permute-done.21.rest_4_
  81.5 0.0 collective-permute-done.22.rest_5_
  81.6 0.0 collective-permute-done.23.rest_6_
  81.6 1.2 %collective-permute-done.24.rest_7_ = bf16[16,2048]{1,0:T(8,128)(2,1)S(1)} collective-permute-done((bf16[16,2048]{1,0:T(8,128)(2,1)S(1)}, bf16[16,2048]{1,0:T(8,128)(2,1)S(1)}, u32[]{:S(2)}, u32[]{:S(2)}) %collective-permute-start.24) | collective-permute-done | bytes 65568 | tf_op jit(solution)/shard_map/ppermute | solution.py:306
  82.8 2.4 %place.1 = bf16[1024,2048]{1,0:T(8,128)(2,1)} custom-call(bf16[1024,128]{1,0:T(8,128)(2,1)S(1)} %copy-done.4, bf16[16,2048]{1,0:T(8,128)(2,1)S(1)} %get-tuple-element.51.rest_0_, bf16[16,2048]{1,0:T(8,128)(2,1)S(1)} %collective-permute-done.14.rest_1_, bf16[16,2048]{1,0:T(8,128)(2,1)S(1)} %collective-permute-done.15.rest_2_, ...), custom_call_target="tpu_custom_call" | custom-call | flops 536870912 | bytes 4194304 | tf_op jit(solution)/shard_map/place/pallas_call | solution.py:284
  (13 shorter events, 0.2 us)
Async XLA Ops:
  5.5 8.3 %collective-permute-start = (bf16[32,2048]{1,0:T(8,128)(2,1)}, bf16[32,2048]{1,0:T(8,128)(2,1)S(1)}, u32[]{:S(2)}, u32[]{:S(2)}) collective-permute-start(bf16[32,2048]{1,0:T(8,128)(2,1)} %get-tuple-element.39), channel_id=1, source_target_pairs={{0,2},{1,3},{2,6},{3,7},{4,0},{5,1},{6,4},{7,5},{8,10},{9,11},{10,... | collective-permute-start | bytes 393224 | tf_op jit(solution)/shard_map/ppermute | solution.py:306
  8.6 9.5 %collective-permute-start.1 = (bf16[32,2048]{1,0:T(8,128)(2,1)}, bf16[32,2048]{1,0:T(8,128)(2,1)S(1)}, u32[]{:S(2)}, u32[]{:S(2)}) collective-permute-start(bf16[32,2048]{1,0:T(8,128)(2,1)} %get-tuple-element.40), channel_id=1, source_target_pairs={{0,10},{1,11},{2,14},{3,15},{4,8},{5,9},{6,12},{7,13},{8,2},{9,3},... | collective-permute-start | bytes 393224 | tf_op jit(solution)/shard_map/ppermute | solution.py:306
  12.1 8.7 %collective-permute-start.2 = (bf16[32,2048]{1,0:T(8,128)(2,1)}, bf16[32,2048]{1,0:T(8,128)(2,1)S(1)}, u32[]{:S(2)}, u32[]{:S(2)}) collective-permute-start(bf16[32,2048]{1,0:T(8,128)(2,1)} %get-tuple-element.41), channel_id=1, source_target_pairs={{0,18},{1,19},{2,22},{3,23},{4,16},{5,17},{6,20},{7,21},{8,26},{9,... | collective-permute-start | bytes 393224 | tf_op jit(solution)/shard_map/ppermute | solution.py:306
  13.5 10.2 %collective-permute-start.3 = (bf16[32,2048]{1,0:T(8,128)(2,1)}, bf16[32,2048]{1,0:T(8,128)(2,1)S(1)}, u32[]{:S(2)}, u32[]{:S(2)}) collective-permute-start(bf16[32,2048]{1,0:T(8,128)(2,1)} %get-tuple-element.42), channel_id=1, source_target_pairs={{0,26},{1,27},{2,30},{3,31},{4,24},{5,25},{6,28},{7,29},{8,18},{9,... | collective-permute-start | bytes 393224 | tf_op jit(solution)/shard_map/ppermute | solution.py:306
  23.7 4.3 %collective-permute-start.5 = (bf16[128,2048]{1,0:T(8,128)(2,1)S(1)}, bf16[128,2048]{1,0:T(8,128)(2,1)S(1)}, u32[]{:S(2)}, u32[]{:S(2)}) collective-permute-start(bf16[128,2048]{1,0:T(8,128)(2,1)S(1)} %join.4.refs_0_), channel_id=1, source_target_pairs={{0,1},{1,0},{2,3},{3,2},{4,5},{5,4},{6,7},{7,6},{8,9},{9,8},{10,11... | collective-permute-start | bytes 1572872 | tf_op jit(solution)/shard_map/ppermute | solution.py:321
  23.8 15.2 %collective-permute-start.4 = (bf16[128,2048]{1,0:T(8,128)(2,1)S(1)}, bf16[128,2048]{1,0:T(8,128)(2,1)S(1)}, u32[]{:S(2)}, u32[]{:S(2)}) collective-permute-start(bf16[128,2048]{1,0:T(8,128)(2,1)S(1)} %join.4.refs_0_), channel_id=1, source_target_pairs={{0,2},{1,3},{2,6},{3,7},{4,0},{5,1},{6,4},{7,5},{8,10},{9,11},{10,... | collective-permute-start | bytes 1572872 | tf_op jit(solution)/shard_map/ppermute | solution.py:315
  24.6 12.0 %collective-permute-start.6 = (bf16[32,2048]{1,0:T(8,128)(2,1)}, bf16[32,2048]{1,0:T(8,128)(2,1)S(1)}, u32[]{:S(2)}, u32[]{:S(2)}) collective-permute-start(bf16[32,2048]{1,0:T(8,128)(2,1)} %get-tuple-element.45), channel_id=1, source_target_pairs={{0,8},{1,9},{2,10},{3,11},{4,12},{5,13},{6,14},{7,15},{8,0},{9,1},... | collective-permute-start | bytes 393224 | tf_op jit(solution)/shard_map/ppermute | solution.py:306
  25.5 11.1 %collective-permute-start.7 = (bf16[32,2048]{1,0:T(8,128)(2,1)}, bf16[32,2048]{1,0:T(8,128)(2,1)S(1)}, u32[]{:S(2)}, u32[]{:S(2)}) collective-permute-start(bf16[32,2048]{1,0:T(8,128)(2,1)} %get-tuple-element.46), channel_id=1, source_target_pairs={{0,16},{1,17},{2,18},{3,19},{4,20},{5,21},{6,22},{7,23},{8,24},{9,... | collective-permute-start | bytes 393224 | tf_op jit(solution)/shard_map/ppermute | solution.py:306
  26.0 10.6 %collective-permute-start.8 = (bf16[32,2048]{1,0:T(8,128)(2,1)}, bf16[32,2048]{1,0:T(8,128)(2,1)S(1)}, u32[]{:S(2)}, u32[]{:S(2)}) collective-permute-start(bf16[32,2048]{1,0:T(8,128)(2,1)} %get-tuple-element.47), channel_id=1, source_target_pairs={{0,24},{1,25},{2,26},{3,27},{4,28},{5,29},{6,30},{7,31},{8,16},{9,... | collective-permute-start | bytes 393224 | tf_op jit(solution)/shard_map/ppermute | solution.py:306
  28.1 2.2 %copy-start = (bf16[1,2048,1024]{2,1,0:T(8,128)(2,1)S(1)}, bf16[1,2048,1024]{2,1,0:T(8,128)(2,1)}, u32[]{:S(2)}) copy-start(bf16[1,2048,1024]{2,1,0:T(8,128)(2,1)} %refs_2_.3) | copy-start | bytes 12582916
  30.2 2.2 %copy-start.2 = (bf16[1,1024,2048]{2,1,0:T(8,128)(2,1)S(1)}, bf16[1,1024,2048]{2,1,0:T(8,128)(2,1)}, u32[]{:S(2)}) copy-start(bf16[1,1024,2048]{2,1,0:T(8,128)(2,1)} %refs_3_.3) | copy-start | bytes 12582916
  32.4 4.2 %copy-start.5 = (bf16[32,2048]{1,0:T(8,128)(2,1)S(1)}, bf16[32,2048]{1,0:T(8,128)(2,1)}, u32[]{:S(2)}) copy-start(bf16[32,2048]{1,0:T(8,128)(2,1)} %get-tuple-element.44.refs_0_) | copy-start | bytes 393220
  32.4 9.9 %copy-start.3 = (bf16[1,1024,2048]{2,1,0:T(8,128)(2,1)S(1)}, bf16[1,1024,2048]{2,1,0:T(8,128)(2,1)}, u32[]{:S(2)}) copy-start(bf16[1,1024,2048]{2,1,0:T(8,128)(2,1)} %refs_3_.3) | copy-start | bytes 12582916
  36.5 5.8 %copy-start.1 = (bf16[1,2048,1024]{2,1,0:T(8,128)(2,1)S(1)}, bf16[1,2048,1024]{2,1,0:T(8,128)(2,1)}, u32[]{:S(2)}) copy-start(bf16[1,2048,1024]{2,1,0:T(8,128)(2,1)} %refs_2_.3) | copy-start | bytes 12582916
  39.1 3.3 %collective-permute-start.9 = (bf16[128,2048]{1,0:T(8,128)(2,1)S(1)}, bf16[128,2048]{1,0:T(8,128)(2,1)S(1)}, u32[]{:S(2)}, u32[]{:S(2)}) collective-permute-start(bf16[128,2048]{1,0:T(8,128)(2,1)S(1)} %join.6.refs_0_), channel_id=1, source_target_pairs={{0,1},{1,0},{2,3},{3,2},{4,5},{5,4},{6,7},{7,6},{8,9},{9,8},{10,11... | collective-permute-start | bytes 1572872 | tf_op jit(solution)/shard_map/ppermute | solution.py:321
  39.2 3.2 %collective-permute-start.10 = (bf16[128,2048]{1,0:T(8,128)(2,1)S(1)}, bf16[128,2048]{1,0:T(8,128)(2,1)S(1)}, u32[]{:S(2)}, u32[]{:S(2)}) collective-permute-start(bf16[128,2048]{1,0:T(8,128)(2,1)S(1)} %join.5.refs_2_.refs_1_), channel_id=1, source_target_pairs={{0,1},{1,0},{2,3},{3,2},{4,5},{5,4},{6,7},{7,6},{8,9},{9,8},{10,11... | collective-permute-start | bytes 1572872 | tf_op jit(solution)/shard_map/ppermute | solution.py:321
  39.7 14.8 %collective-permute-start.17 = (bf16[128,2048]{1,0:T(8,128)(2,1)S(1)}, bf16[128,2048]{1,0:T(8,128)(2,1)S(1)}, u32[]{:S(2)}, u32[]{:S(2)}) collective-permute-start(bf16[128,2048]{1,0:T(8,128)(2,1)S(1)} %join.6.refs_0_), channel_id=1, source_target_pairs={{0,2},{1,3},{2,6},{3,7},{4,0},{5,1},{6,4},{7,5},{8,10},{9,11},{10,... | collective-permute-start | bytes 1572872 | tf_op jit(solution)/shard_map/ppermute | solution.py:315
  40.7 1.5 %collective-permute-start.11 = (bf16[64,2048]{1,0:T(8,128)(2,1)S(1)}, bf16[64,2048]{1,0:T(8,128)(2,1)S(1)}, u32[]{:S(2)}, u32[]{:S(2)}) collective-permute-start(bf16[64,2048]{1,0:T(8,128)(2,1)S(1)} %get-tuple-element.43.refs_4_.refs_1_), channel_id=1, source_target_pairs={{0,1},{1,0},{2,3},{3,2},{4,5},{5,4},{6,7},{7,6},{8,9},{9,8},{10,11... | collective-permute-start | bytes 786440 | tf_op jit(solution)/shard_map/ppermute | solution.py:321
  47.7 8.6 %collective-permute-start.12 = (bf16[128,2048]{1,0:T(8,128)(2,1)S(1)}, bf16[128,2048]{1,0:T(8,128)(2,1)S(1)}, u32[]{:S(2)}, u32[]{:S(2)}) collective-permute-start(bf16[128,2048]{1,0:T(8,128)(2,1)S(1)} %get-tuple-element.50.refs_1_), channel_id=1, source_target_pairs={{0,1},{1,0},{2,3},{3,2},{4,5},{5,4},{6,7},{7,6},{8,9},{9,8},{10,11... | collective-permute-start | bytes 1572872 | tf_op jit(solution)/shard_map/ppermute | solution.py:321
  54.5 2.0 %collective-permute-start.18 = (bf16[128,2048]{1,0:T(8,128)(2,1)S(1)}, bf16[128,2048]{1,0:T(8,128)(2,1)S(1)}, u32[]{:S(2)}, u32[]{:S(2)}) collective-permute-start(bf16[128,2048]{1,0:T(8,128)(2,1)S(1)} %join.7.refs_0_), channel_id=1, source_target_pairs={{0,1},{1,0},{2,3},{3,2},{4,5},{5,4},{6,7},{7,6},{8,9},{9,8},{10,11... | collective-permute-start | bytes 1572872 | tf_op jit(solution)/shard_map/ppermute | solution.py:321
  54.6 8.7 %collective-permute-start.13 = (bf16[64,2048]{1,0:T(8,128)(2,1)S(1)}, bf16[64,2048]{1,0:T(8,128)(2,1)S(1)}, u32[]{:S(2)}, u32[]{:S(2)}) collective-permute-start(bf16[64,2048]{1,0:T(8,128)(2,1)S(1)} %add_up.4.refs_6_), channel_id=1, source_target_pairs={{2,0},{3,1},{6,2},{7,3},{0,4},{1,5},{4,6},{5,7},{10,8},{11,9},{14,... | collective-permute-start | bytes 786440 | tf_op jit(solution)/shard_map/ppermute | solution.py:318
  60.6 10.2 %collective-permute-start.19 = (bf16[64,2048]{1,0:T(8,128)(2,1)S(1)}, bf16[64,2048]{1,0:T(8,128)(2,1)S(1)}, u32[]{:S(2)}, u32[]{:S(2)}) collective-permute-start(bf16[64,2048]{1,0:T(8,128)(2,1)S(1)} %get-tuple-element.56), channel_id=1, source_target_pairs={{0,1},{1,0},{2,3},{3,2},{4,5},{5,4},{6,7},{7,6},{8,9},{9,8},{10,11... | collective-permute-start | bytes 786440 | tf_op jit(solution)/shard_map/ppermute | solution.py:321
  60.8 10.0 %collective-permute-start.20 = (bf16[64,2048]{1,0:T(8,128)(2,1)S(1)}, bf16[64,2048]{1,0:T(8,128)(2,1)S(1)}, u32[]{:S(2)}, u32[]{:S(2)}) collective-permute-start(bf16[64,2048]{1,0:T(8,128)(2,1)S(1)} %add_up.6.refs_4_), channel_id=1, source_target_pairs={{0,2},{1,3},{2,6},{3,7},{4,0},{5,1},{6,4},{7,5},{8,10},{9,11},{10,... | collective-permute-start | bytes 786440 | tf_op jit(solution)/shard_map/ppermute | solution.py:315
  63.4 11.7 %collective-permute-start.14 = (bf16[16,2048]{1,0:T(8,128)(2,1)S(1)}, bf16[16,2048]{1,0:T(8,128)(2,1)S(1)}, u32[]{:S(2)}, u32[]{:S(2)}) collective-permute-start(bf16[16,2048]{1,0:T(8,128)(2,1)S(1)} %get-tuple-element.52), channel_id=1, source_target_pairs={{0,8},{1,9},{2,10},{3,11},{4,12},{5,13},{6,14},{7,15},{8,0},{9,1},... | collective-permute-start | bytes 196616 | tf_op jit(solution)/shard_map/ppermute | solution.py:306
  64.1 11.4 %collective-permute-start.15 = (bf16[16,2048]{1,0:T(8,128)(2,1)S(1)}, bf16[16,2048]{1,0:T(8,128)(2,1)S(1)}, u32[]{:S(2)}, u32[]{:S(2)}) collective-permute-start(bf16[16,2048]{1,0:T(8,128)(2,1)S(1)} %get-tuple-element.53), channel_id=1, source_target_pairs={{0,16},{1,17},{2,18},{3,19},{4,20},{5,21},{6,22},{7,23},{8,24},{9,... | collective-permute-start | bytes 196616 | tf_op jit(solution)/shard_map/ppermute | solution.py:306
  64.5 17.0 %collective-permute-start.16 = (bf16[16,2048]{1,0:T(8,128)(2,1)S(1)}, bf16[16,2048]{1,0:T(8,128)(2,1)S(1)}, u32[]{:S(2)}, u32[]{:S(2)}) collective-permute-start(bf16[16,2048]{1,0:T(8,128)(2,1)S(1)} %get-tuple-element.54), channel_id=1, source_target_pairs={{0,24},{1,25},{2,26},{3,27},{4,28},{5,29},{6,30},{7,31},{8,16},{9,... | collective-permute-start | bytes 196616 | tf_op jit(solution)/shard_map/ppermute | solution.py:306
  70.9 10.7 %collective-permute-start.21 = (bf16[16,2048]{1,0:T(8,128)(2,1)S(1)}, bf16[16,2048]{1,0:T(8,128)(2,1)S(1)}, u32[]{:S(2)}, u32[]{:S(2)}) collective-permute-start(bf16[16,2048]{1,0:T(8,128)(2,1)S(1)} %get-tuple-element.57.refs_6_), channel_id=1, source_target_pairs={{0,2},{1,3},{2,6},{3,7},{4,0},{5,1},{6,4},{7,5},{8,10},{9,11},{10,... | collective-permute-start | bytes 196616 | tf_op jit(solution)/shard_map/ppermute | solution.py:306
  73.4 8.2 %collective-permute-start.22 = (bf16[16,2048]{1,0:T(8,128)(2,1)S(1)}, bf16[16,2048]{1,0:T(8,128)(2,1)S(1)}, u32[]{:S(2)}, u32[]{:S(2)}) collective-permute-start(bf16[16,2048]{1,0:T(8,128)(2,1)S(1)} %get-tuple-element.58), channel_id=1, source_target_pairs={{0,10},{1,11},{2,14},{3,15},{4,8},{5,9},{6,12},{7,13},{8,2},{9,3},... | collective-permute-start | bytes 196616 | tf_op jit(solution)/shard_map/ppermute | solution.py:306
  75.1 6.5 %collective-permute-start.23 = (bf16[16,2048]{1,0:T(8,128)(2,1)S(1)}, bf16[16,2048]{1,0:T(8,128)(2,1)S(1)}, u32[]{:S(2)}, u32[]{:S(2)}) collective-permute-start(bf16[16,2048]{1,0:T(8,128)(2,1)S(1)} %get-tuple-element.59), channel_id=1, source_target_pairs={{0,18},{1,19},{2,22},{3,23},{4,16},{5,17},{6,20},{7,21},{8,26},{9,... | collective-permute-start | bytes 196616 | tf_op jit(solution)/shard_map/ppermute | solution.py:306
  75.5 7.2 %collective-permute-start.24 = (bf16[16,2048]{1,0:T(8,128)(2,1)S(1)}, bf16[16,2048]{1,0:T(8,128)(2,1)S(1)}, u32[]{:S(2)}, u32[]{:S(2)}) collective-permute-start(bf16[16,2048]{1,0:T(8,128)(2,1)S(1)} %get-tuple-element.60), channel_id=1, source_target_pairs={{0,26},{1,27},{2,30},{3,31},{4,24},{5,25},{6,28},{7,29},{8,18},{9,... | collective-permute-start | bytes 196616 | tf_op jit(solution)/shard_map/ppermute | solution.py:306
  77.7 5.1 %copy-start.4 = (bf16[1024,128]{1,0:T(8,128)(2,1)S(1)}, bf16[1024,128]{1,0:T(8,128)(2,1)}, u32[]{:S(2)}) copy-start(bf16[1024,128]{1,0:T(8,128)(2,1)} %get-tuple-element.38.spot) | copy-start | bytes 786436
